TPU v7x, 32 devices: a whole 2x2x4 slice. The times are simulated.
32 devices in a mesh: seq: 8 (over z, y), wsh: 4 (over x, core).
Axes of the slice: x: 2, y: 2, z: 4, core: 2. Of those that a mesh axis runs over, the one named last changes fastest.
Arguments:
- hidden: bfloat16 [4, 2048, 2048], P('wsh', 'seq'), may hold values from -6 to 6
- teacher: bfloat16 [4, 2048, 2048], P('wsh', 'seq'), may hold values from -15 to 15
- cotangent: bfloat16 [4, 2048, 2048], P('wsh', 'seq'), may hold values from -6 to 6
- lengths: int32 [4], P('wsh'), may hold values from 1024 to 2048, as said below
- norm_gain: bfloat16 [2048], P('wsh'), may hold values from 0.5 to 1.5
- in_weight: bfloat16 [2048, 8192], P('wsh'), may hold values from -0.125 to 0.125
- conv_weight: bfloat16 [4, 4096], P(None, 'wsh'), may hold values from -3 to 3
- conv_bias: bfloat16 [4096], P('wsh'), may hold values from -3 to 3
- x_weight: bfloat16 [160, 4096], P(None, 'wsh'), may hold values from -0.09375 to 0.09375
- dt_weight: bfloat16 [128, 4096], P(None, 'wsh'), may hold values from -0.5 to 0.5
- dt_bias: bfloat16 [4096], P('wsh'), may hold values from -12 to -1
- a_log: bfloat16 [16, 4096], P(None, 'wsh'), may hold values from -1.3828125 to 1.3828125
- skip_gain: bfloat16 [4096], P('wsh'), may hold values from 0.5 to 1.5
- out_weight: bfloat16 [4096, 2048], P('wsh'), may hold values from -0.25 to 0.25
Outputs:
- output: bfloat16 [4, 2048, 2048], P('wsh', 'seq')
- loss: float32 [], replicated
- hidden_grad: bfloat16 [4, 2048, 2048], P('wsh', 'seq')
- norm_gain_grad: float32 [2048], P('wsh')
- in_weight_grad: float32 [2048, 8192], P('wsh')
- conv_weight_grad: float32 [4, 4096], P(None, 'wsh')
- conv_bias_grad: float32 [4096], P('wsh')
- x_weight_grad: float32 [160, 4096], P(None, 'wsh')
- dt_weight_grad: float32 [128, 4096], P(None, 'wsh')
- dt_bias_grad: float32 [4096], P('wsh')
- a_log_grad: float32 [16, 4096], P(None, 'wsh')
- skip_gain_grad: float32 [4096], P('wsh')
- out_weight_grad: float32 [4096, 2048], P('wsh')
Inputs may be any that keep to these rules, and one draw needn't show every extreme that they name: lengths[s] counts the valid tokens at the start of sequence s; in every draw one sequence has all 2048 tokens valid.
All inputs are finite; a program needn't handle non-finite values.
Results may differ from a plain program's by a relative error of at most 0.012.
Values may be sent and summed in bfloat16 or wider, within the bound.
No kernel may reach another device: no remote copies, remote signals or barrier semaphores. Data moves between devices by JAX's collectives and lax.ppermute only.
A program may use at most 384 MiB of HBM per device.

v0:
```python
from functools import partial

import jax
import jax.numpy as jnp
from jax import lax
from jax.sharding import PartitionSpec as P

SCAN_BLOCK = 32


NORM_EPS = 1e-05
FULL_PRECISION = lax.Precision.HIGHEST
ROWS_FIRST = (((0,), (0,)), ((), ()))
COLS_LAST = (((1,), (1,)), ((), ()))


def passed_along(block, axis, distance):
    devices = range(lax.axis_size(axis))
    route = [(i - distance, i) for i in devices if i - distance in devices]
    return lax.ppermute(block, axis, route)


def carried_in(shard, axis, combine, identity, reverse):
    length, position = (lax.axis_size(axis), lax.axis_index(axis))
    everything = jax.tree.map(lambda part: lax.all_gather(part, axis), shard)
    start = jax.tree.map(
        lambda part, zero: jnp.broadcast_to(jnp.asarray(zero, part.dtype), part.shape),
        shard,
        identity,
    )

    def hop(k, before):
        at = length - 1 - k if reverse else k
        reached = at > position if reverse else at < position
        new = combine(before, jax.tree.map(lambda part: part[at], everything))
        return jax.tree.map(lambda a, b: jnp.where(reached, a, b), new, before)

    return lax.fori_loop(0, length, hop, start)


def shortened(shard):
    return jax.tree.map(lambda a: a.astype(jnp.bfloat16) if a.dtype == jnp.float32 else a, shard)


def silu_value(v):
    return v * jax.nn.sigmoid(v)


def silu_slope(v):
    sigma = jax.nn.sigmoid(v)
    return sigma * (1.0 + v * (1.0 - sigma))


def lower_ones(size):
    row_place = lax.broadcasted_iota(jnp.int32, (size, size), 0)
    column_place = lax.broadcasted_iota(jnp.int32, (size, size), 1)
    return (column_place <= row_place).astype(jnp.float32)


def product(left, right, dims):
    return lax.dot_general(left, right, dims, preferred_element_type=jnp.float32)


def chain_step(earlier, later):
    return (earlier[0] * later[0], later[0] * earlier[1] + later[1])


def block_states(rate, lower, h_start, rise_k, step_k, act_k, b_k):
    exponent = rate[None] * rise_k[:, None, :]
    drive = (step_k * act_k)[:, None, :] * b_k[:, :, None]
    lifted = (drive * jnp.exp(-exponent)).reshape(rise_k.shape[0], -1)
    summed = jnp.dot(lower, lifted, precision=FULL_PRECISION).reshape(drive.shape)
    return jnp.exp(exponent) * (h_start[None] + summed)


def fold_blocks(rate, exponent_src, weights, vectors):

    def add_block(running, pieces):
        expo_k, weight_k, vector_k = pieces
        term = (
            jnp.exp(rate[None] * expo_k[:, None, :]) * weight_k[:, None, :] * vector_k[:, :, None]
        )
        return (running + jnp.sum(term, axis=0), None)

    running, _ = lax.scan(
        add_block, jnp.zeros(rate.shape, jnp.float32), (exponent_src, weights, vectors)
    )
    return running


def regroup(v, dim, outer, middle):
    shape = v.shape
    split_shape = shape[:dim] + (outer, middle, shape[dim] // (outer * middle)) + shape[dim + 1 :]
    return jnp.swapaxes(v.reshape(split_shape), dim, dim + 1).reshape(shape)


def local(
    hidden,
    teacher,
    cotangent,
    lengths,
    norm_gain,
    in_weight,
    conv_weight,
    conv_bias,
    x_weight,
    dt_weight,
    dt_bias,
    a_log,
    skip_gain,
    out_weight,
):
    gathered = (
        lax.all_gather(norm_gain, "wsh", axis=0, tiled=True),
        lax.all_gather(in_weight, "wsh", axis=0, tiled=True),
        lax.all_gather(conv_weight, "wsh", axis=1, tiled=True),
        lax.all_gather(conv_bias, "wsh", axis=0, tiled=True),
        lax.all_gather(x_weight, "wsh", axis=1, tiled=True),
        lax.all_gather(dt_weight, "wsh", axis=1, tiled=True),
        lax.all_gather(dt_bias, "wsh", axis=0, tiled=True),
        lax.all_gather(a_log, "wsh", axis=1, tiled=True),
        lax.all_gather(skip_gain, "wsh", axis=0, tiled=True),
        lax.all_gather(out_weight, "wsh", axis=0, tiled=True),
    )
    (
        gain_all,
        in_all,
        conv_all,
        conv_bias_all,
        x_all,
        dt_all,
        dt_bias_all,
        log_rate_all,
        skip_all,
        out_all,
    ) = gathered
    tokens = hidden.shape[1]
    width = hidden.shape[2]
    inner = out_all.shape[0]
    state_size = log_rate_all.shape[0]
    rank = dt_all.shape[0]
    taps = conv_all.shape[0]
    blocks = tokens // SCAN_BLOCK
    seq_count = lax.axis_size("seq")
    shard_count = lax.axis_size("wsh")
    arrange = partial(regroup, outer=shard_count, middle=seq_count)
    rows_in = hidden[0].astype(jnp.float32)
    positions = lax.axis_index("seq") * tokens + lax.iota(jnp.int32, tokens)
    valid = (positions < lengths[0]).astype(jnp.float32)
    gain_f = gain_all.astype(jnp.float32)
    scale = lax.rsqrt(jnp.mean(rows_in * rows_in, axis=1, keepdims=True) + NORM_EPS)
    normalized_input = (rows_in * scale * gain_f).astype(jnp.bfloat16)
    joint_projection = jnp.dot(normalized_input, in_all, preferred_element_type=jnp.float32)
    x_part = (joint_projection[:, :inner] * valid[:, None]).astype(jnp.bfloat16)
    z_part = joint_projection[:, inner:]
    edge = passed_along(x_part[tokens - (taps - 1) :], "seq", 1)
    padded = jnp.concatenate([edge, x_part], axis=0).astype(jnp.float32)
    conv_f = conv_all.astype(jnp.float32)
    conv_out = jnp.broadcast_to(conv_bias_all.astype(jnp.float32), (tokens, inner))
    for tap in range(taps):
        conv_out = conv_out + conv_f[tap] * padded[tap : tap + tokens]
    act_low = silu_value(conv_out).astype(jnp.bfloat16)
    act_use = act_low.astype(jnp.float32)
    proj = product(act_low, x_all, COLS_LAST).astype(jnp.bfloat16)
    dt_low = proj[:, :rank]
    b_in = proj[:, rank : rank + state_size].astype(jnp.float32)
    c_out = proj[:, rank + state_size :].astype(jnp.float32)
    step_arg = jnp.dot(dt_low, dt_all, preferred_element_type=jnp.float32) + dt_bias_all.astype(
        jnp.float32
    )
    step = jax.nn.softplus(step_arg)
    rate = -jnp.exp(log_rate_all.astype(jnp.float32))
    lower = lower_ones(SCAN_BLOCK)

    def to_blocks(v):
        return v.reshape((blocks, SCAN_BLOCK) + v.shape[1:])

    step_b = to_blocks(step)
    act_b = to_blocks(act_use)
    b_blocks = to_blocks(b_in)
    c_blocks = to_blocks(c_out)
    rise = jnp.einsum("qs,kse->kqe", lower, step_b, precision=FULL_PRECISION)
    block_sum = rise[:, -1]
    offsets = jnp.cumsum(block_sum, axis=0) - block_sum
    climb = rise + offsets[:, None]
    device_total = offsets[-1] + block_sum[-1]
    device_decay = jnp.exp(rate * device_total[None])
    zero_state = jnp.zeros(rate.shape, jnp.float32)
    unit_state = jnp.ones(rate.shape, jnp.float32)

    def one_block(h_start, pieces):
        rise_k, step_k, act_k, b_k, c_k = pieces
        states = block_states(rate, lower, h_start, rise_k, step_k, act_k, b_k)
        return (states[-1], (jnp.sum(states * c_k[:, :, None], axis=1), h_start))

    last_zero, (scan_out, starts) = lax.scan(
        one_block, zero_state, (rise, step_b, act_b, b_blocks, c_blocks)
    )
    _, carry_in = carried_in(
        (device_decay, last_zero), "seq", chain_step, (unit_state, zero_state), False
    )
    fix = lax.map(
        lambda item: jnp.sum(
            jnp.exp(rate[None] * item[0][:, None, :]) * carry_in[None] * item[1][:, :, None], axis=1
        ),
        (climb, c_blocks),
    )
    scan_out = scan_out + fix
    starts = starts + jnp.exp(rate[None] * offsets[:, None, :]) * carry_in[None]
    skip_f = skip_all.astype(jnp.float32)
    mixed = scan_out.reshape(tokens, inner) + skip_f * act_use
    gate_z = silu_value(z_part)
    gated_output = (mixed * gate_z).astype(jnp.bfloat16)
    full = rows_in + jnp.dot(gated_output, out_all, preferred_element_type=jnp.float32)
    miss = full - teacher[0].astype(jnp.float32)
    loss_part = jnp.sum(valid[:, None] * miss * miss)
    count_part = jnp.sum(valid)
    loss_sum, count = lax.psum((loss_part, count_part), ("seq", "wsh"))
    loss = loss_sum / (width * count)
    back_set = (in_all, x_all, dt_all, out_all)
    in_back, x_back, dt_back, out_back = back_set
    g_full = cotangent[0].astype(jnp.float32) + 2.0 / (width * count) * valid[:, None] * miss
    g_branch = g_full.astype(jnp.bfloat16)
    out_grad = product(arrange(gated_output, 1), g_branch, ROWS_FIRST)
    g_gated = product(g_branch, out_back, COLS_LAST)
    g_mixed = g_gated * gate_z
    g_z = g_gated * mixed * silu_slope(z_part)
    skip_grad = arrange(jnp.sum(g_mixed * act_use, axis=0), 0)
    dy_blocks = to_blocks(g_mixed)
    chain_value = fold_blocks(rate, climb, dy_blocks, c_blocks)
    _, carry_back = carried_in(
        (device_decay, chain_value), "seq", chain_step, (unit_state, zero_state), True
    )

    def back_block(carry, pieces):
        g_next, rate_sum = carry
        rise_k, step_k, act_k, b_k, c_k, dy_k, h_start = pieces
        exponent = rate[None] * rise_k[:, None, :]
        fall = jnp.exp(exponent)
        lift = jnp.exp(-exponent)
        drive_weight = step_k * act_k
        drive = drive_weight[:, None, :] * b_k[:, :, None]
        summed = jnp.dot(
            lower, (drive * lift).reshape(SCAN_BLOCK, -1), precision=FULL_PRECISION
        ).reshape(drive.shape)
        states = fall * (h_start[None] + summed)
        previous = jnp.concatenate([h_start[None], states[:-1]], axis=0)
        source = dy_k[:, None, :] * c_k[:, :, None]
        back_sum = jnp.dot(
            lower.T, (source * fall).reshape(SCAN_BLOCK, -1), precision=FULL_PRECISION
        ).reshape(drive.shape)
        g_state = lift * (back_sum + fall[-1][None] * g_next[None])
        rate_term = g_state * previous * jnp.exp(rate[None] * step_k[:, None, :])
        along_b = jnp.sum(g_state * b_k[:, :, None], axis=1)
        g_step = jnp.sum(rate_term * rate[None], axis=1) + act_k * along_b
        g_act = step_k * along_b
        g_b = jnp.sum(g_state * drive_weight[:, None, :], axis=2)
        g_c = jnp.sum(states * dy_k[:, None, :], axis=2)
        rate_sum = rate_sum + jnp.sum(rate_term * step_k[:, None, :], axis=0)
        return ((fall[0] * g_state[0], rate_sum), (g_step, g_act, g_b, g_c))

    (_, rate_total), (g_step_b, g_act_b, g_b_b, g_c_b) = lax.scan(
        back_block,
        (carry_back, zero_state),
        (rise, step_b, act_b, b_blocks, c_blocks, dy_blocks, starts),
        reverse=True,
    )
    log_rate_grad = arrange(rate_total * rate, 1)
    g_arg = g_step_b.reshape(tokens, inner) * jax.nn.sigmoid(step_arg)
    dt_bias_grad = arrange(jnp.sum(g_arg, axis=0), 0)
    g_pre = g_arg.astype(jnp.bfloat16)
    dt_grad = product(dt_low, arrange(g_pre, 1), ROWS_FIRST)
    g_dt_low = product(g_pre, dt_back, COLS_LAST)
    g_proj = jnp.concatenate(
        [g_dt_low, g_b_b.reshape(tokens, state_size), g_c_b.reshape(tokens, state_size)], axis=1
    ).astype(jnp.bfloat16)
    x_grad = product(g_proj, arrange(act_low, 1), ROWS_FIRST)
    g_act = (
        g_mixed * skip_f
        + g_act_b.reshape(tokens, inner)
        + jnp.dot(g_proj, x_back, preferred_element_type=jnp.float32)
    )
    g_conv = g_act * silu_slope(conv_out)
    conv_bias_grad = arrange(jnp.sum(g_conv, axis=0), 0)
    conv_grad = arrange(
        jnp.stack([jnp.sum(g_conv * padded[tap : tap + tokens], axis=0) for tap in range(taps)]), 1
    )
    g_padded = jnp.zeros((tokens + taps - 1, inner), jnp.float32)
    for tap in range(taps):
        g_padded = g_padded + jnp.pad(conv_f[tap] * g_conv, ((tap, taps - 1 - tap), (0, 0)))
    back_edge = passed_along(shortened(g_padded[: taps - 1]), "seq", -1)
    g_x_in = g_padded[taps - 1 :] + jnp.concatenate(
        [jnp.zeros((tokens - (taps - 1), inner), jnp.float32), back_edge], axis=0
    )
    g_both = jnp.concatenate([g_x_in * valid[:, None], g_z], axis=1).astype(jnp.bfloat16)
    in_grad = product(arrange(normalized_input, 1), g_both, ROWS_FIRST)
    g_normed = product(g_both, in_back, COLS_LAST)
    gain_grad = arrange(jnp.sum(g_normed * rows_in * scale, axis=0), 0)
    weighted = g_normed * gain_f
    g_rows = (
        g_full
        + scale * weighted
        - rows_in * scale * scale * scale * jnp.mean(weighted * rows_in, axis=1, keepdims=True)
    )
    shares = (
        lax.psum_scatter(gain_grad, "seq", scatter_dimension=0, tiled=True),
        lax.psum_scatter(in_grad, "seq", scatter_dimension=0, tiled=True),
        lax.psum_scatter(conv_grad, "seq", scatter_dimension=1, tiled=True),
        lax.psum_scatter(conv_bias_grad, "seq", scatter_dimension=0, tiled=True),
        lax.psum_scatter(x_grad, "seq", scatter_dimension=1, tiled=True),
        lax.psum_scatter(dt_grad, "seq", scatter_dimension=1, tiled=True),
        lax.psum_scatter(dt_bias_grad, "seq", scatter_dimension=0, tiled=True),
        lax.psum_scatter(log_rate_grad, "seq", scatter_dimension=1, tiled=True),
        lax.psum_scatter(skip_grad, "seq", scatter_dimension=0, tiled=True),
        lax.psum_scatter(out_grad, "seq", scatter_dimension=0, tiled=True),
    )
    shares = (
        lax.psum_scatter(shares[0], "wsh", scatter_dimension=0, tiled=True),
        lax.psum_scatter(shares[1], "wsh", scatter_dimension=0, tiled=True),
        lax.psum_scatter(shares[2], "wsh", scatter_dimension=1, tiled=True),
        lax.psum_scatter(shares[3], "wsh", scatter_dimension=0, tiled=True),
        lax.psum_scatter(shares[4], "wsh", scatter_dimension=1, tiled=True),
        lax.psum_scatter(shares[5], "wsh", scatter_dimension=1, tiled=True),
        lax.psum_scatter(shares[6], "wsh", scatter_dimension=0, tiled=True),
        lax.psum_scatter(shares[7], "wsh", scatter_dimension=1, tiled=True),
        lax.psum_scatter(shares[8], "wsh", scatter_dimension=0, tiled=True),
        lax.psum_scatter(shares[9], "wsh", scatter_dimension=0, tiled=True),
    )
    owned = (
        lax.all_gather(shares[0], "seq", axis=0, tiled=True),
        lax.all_gather(shares[1], "seq", axis=0, tiled=True),
        lax.all_gather(shares[2], "seq", axis=1, tiled=True),
        lax.all_gather(shares[3], "seq", axis=0, tiled=True),
        lax.all_gather(shares[4], "seq", axis=1, tiled=True),
        lax.all_gather(shares[5], "seq", axis=1, tiled=True),
        lax.all_gather(shares[6], "seq", axis=0, tiled=True),
        lax.all_gather(shares[7], "seq", axis=1, tiled=True),
        lax.all_gather(shares[8], "seq", axis=0, tiled=True),
        lax.all_gather(shares[9], "seq", axis=0, tiled=True),
    )
    return (
        full[None].astype(jnp.bfloat16),
        loss,
        g_rows[None].astype(jnp.bfloat16),
        owned[0],
        owned[1],
        owned[2],
        owned[3],
        owned[4],
        owned[5],
        owned[6],
        owned[7],
        owned[8],
        owned[9],
    )


def solution(mesh):
    placed = (
        P("wsh", "seq", None),
        P("wsh", "seq", None),
        P("wsh", "seq", None),
        P("wsh"),
        P("wsh"),
        P("wsh", None),
        P(None, "wsh"),
        P("wsh"),
        P(None, "wsh"),
        P(None, "wsh"),
        P("wsh"),
        P(None, "wsh"),
        P("wsh"),
        P("wsh", None),
    )
    return jax.shard_map(
        local,
        mesh=mesh,
        in_specs=placed,
        out_specs=(
            P("wsh", "seq", None),
            P(),
            P("wsh", "seq", None),
            P("wsh"),
            P("wsh", None),
            P(None, "wsh"),
            P("wsh"),
            P(None, "wsh"),
            P(None, "wsh"),
            P("wsh"),
            P(None, "wsh"),
            P("wsh"),
            P("wsh", None),
        ),
        check_vma=False,
    )
```

profile of v0, /device:TPU:0, one launch (start us, length us, event | category | flops | bytes accessed | tf_op | source)
XLA Modules:
  0.0 4317.4 jit_solution(2337657159534583440)
XLA Ops:
  22.8 191.1 %all-gather.17.cloned.1.call-done = bf16[2048,8192]{1,0:T(8,128)(2,1)} async-done(((bf16[512,8192]{1,0:T(8,128)(2,1)}), bf16[2048,8192]{1,0:T(8,128)(2,1)}) %all-gather.17.cloned.1.call-update) | async-done | bytes 33554448 | tf_op jit(solution)/shard_map/all_gather | solution.py:115
  213.9 17.6 fusion.61
  281.2 368.0 %while.93 = (s32[]{:T(128)}, f32[16,4096]{1,0:T(8,128)S(1)}, f32[8,32,4096]{2,1,0:T(8,128)}, f32[8,16,4096]{2,1,0:T(8,128)}, f32[16,4096]{1,0:T(8,128)S(1)}, /*i...) while((s32[]{:T(128)}, f32[16,4096]{1,0:T(8,128)S(1)}, ...), condition=%wide.region_3.4_spmd.clone, body=%wide.region_1.0_spmd.clone.sunk | while | flops 824182784 | bytes 117190784 | solution.py:196
  663.3 35.2 all-gather.31.cloned.1.call-done
  711.7 43.2 %while.92 = (s32[]{:T(128)}, f32[8,32,4096]{2,1,0:T(8,128)}, f32[16,4096]{1,0:T(8,128)S(1)}, f32[8,32,4096]{2,1,0:T(8,128)}, f32[16,4096]{1,0:T(8,128)S(1)}, /*index=5*/f32[8,32,16]{1,2,0:T(8,128)}, s32[]{:T(128)}) while((s32[]{:T(128)}, f32[8,32,4096]{2,1,0:T(8,128)}, f32[16,4096]{1,0:T(8,128)S(1)}, f32[8,32,4096]{2,1,0:T(8,128)}, ...), condition=%wide.region_9.10_spmd, body=%wide.region_7.9_spmd.sunk | while | flops 8257538 | bytes 3680353 | solution.py:202
  766.4 38.0 all-gather.23.cloned.1.call-done
  817.7 39.8 all-reduce.14
  878.2 31.2 while.95
  937.2 23.3 all-gather.33.cloned.1.call-done
  977.1 1334.9 %while.97 = (s32[]{:T(128)}, f32[16,4096]{1,0:T(8,128)S(1)}, f32[16,4096]{1,0:T(8,128)}, f32[8,32,4096]{2,1,0:T(8,128)}, f32[8,32,4096]{2,1,0:T(8,128)}, /*index...) while((s32[]{:T(128)}, f32[16,4096]{1,0:T(8,128)S(1)}, ...), condition=%wide.region_25.26_spmd.clone.clone, body=%wide.region_19.25_spmd.clone.clone.sunk | while | flops 1686572032 | bytes 479758848 | solution.py:262
  1099.3 16.4 multiply_reduce_fusion.20
  1265.3 16.4 multiply_reduce_fusion.20
  1431.9 16.4 multiply_reduce_fusion.20
  1928.7 16.4 multiply_reduce_fusion.20
  2352.0 26.3 fusion.45
  2399.9 1034.3 %reduce-scatter.17.cloned.1.call-done = f32[256,8192]{1,0:T(8,128)} async-done(((f32[2048,8192]{1,0:T(8,128)}), f32[256,8192]{1,0:T(8,128)}) %reduce-scatter.17.cloned.1.call-update) | async-done | bytes 8388624 | tf_op jit(solution)/shard_map/reduce_scatter | solution.py:307
  3434.3 70.2 %reduce-scatter.37.cloned.1.call-done = f32[512,4]{1,0:T(8,128)} async-done(((f32[4096,4]{1,0:T(8,128)}), f32[512,4]{1,0:T(8,128)}) %reduce-scatter.37.cloned.1.call-update) | async-done | bytes 8208
  3504.6 64.2 %reduce-scatter.29.cloned.1.call-done = f32[16,512]{1,0:T(8,128)} async-done(((f32[16,4096]{1,0:T(8,128)}), f32[16,512]{1,0:T(8,128)}) %reduce-scatter.29.cloned.1.call-update) | async-done | bytes 32784 | tf_op jit(solution)/shard_map/reduce_scatter | solution.py:313
  3568.8 70.5 %reduce-scatter.25.cloned.1.call-done = f32[128,512]{1,0:T(8,128)} async-done(((f32[128,4096]{1,0:T(8,128)}), f32[128,512]{1,0:T(8,128)}) %reduce-scatter.25.cloned.1.call-update) | async-done | bytes 262160 | tf_op jit(solution)/shard_map/reduce_scatter | solution.py:311
  3639.4 74.1 %reduce-scatter.21.cloned.1.call-done = f32[160,512]{1,0:T(8,128)} async-done(((f32[160,4096]{1,0:T(8,128)}), f32[160,512]{1,0:T(8,128)}) %reduce-scatter.21.cloned.1.call-update) | async-done | bytes 327696 | tf_op jit(solution)/shard_map/reduce_scatter | solution.py:310
  3713.6 45.7 %reduce-scatter.35.cloned.1.call-done = f32[128,2048]{1,0:T(8,128)} async-done(((f32[512,2048]{1,0:T(8,128)}), f32[128,2048]{1,0:T(8,128)}) %reduce-scatter.35.cloned.1.call-update) | async-done | bytes 1048592 | tf_op jit(solution)/shard_map/reduce_scatter | solution.py:327
  3759.3 74.3 %reduce-scatter.19.cloned.1.call-done = f32[64,8192]{1,0:T(8,128)} async-done(((f32[256,8192]{1,0:T(8,128)}), f32[64,8192]{1,0:T(8,128)}) %reduce-scatter.19.cloned.1.call-update) | async-done | bytes 2097168 | tf_op jit(solution)/shard_map/reduce_scatter | solution.py:319
  3841.2 17.0 fusion.58
  3858.3 21.6 all-reduce.6
  3886.1 33.4 all-reduce.15
  3925.7 18.5 all-gather.4
  3960.7 18.4 all-gather.6
  3983.3 26.5 all_gather.98
  4009.7 31.1 all_gather.103
  4040.9 32.7 all_gather.101
  4073.6 34.1 all_gather.100
  4107.6 180.3 %all-gather.25.cloned.1.call-done = f32[512,8192]{1,0:T(8,128)} async-done(((f32[64,8192]{1,0:T(8,128)}), f32[512,8192]{1,0:T(8,128)}) %all-gather.25.cloned.1.call-update) | async-done | bytes 16777232 | tf_op jit(solution)/shard_map/all_gather | solution.py:331
  (943 shorter events, 2003.7 us)
Async XLA Ops:
  7.2 206.7 %all-gather.17.cloned.1.call-start = ((), (), s32[]{:S(2)}) async-start(), calls=%async_computation.12 | async-start | bytes 41943040 | tf_op jit(solution)/shard_map/all_gather | solution.py:115
  7.9 252.4 %all-gather.19.cloned.1.call-start = ((), (), s32[]{:S(2)}) async-start(), calls=%async_computation.13 | async-start | bytes 1638400 | tf_op jit(solution)/shard_map/all_gather | solution.py:118
  8.7 254.7 %all-gather.21.cloned.1.call-start = ((), (), s32[]{:S(2)}) async-start(), calls=%async_computation.14 | async-start | bytes 1310720 | tf_op jit(solution)/shard_map/all_gather | solution.py:119
  9.4 653.9 %all-gather.29.cloned.1.call-start = ((), (), s32[]{:S(2)}) async-start(), calls=%async_computation.28 | async-start | bytes 2359296 | tf_op jit(solution)/shard_map/all_gather | solution.py:25
  22.7 231.6 %copy-start.44 = (f32[1,4096]{1,0:T(1,128)}, f32[1,4096]{1,0:T(1,128)S(1)}, u32[]{:S(2)}) copy-start(f32[1,4096]{1,0:T(1,128)S(1)} %get-tuple-element.1194) | copy-start | bytes 49156
  22.7 231.6 %copy-start.46 = (f32[1,4096]{1,0:T(1,128)}, f32[1,4096]{1,0:T(1,128)S(1)}, u32[]{:S(2)}) copy-start(f32[1,4096]{1,0:T(1,128)S(1)} %get-tuple-element.1195) | copy-start | bytes 49156
  22.7 231.6 %copy-start.48 = (f32[1,4096]{1,0:T(1,128)}, f32[1,4096]{1,0:T(1,128)S(1)}, u32[]{:S(2)}) copy-start(f32[1,4096]{1,0:T(1,128)S(1)} %get-tuple-element.1196) | copy-start | bytes 49156
  234.2 19.4 collective-permute-start
  278.7 419.8 %all-gather.31.cloned.1.call-start = ((), (), s32[]{:S(2)}) async-start(), calls=%async_computation.29 | async-start | bytes 2359296 | tf_op jit(solution)/shard_map/all_gather | solution.py:25
  650.0 154.4 %all-gather.23.cloned.1.call-start = ((), (), s32[]{:S(2)}) async-start(), calls=%async_computation.15 | async-start | bytes 20971520 | tf_op jit(solution)/shard_map/all_gather | solution.py:123
  650.5 309.9 %all-gather.33.cloned.1.call-start = ((), (), s32[]{:S(2)}) async-start(), calls=%async_computation.30 | async-start | bytes 2359296 | tf_op jit(solution)/shard_map/all_gather | solution.py:25
  910.1 1489.3 %reduce-scatter.33.cloned.1.call-start = ((), (), s32[]{:S(2)}) async-start(), calls=%async_computation.25 | async-start | bytes 37748736 | tf_op jit(solution)/shard_map/reduce_scatter | solution.py:315
  937.1 2497.1 %reduce-scatter.17.cloned.1.call-start = ((), (), s32[]{:S(2)}) async-start(), calls=%async_computation.16 | async-start | bytes 75497472 | tf_op jit(solution)/shard_map/reduce_scatter | solution.py:307
  977.1 1336.7 %copy-start.40 = (f32[4096]{0:T(1024)S(1)}, f32[4096]{0:T(1024)}, u32[]{:S(2)}) copy-start(f32[4096]{0:T(1024)} %copy-done.39) | copy-start | bytes 49156
  2345.5 5.8 collective-permute-start.1
  2378.3 1126.2 %reduce-scatter.37.cloned.1.call-start = ((), (), s32[]{:S(2)}) async-start(), calls=%async_computation.31 | async-start | bytes 2359296
  2380.4 1188.3 %reduce-scatter.29.cloned.1.call-start = ((), (), s32[]{:S(2)}) async-start(), calls=%async_computation.23 | async-start | bytes 294912 | tf_op jit(solution)/shard_map/reduce_scatter | solution.py:313
  2381.5 1257.8 %reduce-scatter.25.cloned.1.call-start = ((), (), s32[]{:S(2)}) async-start(), calls=%async_computation.21 | async-start | bytes 2359296 | tf_op jit(solution)/shard_map/reduce_scatter | solution.py:311
  2392.1 1321.4 %reduce-scatter.21.cloned.1.call-start = ((), (), s32[]{:S(2)}) async-start(), calls=%async_computation.19 | async-start | bytes 2949120 | tf_op jit(solution)/shard_map/reduce_scatter | solution.py:310
  2399.3 1360.0 %reduce-scatter.35.cloned.1.call-start = ((), (), s32[]{:S(2)}) async-start(), calls=%async_computation.26 | async-start | bytes 5242880 | tf_op jit(solution)/shard_map/reduce_scatter | solution.py:327
  2399.9 1433.7 %reduce-scatter.19.cloned.1.call-start = ((), (), s32[]{:S(2)}) async-start(), calls=%async_computation.17 | async-start | bytes 10485760 | tf_op jit(solution)/shard_map/reduce_scatter | solution.py:319
  3434.2 399.4 %copy-start.67 = (u32[32]{0:T(128)S(1)}, u32[32]{0:T(128)}, u32[]{:S(2)}) copy-start(u32[32]{0:T(128)} %constant.220) | copy-start | bytes 388
  3434.2 400.0 %copy-start.65 = (u32[32]{0:T(128)S(1)}, u32[32]{0:T(128)}, u32[]{:S(2)}) copy-start(u32[32]{0:T(128)} %constant.210) | copy-start | bytes 388
  3434.2 404.5 %copy-start.55 = (f32[4096]{0:T(1024)S(1)}, f32[4096]{0:T(1024)}, u32[]{:S(2)}) copy-start(f32[4096]{0:T(1024)} %get-tuple-element.1160) | copy-start | bytes 49156
  3434.3 548.1 %reduce-scatter.39.cloned.1.call-start = ((), (), s32[]{:S(2)}) async-start(), calls=%async_computation.32 | async-start | bytes 327680
  3504.5 336.6 %copy-start.20 = (bf16[1,256,2048]{2,1,0:T(8,128)(2,1)S(1)}, bf16[1,256,2048]{2,1,0:T(8,128)(2,1)}, u32[]{:S(2)}) copy-start(bf16[1,256,2048]{2,1,0:T(8,128)(2,1)} %param.26) | copy-start | bytes 3145732
  3504.5 336.6 %copy-start.53 = (f32[4,1,512]{2,1,0:T(1,128)S(1)}, f32[4,1,512]{2,1,0:T(1,128)}, u32[]{:S(2)}) copy-start(f32[4,1,512]{2,1,0:T(1,128)} %copy-done.52) | copy-start | bytes 24580
  3504.5 505.2 %reduce-scatter.31.cloned.1.call-start = ((), (), s32[]{:S(2)}) async-start(), calls=%async_computation.24 | async-start | bytes 40960 | tf_op jit(solution)/shard_map/reduce_scatter | solution.py:325
  3568.8 472.1 %reduce-scatter.27.cloned.1.call-start = ((), (), s32[]{:S(2)}) async-start(), calls=%async_computation.22 | async-start | bytes 327680 | tf_op jit(solution)/shard_map/reduce_scatter | solution.py:323
  3639.3 434.2 %reduce-scatter.23.cloned.1.call-start = ((), (), s32[]{:S(2)}) async-start(), calls=%async_computation.20 | async-start | bytes 409600 | tf_op jit(solution)/shard_map/reduce_scatter | solution.py:322
  3713.5 394.1 %all-gather.27.cloned.1.call-start = ((), (), s32[]{:S(2)}) async-start(), calls=%async_computation.27 | async-start | bytes 9437184 | tf_op jit(solution)/shard_map/all_gather | solution.py:339
  3759.3 528.6 %all-gather.25.cloned.1.call-start = ((), (), s32[]{:S(2)}) async-start(), calls=%async_computation.18 | async-start | bytes 18874368 | tf_op jit(solution)/shard_map/all_gather | solution.py:331
  (133 other events, 2258.3 us)
Sparse Core Ops, SparseCore 0:
  9.6 204.2 all-gather.16
  215.4 18.1 all-gather.18
  235.2 16.7 all-gather.20
  278.8 48.3 all-gather.28
  650.1 48.3 all-gather.30
  699.9 104.3 all-gather.22
  910.2 50.2 all-gather.32
  964.2 541.5 reduce-scatter.32
  2378.4 1055.7 reduce-scatter.16
  3437.6 66.8 reduce-scatter.36
  3508.4 60.2 reduce-scatter.28
  3572.1 67.1 reduce-scatter.24
  3643.4 70.0 reduce-scatter.20
  3715.9 43.3 reduce-scatter.34
  3761.9 71.6 reduce-scatter.18
  3835.9 20.0 reduce-scatter.38
  3858.4 19.3 reduce-scatter.30
  3880.1 20.0 reduce-scatter.26
  3902.8 20.4 reduce-scatter.22
  3925.2 131.7 all-gather.26
  4059.1 228.7 all-gather.24
where the time goes:
time: 4330 us; the launch traced here: 4320 us
  waiting for transfers between devices  1910 us (44%)
  local copies, waits for them, and re-layouts  1050 us (24%)
  other arithmetic  590 us (14%)
  matrix products  394 us (9%)
  blocking collectives  317 us (7%)
    reduce_scatter x1, waiting for transfers between devices, local(): lax.psum_scatter(in_grad, 'seq', scatter_dimension=0, tiled=True)  1030 us
    while x280, local copies, waits for them, and re-layouts  743 us
    all_gather x1, waiting for transfers between devices, local(): lax.all_gather(in_weight, 'wsh', axis=0, tiled=True)  191 us
    all_gather x1, waiting for transfers between devices, local(): lax.all_gather(shares[1], 'seq', axis=0, tiled=True)  180 us
    reduce_sum x8, other arithmetic, back_block(): g_b = jnp.sum(g_state * drive_weight[:, None, :], axis=2)  131 us
    dot_general x8, matrix products, back_block(): jnp.dot(lower.T, (source * fall).reshape(SCAN_BLOCK, -1), precision=FULL_...  89.9 us
    reduce_sum x8, other arithmetic, back_block(): rate_sum = rate_sum + jnp.sum(rate_term * step_k[:, None, :], axis=0)  87.7 us
    dot_general x8, matrix products, back_block(): jnp.dot(lower, (drive * lift).reshape(SCAN_BLOCK, -1), precision=FULL_PRE...  87.1 us
  transfers between devices with their start and end apart: 23, of which 13 were waited for; matrix products, arithmetic and copies ran while one was open for 44% of the time, Pallas kernels for 0%

commit v1 on v0

v1 whole, which is shorter than its diff:
```python
from functools import partial

import jax
import jax.numpy as jnp
from jax import lax
from jax.experimental import pallas as pl
from jax.experimental.pallas import tpu as pltpu
from jax.sharding import PartitionSpec as P

F32 = jnp.float32
BF16 = jnp.bfloat16
NORM_EPS = 1e-05
LOG2E = 1.4426950408889634
LN2 = 0.6931471805599453
GROUP = 8
CHUNK = 32
HALO = 16
VMEM_LIMIT = 56 * 1024 * 1024
ROWS_FIRST = (((0,), (0,)), ((), ()))
COLS_LAST = (((1,), (1,)), ((), ()))
PLAIN = (((1,), (0,)), ((), ()))


def product(left, right, dims):
    return lax.dot_general(left, right, dims, preferred_element_type=F32)


def silu_value(v):
    return v * jax.nn.sigmoid(v)


def silu_slope(v):
    sigma = jax.nn.sigmoid(v)
    return sigma * (1.0 + v * (1.0 - sigma))


def kernel_params():
    return pltpu.CompilerParams(vmem_limit_bytes=VMEM_LIMIT)


def widen(bc_ref, row, size, rep_ref):
    for t0 in range(0, bc_ref.shape[1], 128):
        x=bc_ref[row:row+size, t0:t0+128]
        for k in range(128):
            rep_ref[t0+k]=jnp.broadcast_to(x[:, k:k+1], (size, 128))

def tiled(x, width):
    return jnp.concatenate([x]*(width//128), axis=1)

def put_fold(fold_ref,k,v):
    for i in range(v.shape[1]//128):
        fold_ref[i,8*k:8*k+8,:]=v[:,128*i:128*i+128]

def get_fold(fold_ref):
    def tree(x):
        while len(x)>1: x=[a+b for a,b in zip(x[::2],x[1::2])]
        return x[0]
    return jnp.concatenate([tree([fold_ref[i,pl.ds(r,GROUP,stride=8),:] for r in range(8)]) for i in range(fold_ref.shape[0])],axis=1)

def p1_kernel(step_ref, act_ref, bc_ref, rate_ref, last_ref, total_ref, dx_ref, brep_ref, *, eb, n):
    widen(bc_ref,0,n,brep_ref)
    step=step_ref[...]
    dx_ref[...]=step*act_ref[...].astype(F32)
    total_ref[0]=jnp.sum(step,axis=0,keepdims=True)
    tokens,width=step_ref.shape
    for e in range(0,width,eb):
        sl=slice(e,e+eb)
        rate=rate_ref[:,sl]
        def group(g,h):
            base=pl.multiple_of(g*GROUP,GROUP)
            s8=step_ref[pl.ds(base,GROUP),sl]
            x8=dx_ref[pl.ds(base,GROUP),sl]
            for k in range(GROUP):
                d=jnp.exp2(rate*s8[k:k+1])
                h=d*h+tiled(brep_ref[base+k],eb)*x8[k:k+1]
            return h
        last_ref[0,:,sl]=lax.fori_loop(0,tokens//GROUP,group,jnp.zeros((n,eb),F32))

def p1(step,act,bc,rate,seqs,eb=512):
    rows,width=step.shape; tokens=rows//seqs; n=rate.shape[0]
    return pl.pallas_call(partial(p1_kernel,eb=eb,n=n),grid=(seqs,),
        in_specs=[pl.BlockSpec((tokens,width),lambda s:(s,0)),pl.BlockSpec((tokens,width),lambda s:(s,0)),
                  pl.BlockSpec((bc.shape[0],tokens),lambda s:(0,s)),pl.BlockSpec((n,width),lambda s:(0,0))],
        out_specs=[pl.BlockSpec((1,n,width),lambda s:(s,0,0)),pl.BlockSpec((1,1,width),lambda s:(s,0,0))],
        out_shape=[jax.ShapeDtypeStruct((seqs,n,width),F32),jax.ShapeDtypeStruct((seqs,1,width),F32)],
        scratch_shapes=[pltpu.VMEM((tokens,width),F32),pltpu.VMEM((tokens,n,128),F32)],
        compiler_params=kernel_params())(step,act,bc,rate)

def p2_kernel(step_ref, act_ref, z_ref, bc_ref, rate_ref, skip_ref, carry_ref, mixed_ref, gated_ref, starts_ref, dx_ref, fold_ref, brep_ref, crep_ref, *, eb, n):
    widen(bc_ref,0,n,brep_ref)
    widen(bc_ref,n,n,crep_ref)
    dx_ref[...]=step_ref[...]*act_ref[...].astype(F32)
    tokens,width=step_ref.shape
    for e in range(0,width,eb):
        sl=slice(e,e+eb)
        rate=rate_ref[:,sl]
        def chunk(c,h):
            starts_ref[0,c,:,sl]=h
            def group(j,h):
                g=c*(CHUNK//GROUP)+j
                base=pl.multiple_of(g*GROUP,GROUP)
                s8=step_ref[pl.ds(base,GROUP),sl]
                x8=dx_ref[pl.ds(base,GROUP),sl]
                for k in range(GROUP):
                    d=jnp.exp2(rate*s8[k:k+1])
                    h=d*h+tiled(brep_ref[base+k],eb)*x8[k:k+1]
                    p=tiled(crep_ref[base+k],eb)*h
                    put_fold(fold_ref,k,sum(p[8*i:8*i+8] for i in range(n//8)))
                mixed_ref[pl.ds(base,GROUP),sl]=get_fold(fold_ref)
                return h
            return lax.fori_loop(0,CHUNK//GROUP,group,h)
        lax.fori_loop(0,tokens//CHUNK,chunk,carry_ref[0,:,sl])
    def gate(i,_):
        rows=pl.ds(pl.multiple_of(i*16,16),16)
        m=mixed_ref[rows,:]+skip_ref[...]*act_ref[rows,:].astype(F32)
        mixed_ref[rows,:]=m
        z=z_ref[rows,:]
        gated_ref[rows,:]=(m*(z*jax.nn.sigmoid(z))).astype(BF16)
        return 0
    lax.fori_loop(0,tokens//16,gate,0)

def p2(step,act,z,bc,rate,skip,carry,seqs,eb=512):
    rows,width=step.shape; tokens=rows//seqs; n=rate.shape[0]
    blk=pl.BlockSpec((tokens,width),lambda s:(s,0))
    nch=tokens//CHUNK
    return pl.pallas_call(partial(p2_kernel,eb=eb,n=n),grid=(seqs,),
        in_specs=[blk,blk,blk,pl.BlockSpec((bc.shape[0],tokens),lambda s:(0,s)),pl.BlockSpec((n,width),lambda s:(0,0)),
                  pl.BlockSpec((1,width),lambda s:(0,0)),pl.BlockSpec((1,n,width),lambda s:(s,0,0))],
        out_specs=[blk,blk,pl.BlockSpec((1,nch,n,width),lambda s:(s,0,0,0))],
        out_shape=[jax.ShapeDtypeStruct((rows,width),F32),jax.ShapeDtypeStruct((rows,width),BF16),jax.ShapeDtypeStruct((seqs,nch,n,width),F32)],
        scratch_shapes=[pltpu.VMEM((tokens,width),F32),pltpu.VMEM((eb//128,64,128),F32),pltpu.VMEM((tokens,n,128),F32),pltpu.VMEM((tokens,n,128),F32)],
        compiler_params=kernel_params())(step,act,z,bc,rate,skip,carry)

def b1_kernel(step_ref, dy_ref, bc_ref, rate_ref, first_ref, crep_ref, *, eb, n):
    widen(bc_ref,n,n,crep_ref)
    tokens,width=step_ref.shape
    for e in range(0,width,eb):
        sl=slice(e,e+eb)
        rate=rate_ref[:,sl]
        def group(j,h):
            g=tokens//GROUP-1-j
            base=pl.multiple_of(g*GROUP,GROUP)
            s8=step_ref[pl.ds(base,GROUP),sl]
            y8=dy_ref[pl.ds(base,GROUP),sl]
            for k in reversed(range(GROUP)):
                h=jnp.exp2(rate*s8[k:k+1])*(h+tiled(crep_ref[base+k],eb)*y8[k:k+1])
            return h
        first_ref[0,:,sl]=lax.fori_loop(0,tokens//GROUP,group,jnp.zeros((n,eb),F32))

def b1(step,dy,bc,rate,seqs,eb=512):
    rows,width=step.shape; tokens=rows//seqs; n=rate.shape[0]
    blk=pl.BlockSpec((tokens,width),lambda s:(s,0))
    return pl.pallas_call(partial(b1_kernel,eb=eb,n=n),grid=(seqs,),
        in_specs=[blk,blk,pl.BlockSpec((bc.shape[0],tokens),lambda s:(0,s)),pl.BlockSpec((n,width),lambda s:(0,0))],
        out_specs=pl.BlockSpec((1,n,width),lambda s:(s,0,0)),
        out_shape=jax.ShapeDtypeStruct((seqs,n,width),F32),
        scratch_shapes=[pltpu.VMEM((tokens,n,128),F32)],
        compiler_params=kernel_params())(step,dy,bc,rate)

def one_less_exp(s):
    return jnp.where(s<0.01, s*(1.0-s*(0.5-s*(1.0/6.0))), 1.0-jnp.exp(-s))

def b2_kernel(step_ref, act_ref, dy_ref, bc_ref, rate_ref, skip_ref, starts_ref, carry_ref,
              gpre_ref, gact_ref, gb_ref, gc_ref, alog_ref, dtb_ref,
              dx_ref, prev_ref, dec_ref, folda_ref, folds_ref, pb_ref, pc_ref, g_ref, brep_ref, crep_ref, *, eb, n):
    widen(bc_ref,0,n,brep_ref)
    widen(bc_ref,n,n,crep_ref)
    tokens,width=step_ref.shape
    nch=tokens//CHUNK; per=CHUNK//GROUP
    dx_ref[...]=step_ref[...]*act_ref[...].astype(F32)
    g_ref[...]=carry_ref[0]
    @pl.when(pl.program_id(0)==0)
    def _():
        alog_ref[...]=jnp.zeros_like(alog_ref)
        dtb_ref[...]=jnp.zeros_like(dtb_ref)
    ones=jnp.ones((8,128),F32)
    def chunk(cc,_):
        c=nch-1-cc
        for e in range(0,width,eb):
            sl=slice(e,e+eb)
            rate=rate_ref[:,sl]
            def redo(j,h):
                g=c*per+j
                base=pl.multiple_of(g*GROUP,GROUP)
                s8=step_ref[pl.ds(base,GROUP),sl]
                x8=dx_ref[pl.ds(base,GROUP),sl]
                for k in range(GROUP):
                    d=jnp.exp2(rate*s8[k:k+1])
                    prev_ref[j*GROUP+k]=h
                    dec_ref[j*GROUP+k]=d
                    h=d*h+tiled(brep_ref[base+k],eb)*x8[k:k+1]
                return h
            last=lax.fori_loop(0,per,redo,starts_ref[0,c,:,sl])
            def back(jj,carry):
                h,alog,after=carry
                j=per-1-jj
                g=c*per+j
                base=pl.multiple_of(g*GROUP,GROUP)
                s8=step_ref[pl.ds(base,GROUP),sl]
                x8=dx_ref[pl.ds(base,GROUP),sl]
                y8=dy_ref[pl.ds(base,GROUP),sl]
                for k in reversed(range(GROUP)):
                    s=s8[k:k+1]
                    g_state=tiled(crep_ref[base+k],eb)*y8[k:k+1]+h
                    prev=prev_ref[j*GROUP+k]
                    pc=after*y8[k:k+1]
                    pb=g_state*x8[k:k+1]
                    al=g_state*tiled(brep_ref[base+k],eb)
                    h=g_state*dec_ref[j*GROUP+k]
                    q=h*prev
                    alog=alog+q*s
                    qs=q*rate
                    pcs=sum(pc[:,i:i+128] for i in range(0,eb,128))
                    pbs=sum(pb[:,i:i+128] for i in range(0,eb,128))
                    rows=pl.ds(pl.multiple_of((j*GROUP+k)*n,n),n)
                    if e==0:
                        pc_ref[rows,:]=pcs; pb_ref[rows,:]=pbs
                    else:
                        pc_ref[rows,:]+=pcs; pb_ref[rows,:]+=pbs
                    put_fold(folda_ref,k,sum(al[8*i:8*i+8] for i in range(n//8)))
                    put_fold(folds_ref,k,sum(qs[8*i:8*i+8] for i in range(n//8)))
                    after=prev
                gact_ref[pl.ds(base,GROUP),sl]=get_fold(folda_ref)
                dx_ref[pl.ds(base,GROUP),sl]=get_fold(folds_ref)
                return h,alog,after
            h,alog,_u=lax.fori_loop(0,per,back,(g_ref[:,sl],jnp.zeros((n,eb),F32),last))
            g_ref[:,sl]=h
            alog_ref[:,sl]+=alog
        for j in range(per):
            part=pb_ref[j*128:(j+1)*128,:]
            gb_ref[0,pl.ds(c*per+j,1),:]=lax.dot_general(ones,part,(((1,),(1,)),((),())),precision=lax.Precision.HIGHEST,preferred_element_type=F32)[0:1]
            part=pc_ref[j*128:(j+1)*128,:]
            gc_ref[0,pl.ds(c*per+j,1),:]=lax.dot_general(ones,part,(((1,),(1,)),((),())),precision=lax.Precision.HIGHEST,preferred_element_type=F32)[0:1]
        return 0
    lax.fori_loop(0,nch,chunk,0)
    def finish(i,acc):
        rows=pl.ds(pl.multiple_of(i*16,16),16)
        s=step_ref[rows,:]; along=gact_ref[rows,:]
        a=act_ref[rows,:].astype(F32)
        garg=(dx_ref[rows,:]*LN2+a*along)*one_less_exp(s)
        gpre_ref[rows,:]=garg.astype(BF16)
        gact_ref[rows,:]=dy_ref[rows,:]*skip_ref[...]+s*along
        return acc+jnp.sum(garg.reshape(2,8,width),axis=0)
    acc=lax.fori_loop(0,tokens//16,finish,jnp.zeros((8,width),F32))
    dtb_ref[...]+=acc

def b2(step,act,dy,bc,rate,skip,starts,carry,seqs,eb=512):
    rows,width=step.shape; tokens=rows//seqs; n=rate.shape[0]
    blk=pl.BlockSpec((tokens,width),lambda s:(s,0))
    nch=tokens//CHUNK
    full=lambda shape: pl.BlockSpec(shape,lambda s:(0,)*len(shape))
    red=pl.BlockSpec((1,tokens//GROUP,128),lambda s:(s,0,0))
    return pl.pallas_call(partial(b2_kernel,eb=eb,n=n),grid=(seqs,),
        in_specs=[blk,blk,blk,pl.BlockSpec((bc.shape[0],tokens),lambda s:(0,s)),full((n,width)),full((1,width)),
                  pl.BlockSpec((1,nch,n,width),lambda s:(s,0,0,0)),pl.BlockSpec((1,n,width),lambda s:(s,0,0))],
        out_specs=[blk,blk,red,red,full((n,width)),full((8,width))],
        out_shape=[jax.ShapeDtypeStruct((rows,width),BF16),jax.ShapeDtypeStruct((rows,width),F32),
                   jax.ShapeDtypeStruct((seqs,tokens//GROUP,128),F32),jax.ShapeDtypeStruct((seqs,tokens//GROUP,128),F32),
                   jax.ShapeDtypeStruct((n,width),F32),jax.ShapeDtypeStruct((8,width),F32)],
        scratch_shapes=[pltpu.VMEM((tokens,width),F32),pltpu.VMEM((CHUNK,n,eb),F32),pltpu.VMEM((CHUNK,n,eb),F32),
                        pltpu.VMEM((eb//128,64,128),F32),pltpu.VMEM((eb//128,64,128),F32),pltpu.VMEM((CHUNK*n,128),F32),pltpu.VMEM((CHUNK*n,128),F32),
                        pltpu.VMEM((n,width),F32),pltpu.VMEM((tokens,n,128),F32),pltpu.VMEM((tokens,n,128),F32)],
        compiler_params=kernel_params())(step,act,dy,bc,rate,skip,starts,carry)


def swap(v, bit):
    return jax.tree.map(
        lambda a: lax.ppermute(a, "wsh", [(i, i ^ bit) for i in range(lax.axis_size("wsh"))]), v
    )


def shifted(v, distance):
    count = lax.axis_size("seq")
    route = [(i - distance, i) for i in range(count) if 0 <= i - distance < count]
    return jax.tree.map(lambda a: lax.ppermute(a, "seq", route), v)


def spread_out(v):
    one = swap(v, 1)
    two = swap(v, 2)
    return [v, one, two, swap(two, 1)]


def sum_to_owner(parts, own_cast=BF16):
    got1, got3 = swap((parts[1].astype(own_cast), parts[3].astype(own_cast)), 1)
    mine = parts[0] + got1.astype(F32)
    other = (parts[2] + got3.astype(F32)).astype(own_cast)
    return mine + swap(other, 2).astype(F32)


def crossed(v, bit):
    got = jnp.split(swap(v, bit), lax.axis_size("wsh"), axis=1)
    return jnp.concatenate([got[r ^ bit] for r in range(len(got))], axis=1)


def sum_all(v):
    v = v + crossed(v, 1)
    return v + crossed(v.astype(BF16), 2).astype(F32)


def carried(total, state, rate, reverse):
    count = lax.axis_size("seq")
    sign = -1 if reverse else 1
    total, state = shifted((total, state), sign)
    hop = 1
    while hop < count:
        got_total, got_state = shifted((total, state), sign * hop)
        state = state + jnp.exp2(rate[None] * total) * got_state
        total = total + got_total
        hop *= 2
    return state


def reduced(rows):
    return lax.psum_scatter(rows, "seq", scatter_dimension=0, tiled=True)


def local(
    hidden,
    teacher,
    cotangent,
    lengths,
    norm_gain,
    in_weight,
    conv_weight,
    conv_bias,
    x_weight,
    dt_weight,
    dt_bias,
    a_log,
    skip_gain,
    out_weight,
):
    me = lax.axis_index("wsh")
    place = lax.axis_index("seq")
    seqs = lax.axis_size("wsh")
    seq_count = lax.axis_size("seq")
    tokens, width = hidden.shape[1:]
    inner = out_weight.shape[0]
    depth = in_weight.shape[0]
    states = a_log.shape[0]
    rank = dt_weight.shape[0]
    taps = conv_weight.shape[0]
    rows = seqs * tokens

    def slots(pieces):
        return [lax.dynamic_index_in_dim(pieces, me ^ r, 0, False) for r in range(seqs)]

    all_lengths = lax.all_gather(lengths, "wsh", axis=0, tiled=True)
    gain = lax.all_gather(norm_gain, "wsh", axis=0, tiled=True).astype(F32)
    whole = place * 0 + seq_count * tokens
    count = jnp.sum(jnp.minimum(all_lengths, whole)).astype(F32)
    slot_lengths = jnp.stack(slots(all_lengths))
    positions = place * tokens + lax.iota(jnp.int32, tokens)
    valid = (positions[None, :] < slot_lengths[:, None]).astype(F32)
    halo_positions = place * tokens - HALO + lax.iota(jnp.int32, HALO + tokens)
    halo_valid = (halo_positions[None, :] < slot_lengths[:, None]).astype(F32)

    rows_in = hidden[0].astype(F32)
    scale = lax.rsqrt(jnp.mean(rows_in * rows_in, axis=1, keepdims=True) + NORM_EPS)
    normed_own = (rows_in * scale * gain).astype(BF16)
    before = shifted(normed_own[tokens - HALO :], 1)
    normed = jnp.stack(spread_out(jnp.concatenate([before, normed_own], axis=0)))
    normed_tokens = normed[:, HALO:].reshape(rows, width)

    split = in_weight.reshape(depth, 2, seqs, inner)
    mine = [lax.dynamic_index_in_dim(split, me ^ r, 2, False) for r in range(seqs)]
    got = [mine[0]] + [swap(mine[r], r) for r in range(1, seqs)]
    columns = jnp.stack([lax.dynamic_index_in_dim(jnp.stack(got), me ^ j, 0, False) for j in range(seqs)])
    x_columns = columns[:, :, 0].reshape(width, inner)
    z_columns = columns[:, :, 1].reshape(width, inner)

    x_both = product(normed.reshape(seqs * (HALO + tokens), width), x_columns, PLAIN)
    x_in = (x_both.reshape(seqs, HALO + tokens, inner) * halo_valid[:, :, None]).astype(BF16)
    padded = x_in[:, HALO - (taps - 1) :].astype(F32)
    conv_f = conv_weight.astype(F32)
    conv_out = conv_bias.astype(F32) + sum(
        conv_f[tap] * padded[:, tap : tap + tokens] for tap in range(taps)
    )
    conv_out = conv_out.reshape(rows, inner)
    act = silu_value(conv_out).astype(BF16)
    act_f = act.astype(F32)
    proj = sum_all(product(x_weight, act, COLS_LAST)).astype(BF16)
    dt_low = proj[:rank]
    bc = proj[rank:].astype(F32)
    step = jax.nn.softplus(product(dt_low, dt_weight, ROWS_FIRST) + dt_bias.astype(F32))
    log_rate = a_log.astype(F32)
    rate = -jnp.exp(log_rate) * LOG2E
    skip = skip_gain.astype(F32)[None]

    last, total = p1(step, act, bc, rate, seqs)
    z_part = product(normed_tokens, z_columns, PLAIN)
    carry = carried(total, last, rate, False)
    mixed, gated, starts = p2(step, act, z_part, bc, rate, skip, carry, seqs)
    out_parts = product(gated, out_weight, PLAIN).reshape(seqs, tokens, width)
    full = rows_in + sum_to_owner(out_parts)
    own_valid = valid[0][:, None]
    miss = full - teacher[0].astype(F32)
    loss = lax.psum(jnp.sum(own_valid * miss * miss), ("seq", "wsh")) / (width * count)
    g_full = cotangent[0].astype(F32) + 2.0 / (width * count) * own_valid * miss
    g_branch = jnp.stack(spread_out(g_full.astype(BF16))).reshape(rows, width)

    g_gated = product(g_branch, out_weight, COLS_LAST)
    g_mixed = g_gated * silu_value(z_part)
    g_z = (g_gated * mixed * silu_slope(z_part)).astype(BF16)
    out_grad = product(gated, g_branch, ROWS_FIRST)
    out_owned = lax.all_gather(reduced(out_grad.astype(BF16)), "seq", axis=0, tiled=True)
    skip_grad = jnp.sum(g_mixed * act_f, axis=0)

    first = b1(step, g_mixed, bc, rate, seqs)
    carry_back = carried(total, first, rate, True)
    g_pre, g_act_part, g_b, g_c, rate_sum, dt_bias_sum = b2(
        step, act, g_mixed, bc, rate, skip, starts, carry_back, seqs
    )
    g_dt_low = product(dt_weight, g_pre, COLS_LAST)
    g_proj = sum_all(
        jnp.concatenate([g_dt_low, g_b.reshape(rows, states).T, g_c.reshape(rows, states).T], axis=0)
    ).astype(BF16)
    g_act = g_act_part + product(g_proj, x_weight, ROWS_FIRST)
    g_conv = (g_act * silu_slope(conv_out)).reshape(seqs, tokens, inner)
    after = shifted(g_conv[:, : taps - 1].astype(BF16), -1).astype(F32)
    g_padded = jnp.concatenate([g_conv, after], axis=1)
    g_x_in = sum(conv_f[tap] * g_padded[:, taps - 1 - tap : taps - 1 - tap + tokens] for tap in range(taps))
    g_x = (g_x_in * valid[:, :, None]).astype(BF16).reshape(rows, inner)
    conv_grad = [jnp.sum(g_conv * padded[:, tap : tap + tokens], axis=(0, 1)) for tap in range(taps)]
    small = jnp.concatenate(
        [
            product(g_proj, act, PLAIN),
            product(dt_low, g_pre, PLAIN),
            rate_sum * (rate * LN2),
            jnp.stack(conv_grad + [jnp.sum(g_conv, axis=(0, 1)), jnp.sum(dt_bias_sum, axis=0), skip_grad]),
        ],
        axis=0,
    )
    small = lax.psum(small, "seq")
    cut = [0]
    for piece in (x_weight.shape[0], rank, states, taps, 1, 1, 1):
        cut.append(cut[-1] + piece)
    x_grad, dt_grad, log_rate_grad, conv_grad, conv_bias_grad, dt_bias_grad, skip_grad = [
        small[a:b] for a, b in zip(cut, cut[1:])
    ]

    def in_rows(grad):
        piece = depth // seq_count
        grad = grad.astype(BF16).reshape(seqs, seq_count, piece, inner)
        share = reduced(jnp.swapaxes(grad, 0, 1).reshape(width, inner))
        share = slots(share.reshape(seqs, piece, inner))
        got = jnp.stack([share[0]] + [swap(share[r], r) for r in range(1, seqs)])
        row = jnp.concatenate(slots(got), axis=1)
        return lax.all_gather(row, "seq", axis=0, tiled=True).astype(F32)

    in_z = in_rows(product(normed_tokens, g_z, ROWS_FIRST))
    in_x = in_rows(product(normed_tokens, g_x, ROWS_FIRST))
    in_grad = jnp.concatenate([in_x, in_z], axis=1)
    g_normed_parts = product(g_z, z_columns, COLS_LAST) + product(g_x, x_columns, COLS_LAST)
    g_normed = sum_to_owner(g_normed_parts.reshape(seqs, tokens, width))
    gain_grad = lax.psum(jnp.sum(g_normed * rows_in * scale, axis=0), ("seq", "wsh"))
    gain_grad = lax.dynamic_slice_in_dim(gain_grad, me * norm_gain.shape[0], norm_gain.shape[0])
    weighted = g_normed * gain
    g_rows = (
        g_full
        + scale * weighted
        - rows_in * scale * scale * scale * jnp.mean(weighted * rows_in, axis=1, keepdims=True)
    )
    return (
        full[None].astype(BF16),
        loss,
        g_rows[None].astype(BF16),
        gain_grad,
        in_grad,
        conv_grad,
        conv_bias_grad[0],
        x_grad,
        dt_grad,
        dt_bias_grad[0],
        log_rate_grad,
        skip_grad[0],
        out_owned.astype(F32),
    )


def solution(mesh):
    rows = P("wsh", "seq", None)
    first, second = P("wsh", None), P(None, "wsh")
    one = P("wsh")
    return jax.shard_map(
        local,
        mesh=mesh,
        in_specs=(
            rows, rows, rows, one, one, first, second, one, second, second, one, second, one, first,
        ),
        out_specs=(
            rows, P(), rows, one, first, second, one, second, second, one, second, one, first,
        ),
        check_vma=False,
    )
```

time: 4330 us -> 1080 us (0.25)
  waiting for transfers between devices: 1910 us -> 422 us
  local copies, waits for them, and re-layouts: 1050 us -> 86.5 us
  other arithmetic: 590 us -> 70.9 us
  matrix products: 394 us -> 82.2 us
  Pallas kernels: 0 us -> 173 us
  blocking collectives: 317 us -> 155 us
  starting transfers between devices: 5.75 us -> 61.6 us
    reduce_scatter x10 -> x3, waiting for transfers between devices: 1360 us -> 56.8 us  [reduced(): return lax.psum_scatter(rows, 'seq', scatter_dimension=0, tiled=True)]
    while x281 -> x0, local copies, waits for them, and re-layouts: 744 us -> none
    all_gather x9 -> x3, waiting for transfers between devices: 468 us -> 155 us  [the longest x2 141 us: in_rows(): return lax.all_gather(row, 'seq', axis=0, tiled=True).astype(F32)]
    dot_general x37 -> x15, matrix products: 394 us -> 82.2 us  [product(): return lax.dot_general(left, right, dims, preferred_element_type=F32)]
    reduce_sum x50 -> x4, other arithmetic: 323 us -> 13.8 us  [the longest x1 7.81 us: local(): jnp.sum(g_conv * padded[:, tap:tap + tokens], axis=(0, 1))]
    pallas_call x0 -> x4, Pallas kernels: none -> 173 us  [the longest x1 99.1 us: b2(): pl.pallas_call(partial(b2_kernel, eb=eb, n=n), grid=(seqs,), in_specs=[bl...]
    mul x97 -> x0, local copies, waits for them, and re-layouts: 154 us -> none  [the longest x8 35.3 us: block_states(): exponent = rate[None] * rise_k[:, None, :]]
    ppermute x2 -> x41, waiting for transfers between devices: 4.06 us -> 158 us  [the longest x25 89.1 us: swap(): lax.ppermute(a, 'wsh', [(i, i ^ bit) for i in range(lax.axis_size('wsh'))])]
  transfers between devices with their start and end apart: 23 -> 48, of which waited for: 13 -> 28; matrix products, arithmetic and copies ran while one was open for 44% -> 13% of each run, Pallas kernels for 0% -> 11%
where the time goes in v1:
time: 1080 us; the launch traced here: 1070 us
  waiting for transfers between devices  422 us (39%)
  Pallas kernels  173 us (16%)
  blocking collectives  155 us (14%)
  local copies, waits for them, and re-layouts  86.5 us (8%)
  matrix products  82.2 us (8%)
  other arithmetic  70.9 us (7%)
  starting transfers between devices  61.6 us (6%)
  between operations  19 us (2%)
    all_gather x2, waiting for transfers between devices, in_rows(): return lax.all_gather(row, 'seq', axis=0, tiled=True).astype(F32)  141 us
    pallas_call x1, Pallas kernels, b2(): pl.pallas_call(partial(b2_kernel, eb=eb, n=n), grid=(seqs,), in_specs=[bl...  99.1 us
    all_gather x1, blocking collectives, local(): gain = lax.all_gather(norm_gain, 'wsh', axis=0, tiled=True).astype(F32)  89.5 us
    ppermute x25, waiting for transfers between devices, swap(): lax.ppermute(a, 'wsh', [(i, i ^ bit) for i in range(lax.axis_size('wsh'))])  89.1 us
    dot_general x15, matrix products, product(): return lax.dot_general(left, right, dims, preferred_element_type=F32)  82.2 us
    ppermute x16, waiting for transfers between devices, shifted(): return jax.tree.map(lambda a: lax.ppermute(a, 'seq', route), v)  69.1 us
    reduce_scatter x3, waiting for transfers between devices, reduced(): return lax.psum_scatter(rows, 'seq', scatter_dimension=0, tiled=True)  56.8 us
    psum x1, waiting for transfers between devices, local(): small = lax.psum(small, 'seq')  51.5 us
  transfers between devices with their start and end apart: 48, of which 28 were waited for; matrix products, arithmetic and copies ran while one was open for 13% of the time, Pallas kernels for 11%

profile of v1, /device:TPU:0, one launch (start us, length us, event | category | flops | bytes accessed | tf_op | source)
XLA Modules:
  0.0 1070.1 jit_solution(15717322924675251288)
XLA Ops:
  7.3 14.5 %reshape.191 = bf16[512,2,4,1024]{3,2,1,0:T(4,128)(2,1)} reshape(bf16[512,8192]{1,0:T(8,128)(2,1)} %param.19) | data formatting | bytes 16777216 | tf_op jit(solution)/shard_map/reshape | solution.py:366
  21.8 27.4 %constant_dynamic-slice_fusion.9 = (bf16[512,2,1,1024]{3,2,1,0:T(2,128)(2,1)}, bf16[512,2,1,1024]{3,2,1,0:T(2,128)(2,1)S(1)}, bf16[512,2,1,1024]{3,2,1,0:T(2,128)(2,1)S(1)}, bf16[512,2,1,1024]{3,2,1,0:T(2,128)(2,1)S(1)}) fusion(bf16[512,2,4,1024]{3,2,1,0:T(4,128)(2,1)} %reshape.191, s32[]{:T(128)S(6)} %select_n.47, s32[]{:T(128)S(6)} %select_n.50, ...), kind=kLoop, calls=%fused_computation.145 | loop fusion | bytes 16777232 | tf_op jit(solution)/shard_map/jit(dynamic_index_in_dim)/dynamic_slice | solution.py:367
  60.0 89.5 %all-gather = bf16[4,1,512]{2,1,0:T(2,128)(2,1)S(1)} all-gather(bf16[1,1,512]{2,1,0:T(2,128)(2,1)S(1)} %reshape.212), channel_id=1, replica_groups=mesh['seq'=8,'wsh'=4] {'wsh'}, dimensions={0}, use_global_device_ids=true | all-gather | bytes 5120 | tf_op jit(solution)/shard_map/all_gather | solution.py:350
  160.7 22.8 %all-reduce = s32[4]{0:T(128)S(1)} all-reduce(s32[4]{0:T(128)S(1)} %dynamic-update-slice), channel_id=1, replica_groups=mesh['seq'=8,'wsh'=4] {'wsh'}, use_global_device_ids=true, to_apply=%add | all-reduce | flops 4 | bytes 32
  198.7 9.2 fusion
  217.0 7.6 collective-permute-done.8
  230.0 19.9 %shard_map.237 = (f32[4,16,1024]{2,1,0:T(8,128)}, f32[4,1,1024]{2,1,0:T(1,128)}) custom-call(f32[1024,1024]{1,0:T(8,128)} %compare_select_fusion.step_ref, bf16[1024,1024]{1,0:T(8,128)(2,1)} %copy-done.2, f32[32,1024]{1,0:T(8,128)} %slice_convert_fusion.1.bc_ref, f32[16,1024]{1,0:T(8,128)} %fusion.49.rate_ref), custom_call_target="tpu_custom_call" | custom-call | tf_op jit(solution)/shard_map/pallas_call | solution.py:81
  254.3 5.3 collective-permute-done.9
  288.0 6.1 fusion.68.z_ref
  294.9 34.3 %shard_map.238 = (f32[1024,1024]{1,0:T(8,128)}, bf16[1024,1024]{1,0:T(8,128)(2,1)}, f32[4,8,16,1024]{3,2,1,0:T(8,128)}) custom-call(f32[1024,1024]{1,0:T(8,128)} %compare_select_fusion.step_ref, bf16[1024,1024]{1,0:T(8,128)(2,1)} %copy-done.2, f32[1024,1024]{1,0:T(8,128)} %fusion.68.z_ref, f32[32,1024]{1,0:T(8,128)} %slice_convert_fusion.1.bc_ref, ...), custom_call_target="tpu_custom_call" | custom-call | tf_op jit(solution)/shard_map/pallas_call | solution.py:126
  329.2 6.1 fusion.66
  344.2 23.2 %collective-permute-done.18 = bf16[256,2048]{1,0:T(8,128)(2,1)} collective-permute-done((bf16[256,2048]{1,0:T(8,128)(2,1)}, bf16[256,2048]{1,0:T(8,128)(2,1)}, u32[]{:S(2)}, u32[]{:S(2)}) %collective-permute-start.18) | collective-permute-done | bytes 1048608 | tf_op jit(solution)/shard_map/ppermute | solution.py:268
  373.6 22.9 %collective-permute-done.20 = bf16[256,2048]{1,0:T(8,128)(2,1)S(1)} collective-permute-done((bf16[256,2048]{1,0:T(8,128)(2,1)S(1)}, bf16[256,2048]{1,0:T(8,128)(2,1)S(1)}, u32[]{:S(2)}, u32[]{:S(2)}) %collective-permute-start.20) | collective-permute-done | bytes 1048608 | tf_op jit(solution)/shard_map/ppermute | solution.py:268
  401.7 6.3 convolution_convert_fusion
  409.6 14.5 %multiply_reduce_fusion = (f32[1024]{0:T(1024)}, f32[1024,1024]{1,0:T(8,128)}, bf16[1024,1024]{1,0:T(8,128)(2,1)S(1)}) fusion(bf16[1024,1024]{1,0:T(8,128)(2,1)S(1)} %copy-done.3, f32[1024,1024]{1,0:T(8,128)} %fusion.68.z_ref, f32[1024,1024]{1,0:T(8,128)} %get-tuple-element.27, bf16[1024,2048]{1,0:T(8,128)(2,1)} %bitcast.210, bf16[1024,2048]{1,0:T(8,128)(2,1)} %param.27), kind=kOutput, calls=%fused_computation.45 | convolution fusion | flops 4310694912 | bytes 25169920 | tf_op jit(solution)/shard_map/dot_general | solution.py:25
  431.7 19.5 %shard_map.239 = f32[4,16,1024]{2,1,0:T(8,128)} custom-call(f32[1024,1024]{1,0:T(8,128)} %compare_select_fusion.step_ref, f32[1024,1024]{1,0:T(8,128)} %get-tuple-element.44.dy_ref, f32[32,1024]{1,0:T(8,128)} %slice_convert_fusion.1.bc_ref, f32[16,1024]{1,0:T(8,128)} %fusion.49.rate_ref), custom_call_target="tpu_custom_call" | custom-call | tf_op jit(solution)/shard_map/pallas_call | solution.py:153
  452.5 12.9 %collective-permute-done.22 = f32[4,16,1024]{2,1,0:T(8,128)S(1)} collective-permute-done((f32[4,16,1024]{2,1,0:T(8,128)}, f32[4,16,1024]{2,1,0:T(8,128)S(1)}, u32[]{:S(2)}, u32[]{:S(2)}) %collective-permute-start.22) | collective-permute-done | bytes 262176 | tf_op jit(solution)/shard_map/ppermute | solution.py:275
  468.0 10.3 collective-permute-done.23
  495.4 21.7 %collective-permute-done.28 = f32[4,16,1024]{2,1,0:T(8,128)S(1)} collective-permute-done((f32[4,16,1024]{2,1,0:T(8,128)S(1)}, f32[4,16,1024]{2,1,0:T(8,128)S(1)}, u32[]{:S(2)}, u32[]{:S(2)}) %collective-permute-start.28) | collective-permute-done | bytes 262176 | tf_op jit(solution)/shard_map/ppermute | solution.py:275
  517.8 99.1 %shard_map.240 = (bf16[1024,1024]{1,0:T(8,128)(2,1)}, f32[1024,1024]{1,0:T(8,128)}, f32[4,32,128]{2,1,0:T(8,128)}, f32[4,32,128]{2,1,0:T(8,128)}, f32[16,1024]{1,0:T(8,128)}, /*index=5*/f32[8,1024]{1,0:T(8,128)}) custom-call(f32[1024,1024]{1,0:T(8,128)} %compare_select_fusion.step_ref, bf16[1024,1024]{1,0:T(8,128)(2,1)} %copy-done.2, ...), custom_call_target="tpu_custom_call" | custom-call | tf_op jit(solution)/shard_map/pallas_call | solution.py:253
  625.7 8.3 collective-permute-done.30
  660.9 7.8 multiply_reduce_fusion.1
  684.0 56.8 %reduce-scatter.4.cloned.1.call-done = bf16[256,1024]{1,0:T(8,128)(2,1)} async-done(((bf16[2048,1024]{1,0:T(8,128)(2,1)}), bf16[256,1024]{1,0:T(8,128)(2,1)}) %reduce-scatter.4.cloned.1.call-update) | async-done | bytes 524304 | tf_op jit(solution)/shard_map/reduce_scatter | solution.py:315
  751.6 9.1 fusion.69
  760.7 7.1 fusion.67
  775.6 51.5 %all-reduce.4.cloned.1.call-done = f32[311,1024]{1,0:T(8,128)} async-done(((f32[311,1024]{1,0:T(8,128)}), f32[311,1024]{1,0:T(8,128)}) %all-reduce.4.cloned.1.call-update) | async-done | bytes 1273872 | tf_op jit(solution)/shard_map/psum | solution.py:435
  844.1 43.2 %all-reduce.1 = (f32[]{:T(128)}, f32[2048]{0:T(1024)S(1)}) all-reduce(f32[]{:T(128)} %get-tuple-element.65, f32[2048]{0:T(1024)S(1)} %get-tuple-element.35), channel_id=1, replica_groups=mesh['seq'=8,'wsh'=4] {'seq','wsh'}, use_global_device_ids=true, to_apply=%region_2.3 | all-reduce | flops 2049 | bytes 16392 | tf_op jit(solution)/shard_map/psum | solution.py:399
  888.6 13.7 %all-gather.9.cloned.1.call-done = bf16[1024,2048]{1,0:T(8,128)(2,1)} async-done(((bf16[128,2048]{1,0:T(8,128)(2,1)}), bf16[1024,2048]{1,0:T(8,128)(2,1)}) %all-gather.9.cloned.1.call-update) | async-done | bytes 4194320 | tf_op jit(solution)/shard_map/all_gather | solution.py:407
  902.3 6.7 convert_element_type.199
  909.0 67.0 %all-gather.7.cloned.1.call-done = bf16[512,4096]{1,0:T(8,128)(2,1)} async-done(((bf16[64,4096]{1,0:T(8,128)(2,1)}), bf16[512,4096]{1,0:T(8,128)(2,1)}) %all-gather.7.cloned.1.call-update) | async-done | bytes 4194320 | tf_op jit(solution)/shard_map/all_gather | solution.py:450
  976.0 73.8 %all-gather.5.cloned.1.call-done = bf16[512,4096]{1,0:T(8,128)(2,1)} async-done(((bf16[64,4096]{1,0:T(8,128)(2,1)}), bf16[512,4096]{1,0:T(8,128)(2,1)}) %all-gather.5.cloned.1.call-update) | async-done | bytes 4194320 | tf_op jit(solution)/shard_map/all_gather | solution.py:450
  1049.8 11.8 %maximum_convert_fusion = f32[512,8192]{1,0:T(8,128)} fusion(bf16[512,4096]{1,0:T(8,128)(2,1)} %all-gather.7.cloned.1.call-done, bf16[512,4096]{1,0:T(8,128)(2,1)} %all-gather.5.cloned.1.call-done), kind=kLoop, calls=%fused_computation.3 | loop fusion | flops 16777216 | bytes 25165824 | tf_op jit(solution)/shard_map/concatenate | solution.py:454
  (316 shorter events, 221.4 us)
Async XLA Ops:
  7.2 665.3 %reduce-scatter.8.cloned.1.call-start = ((), (), s32[]{:S(2)}) async-start(), calls=%async_computation.8 | async-start | bytes 4718592 | tf_op jit(solution)/shard_map/reduce_scatter | solution.py:315
  51.7 139.7 %collective-permute-start.4 = (bf16[512,2,1024]{2,0,1:T(8,128)(2,1)}, bf16[512,2,1024]{2,0,1:T(8,128)(2,1)}, u32[]{:S(2)}, u32[]{:S(2)}) collective-permute-start(bf16[512,2,1024]{2,0,1:T(8,128)(2,1)} %bitcast.194), channel_id=1, source_target_pairs={{0,1},{1,0},{2,3},{3,2},{4,5},{5,4},{6,7},{7,6},{8,9},{9,8},{10,11... | collective-permute-start | bytes 6291464 | tf_op jit(solution)/shard_map/ppermute | solution.py:268
  54.6 136.8 %collective-permute-start.5 = (bf16[512,2,1024]{2,0,1:T(8,128)(2,1)}, bf16[512,2,1024]{2,0,1:T(8,128)(2,1)}, u32[]{:S(2)}, u32[]{:S(2)}) collective-permute-start(bf16[512,2,1024]{2,0,1:T(8,128)(2,1)} %bitcast.193), channel_id=1, source_target_pairs={{0,2},{1,3},{2,0},{3,1},{4,6},{5,7},{6,4},{7,5},{8,10},{9,11},{10,... | collective-permute-start | bytes 6291464 | tf_op jit(solution)/shard_map/ppermute | solution.py:268
  59.6 131.8 %collective-permute-start.6 = (bf16[512,2,1024]{2,0,1:T(8,128)(2,1)}, bf16[512,2,1024]{2,0,1:T(8,128)(2,1)}, u32[]{:S(2)}, u32[]{:S(2)}) collective-permute-start(bf16[512,2,1024]{2,0,1:T(8,128)(2,1)} %bitcast.192), channel_id=1, source_target_pairs={{0,3},{1,2},{2,1},{3,0},{4,7},{5,6},{6,5},{7,4},{8,11},{9,10},{10,... | collective-permute-start | bytes 6291464 | tf_op jit(solution)/shard_map/ppermute | solution.py:268
  157.2 33.7 %collective-permute-start.2 = (bf16[272,2048]{1,0:T(8,128)(2,1)}, bf16[272,2048]{1,0:T(8,128)(2,1)}, u32[]{:S(2)}, u32[]{:S(2)}) collective-permute-start(bf16[272,2048]{1,0:T(8,128)(2,1)} %get-tuple-element.71), channel_id=1, source_target_pairs={{0,2},{1,3},{2,0},{3,1},{4,6},{5,7},{6,4},{7,5},{8,10},{9,11},{10,... | collective-permute-start | bytes 3342344 | tf_op jit(solution)/shard_map/ppermute | solution.py:268
  190.8 7.8 collective-permute-start.1
  190.9 7.7 collective-permute-start.3
  214.8 9.8 collective-permute-start.8
  249.9 9.7 collective-permute-start.9
  259.6 15.3 %collective-permute-start.11 = (f32[4,16,1024]{2,1,0:T(8,128)S(1)}, f32[4,16,1024]{2,1,0:T(8,128)S(1)}, u32[]{:S(2)}, u32[]{:S(2)}) collective-permute-start(f32[4,16,1024]{2,1,0:T(8,128)S(1)} %collective-permute-done.9), channel_id=1, source_target_pairs={{0,4},{4,8},{8,12},{12,16},{16,20},{20,24},{24,28},{1,5},{5,9},{9,... | collective-permute-start | bytes 786440 | tf_op jit(solution)/shard_map/ppermute | solution.py:275
  270.7 9.9 collective-permute-start.12
  275.0 9.1 collective-permute-start.13
  280.7 13.4 %collective-permute-start.14 = (f32[4,1,1024]{2,1,0:T(1,128)S(1)}, f32[4,1,1024]{2,1,0:T(1,128)S(1)}, u32[]{:S(2)}, u32[]{:S(2)}) collective-permute-start(f32[4,1,1024]{2,1,0:T(1,128)S(1)} %add.234), channel_id=1, source_target_pairs={{0,8},{4,12},{8,16},{12,20},{16,24},{20,28},{1,9},{5,13},{9,17},{1... | collective-permute-start | bytes 49160 | tf_op jit(solution)/shard_map/ppermute | solution.py:275
  284.2 9.9 collective-permute-start.15
  341.9 25.5 %collective-permute-start.18 = (bf16[256,2048]{1,0:T(8,128)(2,1)}, bf16[256,2048]{1,0:T(8,128)(2,1)}, u32[]{:S(2)}, u32[]{:S(2)}) collective-permute-start(bf16[256,2048]{1,0:T(8,128)(2,1)} %fusion.41), channel_id=1, source_target_pairs={{0,2},{1,3},{2,0},{3,1},{4,6},{5,7},{6,4},{7,5},{8,10},{9,11},{10,... | collective-permute-start | bytes 3145736 | tf_op jit(solution)/shard_map/ppermute | solution.py:268
  372.1 24.4 %collective-permute-start.20 = (bf16[256,2048]{1,0:T(8,128)(2,1)S(1)}, bf16[256,2048]{1,0:T(8,128)(2,1)S(1)}, u32[]{:S(2)}, u32[]{:S(2)}) collective-permute-start(bf16[256,2048]{1,0:T(8,128)(2,1)S(1)} %get-tuple-element.47), channel_id=1, source_target_pairs={{0,2},{1,3},{2,0},{3,1},{4,6},{5,7},{6,4},{7,5},{8,10},{9,11},{10,... | collective-permute-start | bytes 3145736 | tf_op jit(solution)/shard_map/ppermute | solution.py:268
  373.6 22.9 %collective-permute-start.19 = (bf16[256,2048]{1,0:T(8,128)(2,1)S(1)}, bf16[256,2048]{1,0:T(8,128)(2,1)S(1)}, u32[]{:S(2)}, u32[]{:S(2)}) collective-permute-start(bf16[256,2048]{1,0:T(8,128)(2,1)S(1)} %get-tuple-element.47), channel_id=1, source_target_pairs={{0,1},{1,0},{2,3},{3,2},{4,5},{5,4},{6,7},{7,6},{8,9},{9,8},{10,11... | collective-permute-start | bytes 3145736 | tf_op jit(solution)/shard_map/ppermute | solution.py:268
  408.0 265.1 %reduce-scatter.6.cloned.1.call-start = ((), (), s32[]{:S(2)}) async-start(), calls=%async_computation.5 | async-start | bytes 4718592 | tf_op jit(solution)/shard_map/reduce_scatter | solution.py:315
  431.6 309.1 %reduce-scatter.4.cloned.1.call-start = ((), (), s32[]{:S(2)}) async-start(), calls=%async_computation.3 | async-start | bytes 4718592 | tf_op jit(solution)/shard_map/reduce_scatter | solution.py:315
  451.2 14.1 %collective-permute-start.22 = (f32[4,16,1024]{2,1,0:T(8,128)}, f32[4,16,1024]{2,1,0:T(8,128)S(1)}, u32[]{:S(2)}, u32[]{:S(2)}) collective-permute-start(f32[4,16,1024]{2,1,0:T(8,128)} %shard_map.239), channel_id=1, source_target_pairs={{4,0},{8,4},{12,8},{16,12},{20,16},{24,20},{28,24},{5,1},{9,5},{13... | collective-permute-start | bytes 786440 | tf_op jit(solution)/shard_map/ppermute | solution.py:275
  465.4 12.9 %collective-permute-start.24 = (f32[4,16,1024]{2,1,0:T(8,128)S(1)}, f32[4,16,1024]{2,1,0:T(8,128)S(1)}, u32[]{:S(2)}, u32[]{:S(2)}) collective-permute-start(f32[4,16,1024]{2,1,0:T(8,128)S(1)} %collective-permute-done.22), channel_id=1, source_target_pairs={{4,0},{8,4},{12,8},{16,12},{20,16},{24,20},{28,24},{5,1},{9,5},{13... | collective-permute-start | bytes 786440 | tf_op jit(solution)/shard_map/ppermute | solution.py:275
  466.7 11.6 %collective-permute-start.23 = (f32[4,1,1024]{2,1,0:T(1,128)S(1)}, f32[4,1,1024]{2,1,0:T(1,128)S(1)}, u32[]{:S(2)}, u32[]{:S(2)}) collective-permute-start(f32[4,1,1024]{2,1,0:T(1,128)S(1)} %copy-done.56), channel_id=1, source_target_pairs={{4,0},{8,4},{12,8},{16,12},{20,16},{24,20},{28,24},{5,1},{9,5},{13... | collective-permute-start | bytes 49160 | tf_op jit(solution)/shard_map/ppermute | solution.py:275
  478.4 9.8 collective-permute-start.26
  488.3 28.8 %collective-permute-start.28 = (f32[4,16,1024]{2,1,0:T(8,128)S(1)}, f32[4,16,1024]{2,1,0:T(8,128)S(1)}, u32[]{:S(2)}, u32[]{:S(2)}) collective-permute-start(f32[4,16,1024]{2,1,0:T(8,128)S(1)} %multiply_add_fusion.1), channel_id=1, source_target_pairs={{16,0},{20,4},{24,8},{28,12},{17,1},{21,5},{25,9},{29,13},{18,2},{... | collective-permute-start | bytes 786440 | tf_op jit(solution)/shard_map/ppermute | solution.py:275
  624.2 9.8 collective-permute-start.30
  653.7 173.4 %all-reduce.4.cloned.1.call-start = ((), (), s32[]{:S(2)}) async-start(), calls=%async_computation.7 | async-start | bytes 2555904 | tf_op jit(solution)/shard_map/psum | solution.py:435
  672.5 229.8 %all-gather.9.cloned.1.call-start = ((), (), s32[]{:S(2)}) async-start(), calls=%async_computation.9 | async-start | bytes 4718592 | tf_op jit(solution)/shard_map/all_gather | solution.py:407
  673.1 302.9 %all-gather.7.cloned.1.call-start = ((), (), s32[]{:S(2)}) async-start(), calls=%async_computation.6 | async-start | bytes 4718592 | tf_op jit(solution)/shard_map/all_gather | solution.py:450
  674.4 8.5 collective-permute-start.39
  683.9 365.9 %all-gather.5.cloned.1.call-start = ((), (), s32[]{:S(2)}) async-start(), calls=%async_computation.4 | async-start | bytes 4718592 | tf_op jit(solution)/shard_map/all_gather | solution.py:450
  769.1 66.3 %collective-permute-start.32 = (bf16[256,2048]{1,0:T(8,128)(2,1)}, bf16[256,2048]{1,0:T(8,128)(2,1)}, u32[]{:S(2)}, u32[]{:S(2)}) collective-permute-start(bf16[256,2048]{1,0:T(8,128)(2,1)} %get-tuple-element.60), channel_id=1, source_target_pairs={{0,1},{1,0},{2,3},{3,2},{4,5},{5,4},{6,7},{7,6},{8,9},{9,8},{10,11... | collective-permute-start | bytes 3145736 | tf_op jit(solution)/shard_map/ppermute | solution.py:268
  774.2 61.2 %collective-permute-start.34 = (bf16[256,2048]{1,0:T(8,128)(2,1)}, bf16[256,2048]{1,0:T(8,128)(2,1)}, u32[]{:S(2)}, u32[]{:S(2)}) collective-permute-start(bf16[256,2048]{1,0:T(8,128)(2,1)} %fusion.39), channel_id=1, source_target_pairs={{0,2},{1,3},{2,0},{3,1},{4,6},{5,7},{6,4},{7,5},{8,10},{9,11},{10,... | collective-permute-start | bytes 3145736 | tf_op jit(solution)/shard_map/ppermute | solution.py:268
  (76 other events, 1737.7 us)
Sparse Core Ops, SparseCore 0:
  408.2 111.3 reduce-scatter.7
  523.6 86.9 reduce-scatter.5
  653.8 86.8 reduce-scatter.3
  745.1 81.8 all-reduce.3
  829.0 73.2 all-gather.8
  904.3 71.6 all-gather.6
  978.1 71.6 all-gather.4

commit v2 on v1

v2 whole, which is shorter than its diff:
```python
from functools import partial

import jax
import jax.numpy as jnp
from jax import lax
from jax.experimental import pallas as pl
from jax.experimental.pallas import tpu as pltpu
from jax.sharding import PartitionSpec as P

F32 = jnp.float32
BF16 = jnp.bfloat16
NORM_EPS = 1e-05
LOG2E = 1.4426950408889634
LN2 = 0.6931471805599453
GROUP = 8
CHUNK = 32
HALO = 16
VMEM_LIMIT = 56 * 1024 * 1024
ROWS_FIRST = (((0,), (0,)), ((), ()))
COLS_LAST = (((1,), (1,)), ((), ()))
PLAIN = (((1,), (0,)), ((), ()))


def product(left, right, dims):
    return lax.dot_general(left, right, dims, preferred_element_type=F32)


def silu_value(v):
    return v * jax.nn.sigmoid(v)


def silu_slope(v):
    sigma = jax.nn.sigmoid(v)
    return sigma * (1.0 + v * (1.0 - sigma))


def kernel_params():
    return pltpu.CompilerParams(vmem_limit_bytes=VMEM_LIMIT)


def cost(microseconds):
    return pl.CostEstimate(flops=int(microseconds * 1e9), bytes_accessed=0, transcendentals=0)


def widen(bc_ref, row, size, rep_ref):
    ones = jnp.ones((128, 128), BF16)
    lane = lax.broadcasted_iota(jnp.int32, (size, 128), 1)
    part = 32

    def block(i, _):
        t0 = pl.multiple_of(i * 128, 128)
        x = bc_ref[row : row + size, pl.ds(t0, 128)]
        for j in range(0, 128, part):
            picked = jnp.concatenate([jnp.where(lane == k, x, 0.0) for k in range(j, j + part)], axis=0)
            wide = jnp.dot(picked.astype(BF16), ones, preferred_element_type=F32)
            rep_ref[pl.ds(t0 + j, part)] = wide.reshape(part, size, 128)
        return 0

    lax.fori_loop(0, bc_ref.shape[1] // 128, block, 0)


def tiled(x, width):
    return jnp.concatenate([x]*(width//128), axis=1)

def put_fold(fold_ref,k,v):
    for i in range(v.shape[1]//128):
        fold_ref[i,8*k:8*k+8,:]=v[:,128*i:128*i+128]

def get_fold(fold_ref):
    def tree(x):
        while len(x)>1: x=[a+b for a,b in zip(x[::2],x[1::2])]
        return x[0]
    return jnp.concatenate([tree([fold_ref[i,pl.ds(r,GROUP,stride=8),:] for r in range(8)]) for i in range(fold_ref.shape[0])],axis=1)

def p1_kernel(step_ref, act_ref, bc_ref, rate_ref, last_ref, total_ref, dx_ref, brep_ref, *, eb, n):
    widen(bc_ref,0,n,brep_ref)
    step=step_ref[...]
    dx_ref[...]=step*act_ref[...].astype(F32)
    total_ref[0]=jnp.sum(step,axis=0,keepdims=True)
    tokens,width=step_ref.shape
    for e in range(0,width,eb):
        sl=slice(e,e+eb)
        rate=rate_ref[:,sl]
        def group(g,h):
            base=pl.multiple_of(g*GROUP,GROUP)
            s8=step_ref[pl.ds(base,GROUP),sl]
            x8=dx_ref[pl.ds(base,GROUP),sl]
            for k in range(GROUP):
                d=jnp.exp2(rate*s8[k:k+1])
                h=d*h+tiled(brep_ref[base+k],eb)*x8[k:k+1]
            return h
        last_ref[0,:,sl]=lax.fori_loop(0,tokens//GROUP,group,jnp.zeros((n,eb),F32))

def p1(first, step, act, bc, rate, tokens, eb=512):
    width = step.shape[1]
    n = rate.shape[0]
    blk = pl.BlockSpec((tokens, width), lambda s: (first + s, 0))
    return pl.pallas_call(
        partial(p1_kernel, eb=eb, n=n),
        grid=(2,),
        in_specs=[
            blk,
            blk,
            pl.BlockSpec((bc.shape[0], tokens), lambda s: (0, first + s)),
            pl.BlockSpec((n, width), lambda s: (0, 0)),
        ],
        out_specs=[
            pl.BlockSpec((1, n, width), lambda s: (s, 0, 0)),
            pl.BlockSpec((1, 1, width), lambda s: (s, 0, 0)),
        ],
        out_shape=[jax.ShapeDtypeStruct((2, n, width), F32), jax.ShapeDtypeStruct((2, 1, width), F32)],
        scratch_shapes=[pltpu.VMEM((tokens, width), F32), pltpu.VMEM((tokens, n, 128), F32)],
        cost_estimate=cost(9),
        compiler_params=kernel_params(),
    )(step, act, bc, rate)


def p2_kernel(step_ref, act_ref, z_ref, bc_ref, rate_ref, skip_ref, carry_ref, mixed_ref, gated_ref, starts_ref, dx_ref, fold_ref, brep_ref, crep_ref, *, eb, n):
    widen(bc_ref,0,n,brep_ref)
    widen(bc_ref,n,n,crep_ref)
    dx_ref[...]=step_ref[...]*act_ref[...].astype(F32)
    tokens,width=step_ref.shape
    for e in range(0,width,eb):
        sl=slice(e,e+eb)
        rate=rate_ref[:,sl]
        def chunk(c,h):
            starts_ref[0,c,:,sl]=h
            def group(j,h):
                g=c*(CHUNK//GROUP)+j
                base=pl.multiple_of(g*GROUP,GROUP)
                s8=step_ref[pl.ds(base,GROUP),sl]
                x8=dx_ref[pl.ds(base,GROUP),sl]
                for k in range(GROUP):
                    d=jnp.exp2(rate*s8[k:k+1])
                    h=d*h+tiled(brep_ref[base+k],eb)*x8[k:k+1]
                    p=tiled(crep_ref[base+k],eb)*h
                    put_fold(fold_ref,k,sum(p[8*i:8*i+8] for i in range(n//8)))
                mixed_ref[pl.ds(base,GROUP),sl]=get_fold(fold_ref)
                return h
            return lax.fori_loop(0,CHUNK//GROUP,group,h)
        lax.fori_loop(0,tokens//CHUNK,chunk,carry_ref[0,:,sl])
    def gate(i,_):
        rows=pl.ds(pl.multiple_of(i*16,16),16)
        m=mixed_ref[rows,:]+skip_ref[...]*act_ref[rows,:].astype(F32)
        mixed_ref[rows,:]=m
        z=z_ref[rows,:]
        gated_ref[rows,:]=(m*(z*jax.nn.sigmoid(z))).astype(BF16)
        return 0
    lax.fori_loop(0,tokens//16,gate,0)

def p2(first, step, act, z, bc, rate, skip, carry, tokens, eb=512):
    width = step.shape[1]
    n = rate.shape[0]
    nch = tokens // CHUNK
    blk = pl.BlockSpec((tokens, width), lambda s: (first + s, 0))
    out = pl.BlockSpec((tokens, width), lambda s: (s, 0))
    rep = pltpu.VMEM((tokens, n, 128), F32)
    return pl.pallas_call(
        partial(p2_kernel, eb=eb, n=n),
        grid=(2,),
        in_specs=[
            blk,
            blk,
            blk,
            pl.BlockSpec((bc.shape[0], tokens), lambda s: (0, first + s)),
            pl.BlockSpec((n, width), lambda s: (0, 0)),
            pl.BlockSpec((1, width), lambda s: (0, 0)),
            pl.BlockSpec((1, n, width), lambda s: (s, 0, 0)),
        ],
        out_specs=[out, out, pl.BlockSpec((1, nch, n, width), lambda s: (s, 0, 0, 0))],
        out_shape=[
            jax.ShapeDtypeStruct((2 * tokens, width), F32),
            jax.ShapeDtypeStruct((2 * tokens, width), BF16),
            jax.ShapeDtypeStruct((2, nch, n, width), F32),
        ],
        scratch_shapes=[pltpu.VMEM((tokens, width), F32), pltpu.VMEM((eb // 128, 64, 128), F32), rep, rep],
        cost_estimate=cost(16),
        compiler_params=kernel_params(),
    )(step, act, z, bc, rate, skip, carry)


def b1_kernel(step_ref, dy_ref, bc_ref, rate_ref, first_ref, crep_ref, *, eb, n):
    widen(bc_ref,n,n,crep_ref)
    tokens,width=step_ref.shape
    for e in range(0,width,eb):
        sl=slice(e,e+eb)
        rate=rate_ref[:,sl]
        def group(j,h):
            g=tokens//GROUP-1-j
            base=pl.multiple_of(g*GROUP,GROUP)
            s8=step_ref[pl.ds(base,GROUP),sl]
            y8=dy_ref[pl.ds(base,GROUP),sl]
            for k in reversed(range(GROUP)):
                h=jnp.exp2(rate*s8[k:k+1])*(h+tiled(crep_ref[base+k],eb)*y8[k:k+1])
            return h
        first_ref[0,:,sl]=lax.fori_loop(0,tokens//GROUP,group,jnp.zeros((n,eb),F32))

def b1(first, step, dy, bc, rate, tokens, eb=512):
    width = step.shape[1]
    n = rate.shape[0]
    return pl.pallas_call(
        partial(b1_kernel, eb=eb, n=n),
        grid=(2,),
        in_specs=[
            pl.BlockSpec((tokens, width), lambda s: (first + s, 0)),
            pl.BlockSpec((tokens, width), lambda s: (s, 0)),
            pl.BlockSpec((bc.shape[0], tokens), lambda s: (0, first + s)),
            pl.BlockSpec((n, width), lambda s: (0, 0)),
        ],
        out_specs=pl.BlockSpec((1, n, width), lambda s: (s, 0, 0)),
        out_shape=jax.ShapeDtypeStruct((2, n, width), F32),
        scratch_shapes=[pltpu.VMEM((tokens, n, 128), F32)],
        cost_estimate=cost(9),
        compiler_params=kernel_params(),
    )(step, dy, bc, rate)


def one_less_exp(s):
    return jnp.where(s<0.01, s*(1.0-s*(0.5-s*(1.0/6.0))), 1.0-jnp.exp(-s))

def b2_kernel(step_ref, act_ref, dy_ref, bc_ref, rate_ref, skip_ref, starts_ref, carry_ref, *refs, eb, n):
    (gpre_ref, gact_ref, gb_ref, gc_ref, alog_ref, dtb_ref, dx_ref, prev_ref, dec_ref, folda_ref, folds_ref,
     pb_ref, pc_ref, g_ref, brep_ref, crep_ref) = refs[-16:]
    widen(bc_ref,0,n,brep_ref)
    widen(bc_ref,n,n,crep_ref)
    tokens,width=step_ref.shape
    nch=tokens//CHUNK; per=CHUNK//GROUP
    dx_ref[...]=step_ref[...]*act_ref[...].astype(F32)
    g_ref[...]=carry_ref[0]
    alog_ref[...]=jnp.zeros_like(alog_ref)
    ones=jnp.ones((8,128),F32)
    def chunk(cc,_):
        c=nch-1-cc
        for e in range(0,width,eb):
            sl=slice(e,e+eb)
            rate=rate_ref[:,sl]
            def redo(j,h):
                g=c*per+j
                base=pl.multiple_of(g*GROUP,GROUP)
                s8=step_ref[pl.ds(base,GROUP),sl]
                x8=dx_ref[pl.ds(base,GROUP),sl]
                for k in range(GROUP):
                    d=jnp.exp2(rate*s8[k:k+1])
                    prev_ref[j*GROUP+k]=h
                    dec_ref[j*GROUP+k]=d
                    h=d*h+tiled(brep_ref[base+k],eb)*x8[k:k+1]
                return h
            last=lax.fori_loop(0,per,redo,starts_ref[0,c,:,sl])
            def back(jj,carry):
                h,alog,after=carry
                j=per-1-jj
                g=c*per+j
                base=pl.multiple_of(g*GROUP,GROUP)
                s8=step_ref[pl.ds(base,GROUP),sl]
                x8=dx_ref[pl.ds(base,GROUP),sl]
                y8=dy_ref[pl.ds(base,GROUP),sl]
                for k in reversed(range(GROUP)):
                    s=s8[k:k+1]
                    g_state=tiled(crep_ref[base+k],eb)*y8[k:k+1]+h
                    prev=prev_ref[j*GROUP+k]
                    pc=after*y8[k:k+1]
                    pb=g_state*x8[k:k+1]
                    al=g_state*tiled(brep_ref[base+k],eb)
                    h=g_state*dec_ref[j*GROUP+k]
                    q=h*prev
                    alog=alog+q*s
                    qs=q*rate
                    pcs=sum(pc[:,i:i+128] for i in range(0,eb,128))
                    pbs=sum(pb[:,i:i+128] for i in range(0,eb,128))
                    rows=pl.ds(pl.multiple_of((j*GROUP+k)*n,n),n)
                    if e==0:
                        pc_ref[rows,:]=pcs; pb_ref[rows,:]=pbs
                    else:
                        pc_ref[rows,:]+=pcs; pb_ref[rows,:]+=pbs
                    put_fold(folda_ref,k,sum(al[8*i:8*i+8] for i in range(n//8)))
                    put_fold(folds_ref,k,sum(qs[8*i:8*i+8] for i in range(n//8)))
                    after=prev
                gact_ref[pl.ds(base,GROUP),sl]=get_fold(folda_ref)
                dx_ref[pl.ds(base,GROUP),sl]=get_fold(folds_ref)
                return h,alog,after
            h,alog,_u=lax.fori_loop(0,per,back,(g_ref[:,sl],jnp.zeros((n,eb),F32),last))
            g_ref[:,sl]=h
            alog_ref[0,:,sl]+=alog
        for j in range(per):
            part=pb_ref[j*128:(j+1)*128,:]
            gb_ref[0,pl.ds(c*per+j,1),:]=lax.dot_general(ones,part,(((1,),(1,)),((),())),precision=lax.Precision.HIGHEST,preferred_element_type=F32)[0:1]
            part=pc_ref[j*128:(j+1)*128,:]
            gc_ref[0,pl.ds(c*per+j,1),:]=lax.dot_general(ones,part,(((1,),(1,)),((),())),precision=lax.Precision.HIGHEST,preferred_element_type=F32)[0:1]
        return 0
    lax.fori_loop(0,nch,chunk,0)
    def finish(i,acc):
        rows=pl.ds(pl.multiple_of(i*16,16),16)
        s=step_ref[rows,:]; along=gact_ref[rows,:]
        a=act_ref[rows,:].astype(F32)
        garg=(dx_ref[rows,:]*LN2+a*along)*one_less_exp(s)
        gpre_ref[rows,:]=garg.astype(BF16)
        dy=dy_ref[rows,:]
        gact_ref[rows,:]=dy*skip_ref[...]+s*along
        return acc[0]+jnp.sum(garg.reshape(2,8,width),axis=0), acc[1]+jnp.sum((dy*a).reshape(2,8,width),axis=0)
    zero=jnp.zeros((8,width),F32)
    acc=lax.fori_loop(0,tokens//16,finish,(zero,zero))
    dtb_ref[0,0]=acc[0]
    dtb_ref[0,1]=acc[1]

def b2(first, count, filled, step, act, dy, bc, rate, skip, starts, carry, tokens, eb=512):
    base = first % 2
    rows, width = step.shape
    n = rate.shape[0]
    nch = tokens // CHUNK
    blk = pl.BlockSpec((tokens, width), lambda i: (first + i, 0))
    full = lambda shape: pl.BlockSpec(shape, lambda i: (0,) * len(shape))
    own = lambda shape: pl.BlockSpec((1, *shape[1:]), lambda i: (i,) + (0,) * (len(shape) - 1))
    red = (count, tokens // GROUP, 128)
    rep = pltpu.VMEM((tokens, n, 128), F32)
    held = pltpu.VMEM((CHUNK, n, eb), F32)
    fold = pltpu.VMEM((eb // 128, 64, 128), F32)
    part = pltpu.VMEM((CHUNK * n, 128), F32)
    extra = () if filled is None else tuple(filled)
    return pl.pallas_call(
        partial(b2_kernel, eb=eb, n=n),
        grid=(count,),
        in_specs=[
            blk,
            blk,
            pl.BlockSpec((tokens, width), lambda i: (base + i, 0)),
            pl.BlockSpec((bc.shape[0], tokens), lambda i: (0, first + i)),
            full((n, width)),
            full((1, width)),
            pl.BlockSpec((1, nch, n, width), lambda i: (base + i, 0, 0, 0)),
            pl.BlockSpec((1, n, width), lambda i: (base + i, 0, 0)),
        ]
        + [pl.BlockSpec(memory_space=pl.ANY)] * len(extra),
        out_specs=[blk, blk, own(red), own(red), own((count, n, width)), own((count, 2, 8, width))],
        out_shape=[
            jax.ShapeDtypeStruct((rows, width), BF16),
            jax.ShapeDtypeStruct((rows, width), F32),
            jax.ShapeDtypeStruct(red, F32),
            jax.ShapeDtypeStruct(red, F32),
            jax.ShapeDtypeStruct((count, n, width), F32),
            jax.ShapeDtypeStruct((count, 2, 8, width), F32),
        ],
        scratch_shapes=[
            pltpu.VMEM((tokens, width), F32),
            held,
            held,
            fold,
            fold,
            part,
            part,
            pltpu.VMEM((n, width), F32),
            rep,
            rep,
        ],
        input_output_aliases={8: 0, 9: 1} if extra else {},
        cost_estimate=cost(25 * count),
        compiler_params=kernel_params(),
    )(step, act, dy, bc, rate, skip, starts, carry, *extra)


def settle_kernel(at_ref, *refs, steps, base, blocks, cols, extra):
    out_ref = refs[-2] if extra else refs[-1]
    rows = out_ref.shape[0]
    i = base + pl.program_id(0)
    for d in range(2):
        for k in range(steps):
            ref = refs[d * steps + k]
            wide = ref.shape[1]

            @pl.when(at_ref[1 + d * steps + i] == k)
            def _():
                for r in range(blocks):
                    start = d * wide
                    if blocks > 1:
                        start = pl.multiple_of((at_ref[0] ^ r) * cols + start, 128)
                    out_ref[:, pl.ds(start, wide)] = ref[r * rows : (r + 1) * rows, :].astype(F32)
                if extra:
                    refs[-1][:, d * wide : (d + 1) * wide] = ref[blocks * rows :, :].astype(F32)


def settle(at, both, shape, blocks, cols, half=0, filled=None, extra=0, part=None):
    steps = len(both[0])
    rows, wide = both[0][0].shape
    piece = (rows - extra // steps) // blocks
    span = blocks * cols if blocks > 1 else 2 * wide
    given = [] if filled is None else [filled]
    count, base = (steps, 0) if part is None else (steps // 2, part * steps // 2)
    out_specs = [pl.BlockSpec((piece, span), lambda i, at_ref: (base + i, half))]
    out_shape = [jax.ShapeDtypeStruct(shape, F32)]
    if extra:
        out_specs.append(pl.BlockSpec((extra // steps, 2 * wide), lambda i, at_ref: (base + i, 0)))
        out_shape.append(jax.ShapeDtypeStruct((extra, 2 * wide), F32))
    whole = pl.BlockSpec((rows, wide), lambda i, at_ref: (0, 0))
    return pl.pallas_call(
        partial(settle_kernel, steps=steps, base=base, blocks=blocks, cols=cols, extra=extra),
        grid_spec=pltpu.PrefetchScalarGridSpec(
            num_scalar_prefetch=1,
            grid=(count,),
            in_specs=[whole] * (2 * steps) + [pl.BlockSpec(memory_space=pl.ANY)] * len(given),
            out_specs=out_specs,
        ),
        out_shape=out_shape,
        input_output_aliases={1 + 2 * steps: 0} if given else {},
        cost_estimate=cost(7 if part is None else 4),
        compiler_params=kernel_params(),
    )(at, *both[0], *both[1], *given)


def cut_rows_kernel(v_ref, *out_refs, cut):
    for ref, first in zip(out_refs, cut):
        ref[...] = v_ref[first : first + ref.shape[0], :]


def cut_rows(v, cut):
    whole = pl.BlockSpec(memory_space=pltpu.VMEM)
    sizes = [b - a for a, b in zip(cut, cut[1:])]
    return pl.pallas_call(
        partial(cut_rows_kernel, cut=cut),
        in_specs=[whole],
        out_specs=[whole] * len(sizes),
        out_shape=[jax.ShapeDtypeStruct((size, v.shape[1]), F32) for size in sizes],
        cost_estimate=cost(2),
        compiler_params=kernel_params(),
    )(v)


def spread_rows_kernel(*refs, count):
    out_ref = refs[-1]
    wide = refs[0].shape[1]
    for h in range(count):
        out_ref[:, h * wide : (h + 1) * wide] = refs[h][...].astype(F32)


def spread_rows(parts, shape, half=0, filled=None, part=None):
    rows, wide = parts[0].shape
    given = [] if filled is None else [filled]
    count, base = (8, 0) if part is None else (4, 4 * part)
    return pl.pallas_call(
        partial(spread_rows_kernel, count=len(parts)),
        grid=(count,),
        in_specs=[pl.BlockSpec((rows // 8, wide), lambda i: (base + i, 0))] * len(parts)
        + [pl.BlockSpec(memory_space=pl.ANY)] * len(given),
        out_specs=pl.BlockSpec((rows // 8, wide * len(parts)), lambda i: (base + i, half)),
        out_shape=jax.ShapeDtypeStruct(shape, F32),
        input_output_aliases={len(parts): 0} if given else {},
        cost_estimate=cost(4),
        compiler_params=kernel_params(),
    )(*parts, *given)


def join_kernel(at_ref, *refs):
    part, me = at_ref[0] % 4, at_ref[1]
    near_ref, next_ref, *far_refs, out_ref = refs
    depth = near_ref.shape[0]
    quarter = depth // 4
    half = quarter // 2

    def put(row, ref):
        out_ref[pl.ds(pl.multiple_of(row, half), ref.shape[0]), :] = ref[...]

    put(me * depth, near_ref)
    put((me ^ 1) * depth, next_ref)
    for k in range(2):
        start = (me ^ (2 + k)) * depth
        own, one, two, end, tail = far_refs[k::2]
        put(start + part * quarter, own)
        put(start + (part ^ 1) * quarter, one)
        put(start + (part ^ 2) * quarter, two)
        put(start + (part ^ 3) * quarter, end)
        put(start + (part ^ 3) * quarter + half, tail)


def join(at, pieces, rows):
    wide = pieces[0].shape[1]
    return pl.pallas_call(
        join_kernel,
        in_specs=[pl.BlockSpec(memory_space=pltpu.SMEM)] + [pl.BlockSpec(memory_space=pltpu.VMEM)] * len(pieces),
        out_specs=pl.BlockSpec(memory_space=pltpu.VMEM),
        out_shape=jax.ShapeDtypeStruct((rows, wide), BF16),
        cost_estimate=cost(4),
        compiler_params=kernel_params(),
    )(at, *pieces)


def swap(v, bit):
    return jax.tree.map(
        lambda a: lax.ppermute(a, "wsh", [(i, i ^ bit) for i in range(lax.axis_size("wsh"))]), v
    )


def shifted(v, distance):
    count = lax.axis_size("seq")
    route = [(i - distance, i) for i in range(count) if 0 <= i - distance < count]
    return jax.tree.map(lambda a: lax.ppermute(a, "seq", route), v)


def spread_out(v):
    one = swap(v, 1)
    two = swap(v, 2)
    return [v, one, two, swap(two, 1)]


def sum_to_owner(parts, own_cast=BF16):
    got1, got3 = swap((parts[1].astype(own_cast), parts[3].astype(own_cast)), 1)
    mine = parts[0] + got1.astype(F32)
    other = (parts[2] + got3.astype(F32)).astype(own_cast)
    return mine + swap(other, 2).astype(F32)


def crossed(v, bit):
    got = jnp.split(swap(v, bit), lax.axis_size("wsh"), axis=1)
    return jnp.concatenate([got[r ^ bit] for r in range(len(got))], axis=1)


def sum_all(v):
    v = v + crossed(v, 1)
    return v + crossed(v.astype(BF16), 2).astype(F32)


def hi_lo(v):
    hi = v.astype(BF16)
    return [hi, (v - hi.astype(F32)).astype(BF16)]


def carried_far(total, state, rate, reverse):
    count = lax.axis_size("seq")
    sign = -1 if reverse else 1
    total, state = shifted((total, state), sign)
    hop = 1
    while hop < count:
        got_total, got_state = shifted((total, state), sign * hop)
        state = state + jnp.exp2(rate[None] * total) * got_state
        total = total + got_total
        hop *= 2
    return state


class Carry:
    def __init__(self, total, state, rate, reverse):
        self.total, self.rate, self.reverse = total, rate, reverse
        self.near = lax.axis_size("seq") == 8
        if self.near:
            self.state = state
            self.moved = [seq_xor(self.packed(total, state), 1)]
        else:
            self.moved = [carried_far(total, state, rate, reverse)]

    def held(self, *others):
        count = len(self.moved)
        got = lax.optimization_barrier((*self.moved, *others))
        self.moved = list(got[:count])
        return got[count] if len(others) == 1 else got[count:]

    def packed(self, t, s):
        return jnp.concatenate([s.astype(BF16)] + hi_lo(t), axis=1)

    def opened(self, v):
        v = v.astype(F32)
        n = self.rate.shape[0]
        return v[:, n : n + 1] + v[:, n + 1 : n + 2], v[:, :n]

    def fall(self, t):
        return jnp.exp2(self.rate[None] * t)

    def second(self):
        if not self.near:
            return self
        place = lax.axis_index("seq")
        self.other_total, self.other_state = self.opened(self.moved[0])
        self.late = (place % 2 == 1) != self.reverse
        early_state = jnp.where(self.late, self.other_state, self.state)
        late_state = jnp.where(self.late, self.state, self.other_state)
        late_total = jnp.where(self.late, self.total, self.other_total)
        message = self.packed(self.total + self.other_total, self.fall(late_total) * early_state + late_state)
        sign = -1 if self.reverse else 1
        self.moved = [shifted(message, sign * 2 * k) for k in range(1, 4)]
        return self

    def result(self):
        if not self.near:
            return self.moved[0]
        got = [self.opened(v) for v in self.moved]
        carry = got[-1][1]
        for t, s in reversed(got[:-1]):
            carry = s + self.fall(t) * carry
        return jnp.where(self.late, self.fall(self.other_total) * carry + self.other_state, carry)


def seq_xor(v, bits):
    return lax.ppermute(v, "seq", [(i, i ^ bits) for i in range(lax.axis_size("seq"))])


def tied(v, *before):
    return lax.optimization_barrier((v, before))[0]


def at_index(v, index, axis):
    return lax.dynamic_index_in_dim(v, index, axis, False)


RING = (0, 2, 4, 6, 7, 5, 3, 1)


def ring_place():
    q = lax.axis_index("seq")
    return jnp.where(q % 2 == 0, q // 2, len(RING) - 1 - q // 2)


def ring_device(place):
    place = place % len(RING)
    return jnp.where(place < len(RING) // 2, 2 * place, 2 * len(RING) - 1 - 2 * place)


def ring_order():
    places = [RING.index(q) for q in range(len(RING))]
    p = ring_place()
    return [(p - k) % len(RING) for k in places] + [(k - p) % len(RING) for k in places]


class Ring:
    def __init__(self, share, between, own=None):
        self.share, self.between = share, between
        self.count, self.steps = len(RING), 0
        self.place = ring_place()
        if own is None:
            self.send([self.chunk(d, 1) for d in range(2)])
        else:
            self.steps = self.count - 1
            self.rounds = [[v] for v in own]
            self.send(own)

    def chunk(self, d, k):
        return self.share(d, ring_device(self.place + (k if d else self.count - k)))

    def send(self, held):
        self.steps += 1
        self.moving = []
        for d in range(2):
            route = [(RING[k], RING[(k + (-1 if d else 1)) % self.count]) for k in range(self.count)]
            self.moving.append(lax.ppermute(held[d], "seq", route))

    def step(self):
        k = self.steps + 1
        if k < self.count:
            self.send([self.added(d, k) for d in range(2)])
        elif k == self.count:
            own = self.between([self.added(d, k) for d in range(2)])
            self.rounds = [[v] for v in own]
            self.send(own)
        else:
            for d in range(2):
                self.rounds[d].append(self.moving[d])
            if k < 2 * self.count - 1:
                self.send(self.moving)

    def added(self, d, k):
        return (self.moving[d].astype(F32) + self.chunk(d, k).astype(F32)).astype(BF16)

    def result(self):
        return self.rounds

    def done(self):
        return self.steps >= self.count and len(self.rounds[0]) == self.count


def advance(rings, *others):
    count = 2 * len(rings)
    got = lax.optimization_barrier((*[v for ring in rings for v in ring.moving], *others))
    for i, ring in enumerate(rings):
        ring.moving = list(got[2 * i : 2 * i + 2])
        ring.step()
    return got[count] if len(others) == 1 else got[count:]


def crossed_blocks(own):
    share = [at_index(own, lax.axis_index("wsh") ^ r, 0) for r in range(own.shape[0])]
    return jnp.stack([share[0]] + [swap(share[r], r) for r in range(1, own.shape[0])])


def reduced(rows):
    return lax.psum_scatter(rows, "seq", scatter_dimension=0, tiled=True)


def local(
    hidden,
    teacher,
    cotangent,
    lengths,
    norm_gain,
    in_weight,
    conv_weight,
    conv_bias,
    x_weight,
    dt_weight,
    dt_bias,
    a_log,
    skip_gain,
    out_weight,
):
    me = lax.axis_index("wsh")
    place = lax.axis_index("seq")
    seqs = lax.axis_size("wsh")
    seq_count = lax.axis_size("seq")
    tokens, width = hidden.shape[1:]
    inner = out_weight.shape[0]
    depth = in_weight.shape[0]
    states = a_log.shape[0]
    rank = dt_weight.shape[0]
    taps = conv_weight.shape[0]
    rows = seqs * tokens

    def slots(pieces):
        return [at_index(pieces, me ^ r, 0) for r in range(seqs)]

    at = jnp.stack([place, me]).astype(jnp.int32)

    quarter = depth // 4
    half = quarter // 2
    part = place % 4

    def columns_from(start, ready):
        def block(r, first, size):
            return lax.dynamic_slice(ready, (first, start + (me ^ r) * inner), (size, inner))

        sent = [block(r, part * quarter, quarter) for r in (2, 3)]
        far = [swap(v, r) for v, r in zip(sent, (2, 3))]
        return far, [block(0, 0, depth), swap(block(1, 0, depth), 1)], sent

    def over_seq(far):
        return [seq_xor(v, bit) for bit in (1, 2) for v in far]

    def ends(by):
        return [seq_xor(v[:half], 1) for v in by[2:]] + [seq_xor(v[half:], 2) for v in by[:2]]

    x_far, x_near, x_sent = columns_from(0, in_weight)

    note = jnp.concatenate([norm_gain.astype(F32), lengths.astype(F32), jnp.zeros((127,), F32)])
    notes = jnp.stack(spread_out(tied(note, x_sent)))
    gain = jnp.concatenate(slots(notes[:, : norm_gain.shape[0]]))
    slot_lengths = notes[:, norm_gain.shape[0]]
    count = jnp.sum(jnp.minimum(slot_lengths, seq_count * tokens))
    positions = place * tokens + lax.iota(jnp.int32, tokens)
    valid = (positions[None, :].astype(F32) < slot_lengths[:, None]).astype(F32)
    halo_positions = place * tokens - HALO + lax.iota(jnp.int32, HALO + tokens)
    halo_valid = (halo_positions[None, :].astype(F32) < slot_lengths[:, None]).astype(F32)

    rows_in = hidden[0].astype(F32)
    scale = lax.rsqrt(jnp.mean(rows_in * rows_in, axis=1, keepdims=True) + NORM_EPS)
    normed_own = (rows_in * scale * gain).astype(BF16)
    before = shifted(normed_own[tokens - HALO :], 1)
    normed_own = tied(jnp.concatenate([before, normed_own], axis=0), x_far)
    normed_one, normed_two = swap(normed_own, 1), swap(normed_own, 2)
    x_by = over_seq(x_far)
    x_ends = ends(x_by)
    normed_two, x_ends = lax.optimization_barrier((normed_two, x_ends))
    normed = [normed_own, normed_one, normed_two, swap(normed_two, 1)]
    x_columns = join(at, [*x_near, *x_far, *x_by, *x_ends], width)
    z_far, z_near, _ = columns_from(seqs * inner, tied(in_weight, normed_two))
    normed = jnp.stack(normed)
    normed_tokens = normed[:, HALO:].reshape(rows, width)

    x_both = product(normed.reshape(seqs * (HALO + tokens), width), x_columns, PLAIN)
    x_in = (x_both.reshape(seqs, HALO + tokens, inner) * halo_valid[:, :, None]).astype(BF16)
    padded = x_in[:, HALO - (taps - 1) :].astype(F32)
    conv_f = conv_weight.astype(F32)
    conv_out = conv_bias.astype(F32) + sum(
        conv_f[tap] * padded[:, tap : tap + tokens] for tap in range(taps)
    )
    conv_out = conv_out.reshape(rows, inner)
    act = silu_value(conv_out).astype(BF16)
    proj = sum_all(tied(product(x_weight, act, COLS_LAST), z_far)).astype(BF16)
    dt_low = proj[:rank]
    bc = proj[rank:].astype(F32)
    step = jax.nn.softplus(product(dt_low, dt_weight, ROWS_FIRST) + dt_bias.astype(F32))
    log_rate = a_log.astype(F32)
    rate = -jnp.exp(log_rate) * LOG2E
    skip = skip_gain.astype(F32)[None]

    z_by = over_seq(tied(z_far, step))
    last_far, total_far = p1(2, step, act, bc, rate, tokens)
    z_by, last_far, total_far = lax.optimization_barrier((z_by, last_far, total_far))
    z_ends = ends(z_by)
    carry_far = Carry(total_far, last_far, rate, False)
    last_near, total_near = p1(0, tied(step, last_far), act, bc, rate, tokens)
    z_ends, last_near, total_near = carry_far.held(z_ends, last_near, total_near)
    carry_far.second()
    carry_near = Carry(total_near, last_near, rate, False)
    z_columns = join(at, [*z_near, *z_far, *z_by, *z_ends], width)
    z_part = product(normed_tokens, z_columns, PLAIN)
    z_part = carry_near.held(carry_far.held(z_part))
    carry_near.second()
    carry_far = carry_far.result()
    mixed_far, gated_far, starts_far = p2(2, step, act, z_part, bc, rate, skip, carry_far, tokens)
    mixed_far, gated_far, starts_far = carry_near.held(mixed_far, gated_far, starts_far)
    carry_near = carry_near.result()

    def parts(gated):
        return product(gated, out_weight, PLAIN).reshape(2, tokens, width)

    far = parts(gated_far)
    far = swap((far[0] + swap(far[1].astype(BF16), 1).astype(F32)).astype(BF16), 2)
    mixed_near, gated_near, starts_near = p2(0, step, act, z_part, bc, rate, skip, carry_near, tokens)
    far, gated_near = lax.optimization_barrier((far, gated_near))
    near = parts(gated_near)
    near = near[0] + swap(near[1].astype(BF16), 1).astype(F32)
    full = rows_in + near + far.astype(F32)
    own_valid = valid[0][:, None]
    miss = full - teacher[0].astype(F32)
    g_full = cotangent[0].astype(F32) + 2.0 / (width * count) * own_valid * miss
    g_own = g_full.astype(BF16)
    loss_part = jnp.sum(own_valid * miss * miss)

    g_one, g_two = swap(g_own, 1), swap(g_own, 2)
    g_branch_near = jnp.concatenate([g_own, g_one], axis=0)

    def into_mixer(g_branch, mixed, first):
        z = z_part[first * tokens : (first + 2) * tokens]
        g_gated = product(g_branch, out_weight, COLS_LAST)
        return g_gated * silu_value(z), (g_gated * mixed * silu_slope(z)).astype(BF16)

    g_mixed_near, g_z_near = into_mixer(g_branch_near, mixed_near, 0)
    first_near = b1(0, step, g_mixed_near, bc, rate, tokens)
    g_two, first_near = lax.optimization_barrier((g_two, first_near))
    back_near = Carry(total_near, first_near, rate, True)
    g_branch_far = jnp.concatenate([g_two, swap(g_two, 1)], axis=0)
    gated = jnp.concatenate([gated_near, gated_far], axis=0)
    out_grad = product(gated, jnp.concatenate([g_branch_near, g_branch_far], axis=0), ROWS_FIRST).astype(BF16)
    by_steps = seq_count == 8
    g_mixed_far, g_z_far = into_mixer(g_branch_far, mixed_far, 2)
    g_mixed_far, g_z_far = back_near.held(g_mixed_far, g_z_far)
    back_near.second()
    first_far = b1(2, step, g_mixed_far, bc, rate, tokens)
    first_far = back_near.held(first_far)
    back_near = back_near.result()
    back_far = Carry(total_far, first_far, rate, True)
    g_z = jnp.concatenate([g_z_near, g_z_far], axis=0)

    def in_shares(g, normed):
        return product(normed, g, ROWS_FIRST).astype(BF16).reshape(seqs, seq_count, depth // seq_count, g.shape[1])

    def way(v, d):
        wide = v.shape[-1] // 2
        return v[..., d * wide : (d + 1) * wide]

    def in_chunk(shares):
        return lambda d, q: at_index(way(shares, d), q, 1).reshape(width // seq_count, inner // 2)

    def in_between(own):
        return [crossed_blocks(v.reshape(seqs, -1, inner // 2)).reshape(v.shape) for v in own]

    out_own = reduced(out_grad)
    pair_near = (step, act, g_mixed_near, bc, rate, skip, starts_near, back_near, tokens)
    zero = b2(0, 1, None, *pair_near)
    zero = back_far.held(*zero)
    back_far.second()
    g_z = tied(g_z, zero)
    z_shares = jnp.swapaxes(in_shares(g_z, normed_tokens), 0, 1).reshape(width, inner)
    one = b2(1, 1, zero[:2], *pair_near)
    one = back_far.held(*one)
    back_far = back_far.result()
    z_shares, back_far = lax.optimization_barrier((z_shares, back_far))
    pair_far = (step, act, g_mixed_far, bc, rate, skip, starts_far, back_far, tokens)
    two = b2(2, 1, one[:2], *pair_far)
    out_own, *two = lax.optimization_barrier((out_own, *two))
    z_own = reduced(tied(z_shares, out_own))
    three = b2(3, 1, two[:2], *pair_far)
    far = [*three[:2], *[jnp.concatenate([v, w]) for v, w in zip(two[2:], three[2:])]]
    near = [jnp.concatenate([v, w]) for v, w in zip(zero[2:], one[2:])]
    g_pre, g_act_part = far[:2]
    g_b, g_c = [jnp.concatenate([near[i], far[2 + i]]).reshape(rows, states).T for i in (0, 1)]
    rate_sum, sums = [jnp.sum(near[i] + far[2 + i], axis=0) for i in (2, 3)]
    dt_bias_grad, skip_grad = jnp.sum(sums, axis=1)
    g_dt_low = product(dt_weight, g_pre, COLS_LAST)
    g_proj = sum_all(
        jnp.concatenate([g_dt_low, g_b, g_c], axis=0)
    ).astype(BF16)
    g_act = g_act_part + product(g_proj, x_weight, ROWS_FIRST)
    g_conv = (g_act * silu_slope(conv_out)).reshape(seqs, tokens, inner)
    g_padded = jnp.pad(g_conv, ((0, 0), (HALO, taps - 1), (0, 0)))
    g_x = sum(
        conv_f[tap] * g_padded[:, taps - 1 - tap : taps - 1 - tap + HALO + tokens] for tap in range(taps)
    )
    g_x = (g_x * halo_valid[:, :, None]).astype(BF16)
    conv_grad = [jnp.sum(g_conv * padded[:, tap : tap + tokens], axis=(0, 1)) for tap in range(taps)]
    small = [
        product(g_proj, act, PLAIN),
        product(dt_low, g_pre, PLAIN),
        rate_sum * (rate * LN2),
        jnp.stack(conv_grad),
        jnp.sum(g_conv, axis=(0, 1))[None],
        dt_bias_grad[None],
        skip_grad[None],
    ]
    cut = [0]
    for piece in small:
        cut.append(cut[-1] + piece.shape[0])
    lines = 16 * seq_count
    small.append(jnp.zeros((-cut[-1] % lines, inner), F32))
    small = jnp.concatenate(small, axis=0)
    normed_all = normed.reshape(seqs * (HALO + tokens), width)
    g_x_all = g_x.reshape(seqs * (HALO + tokens), inner)
    if by_steps:
        x_shares = in_shares(g_x_all, normed_all)
        small_shares = small.astype(BF16).reshape(seq_count, -1, inner)
        z_own, x_shares, small_shares, g_x = lax.optimization_barrier((z_own, x_shares, small_shares, g_x))
        large = width // seq_count
        chunk_of = in_chunk(x_shares)

        def x_chunk(d, q):
            return jnp.concatenate([chunk_of(d, q), at_index(way(small_shares, d), q, 0)], axis=0)

        def x_between(own):
            return [jnp.concatenate([x, v[large:]], axis=0) for x, v in zip(in_between([v[:large] for v in own]), own)]

        x_ring = Ring(x_chunk, x_between)
        out_ring = Ring(None, None, [way(out_own, d) for d in range(2)])
        z_row = crossed_blocks(z_own.reshape(seqs, -1, inner)).reshape(-1, inner)
        rings = [x_ring, out_ring]
        z_row, g_x = advance(rings, z_row, g_x)
        z_ring = Ring(None, None, [way(z_row, d) for d in range(2)])
        rings.append(z_ring)
    after = shifted(g_x[:, HALO - (taps - 1) : HALO], -1)
    g_z = tied(g_z, g_x)

    def to_normed(g, columns, slot):
        return product(g[slot * tokens : (slot + 1) * tokens], columns, COLS_LAST)

    def advanced(*v):
        if by_steps:
            return advance([ring for ring in rings if not ring.done()], *v)
        return v[0] if len(v) == 1 else v

    normed_1, normed_3 = advanced(to_normed(g_z, z_columns, 1), to_normed(g_z, z_columns, 3))
    normed_2, after = advanced(to_normed(g_z, z_columns, 2), after)
    fixed = jnp.pad(after, ((0, 0), (tokens - (taps - 1), 0), (0, 0)))
    g_x = advanced((g_x[:, HALO:] + fixed).reshape(rows, inner))
    normed_1 += to_normed(g_x, x_columns, 1)
    normed_3 += to_normed(g_x, x_columns, 3)
    normed_1, normed_3 = advanced(normed_1.astype(BF16), normed_3.astype(BF16))
    got1, got3 = swap((normed_1, normed_3), 1)
    got1, got3, normed_2 = advanced(got1, got3, normed_2 + to_normed(g_x, x_columns, 2))
    other = swap((normed_2 + got3.astype(F32)).astype(BF16), 2)
    normed_0 = advanced(to_normed(g_z, z_columns, 0))
    normed_0 = advanced(normed_0 + to_normed(g_x, x_columns, 0) + got1.astype(F32))
    if by_steps:
        other = advanced(other)
    g_normed = normed_0 + other.astype(F32)
    gain_part = jnp.sum(g_normed * rows_in * scale, axis=0)
    tail = jnp.concatenate([gain_part, jnp.full((128,), loss_part)])
    if by_steps:
        where = jnp.stack([me] + ring_order()).astype(jnp.int32)
        out_is = partial(settle, where, out_ring.result(), out_weight.shape, 1, width)
        z_is = partial(settle, where, z_ring.result(), in_weight.shape, seqs, inner, half=1)
        assert out_ring.done() and z_ring.done()
        tail, out_owned = advanced(tail + seq_xor(tail, 1), out_is(part=0)[0])
        tail, out_owned = advanced(tail + seq_xor(tail, 2), out_is(part=1, filled=out_owned)[0])
        tail, in_owned = advanced(tail + seq_xor(tail, 4), z_is(part=0)[0])
    else:
        tail = lax.psum(tail, "seq")
    gain_share = slots(tail[:width].reshape(seqs, -1))
    gain_grad = gain_share[0] + sum(swap(gain_share[r], r) for r in range(1, seqs))
    loss_sum = tail[width:] + swap(tail[width:], 1)
    loss = (loss_sum + swap(loss_sum, 2))[0] / (width * count)
    if by_steps:
        gain_grad, loss, in_owned = advanced(gain_grad, loss, z_is(part=1, filled=in_owned)[0])
        while not x_ring.done():
            in_owned = advanced(in_owned)
        in_owned, small = settle(
            where, x_ring.result(), in_weight.shape, seqs, inner, filled=in_owned, extra=small.shape[0]
        )
    if not by_steps:
        x_shares = jnp.swapaxes(in_shares(g_x_all, normed_all), 0, 1)
        x_row = crossed_blocks(reduced(x_shares.reshape(width, inner)).reshape(seqs, -1, inner))
        x_owned = lax.all_gather(jnp.concatenate(slots(x_row), axis=1), "seq", axis=0, tiled=True)
        small = lax.psum(small, "seq")
        out_owned = lax.all_gather(out_own, "seq", axis=0, tiled=True)
        out_owned = spread_rows([out_owned], out_weight.shape)
        in_owned = spread_rows([x_owned], in_weight.shape)
        z_row = crossed_blocks(z_own.reshape(seqs, -1, inner))
        z_owned = lax.all_gather(jnp.concatenate(slots(z_row), axis=1), "seq", axis=0, tiled=True)
        in_owned = spread_rows([z_owned], in_weight.shape, 1, in_owned)
    x_grad, dt_grad, log_rate_grad, conv_grad, conv_bias_grad, dt_bias_grad, skip_grad = cut_rows(small, cut)
    weighted = g_normed * gain
    g_rows = (
        g_full
        + scale * weighted
        - rows_in * scale * scale * scale * jnp.mean(weighted * rows_in, axis=1, keepdims=True)
    )
    return (
        full[None].astype(BF16),
        loss,
        g_rows[None].astype(BF16),
        gain_grad,
        in_owned,
        conv_grad,
        conv_bias_grad[0],
        x_grad,
        dt_grad,
        dt_bias_grad[0],
        log_rate_grad,
        skip_grad[0],
        out_owned,
    )


def solution(mesh):
    rows = P("wsh", "seq", None)
    first, second = P("wsh", None), P(None, "wsh")
    one = P("wsh")
    return jax.shard_map(
        local,
        mesh=mesh,
        in_specs=(
            rows, rows, rows, one, one, first, second, one, second, second, one, second, one, first,
        ),
        out_specs=(
            rows, P(), rows, one, first, second, one, second, second, one, second, one, first,
        ),
        check_vma=False,
    )
```

time: 1080 us -> 748 us (0.69)
  waiting for transfers between devices: 422 us -> 194 us
  blocking collectives: 155 us -> 0 us
  starting transfers between devices: 61.6 us -> 140 us
  local copies, waits for them, and re-layouts: 86.5 us -> 29.9 us
  Pallas kernels: 173 us -> 224 us
  other arithmetic: 70.9 us -> 55 us
    all_gather x3 -> x0, waiting for transfers between devices: 155 us -> none  [the longest x2 141 us: in_rows(): return lax.all_gather(row, 'seq', axis=0, tiled=True).astype(F32)]
    ppermute x0 -> x79, waiting for transfers between devices: none -> 110 us  [the longest x56 94.3 us: send(): self.moving.append(lax.ppermute(held[d], 'seq', route))]
    all_gather x1 -> x0, blocking collectives: 89.5 us -> none  [local(): gain = lax.all_gather(norm_gain, 'wsh', axis=0, tiled=True).astype(F32)]
    ppermute x0 -> x79, starting transfers between devices: none -> 87.2 us  [the longest x56 62.5 us: send(): self.moving.append(lax.ppermute(held[d], 'seq', route))]
    ppermute x16 -> x14, waiting for transfers between devices: 69.1 us -> 0.28 us  [shifted(): return jax.tree.map(lambda a: lax.ppermute(a, 'seq', route), v)]
    psum x1 -> x0, waiting for transfers between devices: 51.5 us -> none  [local(): small = lax.psum(small, 'seq')]
    pallas_call x4 -> x18, Pallas kernels: 173 us -> 224 us  [the longest x4 107 us: b2(): pl.pallas_call(partial(b2_kernel, eb=eb, n=n), grid=(count,), in_specs=[b...]
    psum x1 -> x0, blocking collectives: 43.2 us -> none  [local(): lax.psum(jnp.sum(own_valid * miss * miss), ('seq', 'wsh')) / (width * count)]
  transfers between devices with their start and end apart: 48 -> 134, of which waited for: 28 -> 63; matrix products, arithmetic and copies ran while one was open for 13% -> 17% of each run, Pallas kernels for 11% -> 29%
where the time goes in v2:
time: 748 us; the launch traced here: 741 us
  Pallas kernels  224 us (30%)
  waiting for transfers between devices  194 us (26%)
  starting transfers between devices  140 us (19%)
  matrix products  79.3 us (11%)
  other arithmetic  55 us (7%)
  local copies, waits for them, and re-layouts  29.9 us (4%)
  between operations  20.2 us (3%)
    pallas_call x4, Pallas kernels, b2(): pl.pallas_call(partial(b2_kernel, eb=eb, n=n), grid=(count,), in_specs=[b...  107 us
    ppermute x56, waiting for transfers between devices, send(): self.moving.append(lax.ppermute(held[d], 'seq', route))  94.3 us
    dot_general x23, matrix products, product(): return lax.dot_general(left, right, dims, preferred_element_type=F32)  79.3 us
    ppermute x39, waiting for transfers between devices, swap(): lax.ppermute(a, 'wsh', [(i, i ^ bit) for i in range(lax.axis_size('wsh'))])  63.6 us
    ppermute x56, starting transfers between devices, send(): self.moving.append(lax.ppermute(held[d], 'seq', route))  62.5 us
    pallas_call x2, Pallas kernels, p2(): pl.pallas_call(partial(p2_kernel, eb=eb, n=n), grid=(2,), in_specs=[blk,...  34.9 us
    pallas_call x5, Pallas kernels, settle(): pl.pallas_call(partial(settle_kernel, steps=steps, base=base, blocks=bloc...  30.2 us
    ppermute x39, starting transfers between devices, swap(): lax.ppermute(a, 'wsh', [(i, i ^ bit) for i in range(lax.axis_size('wsh'))])  27.1 us
  transfers between devices with their start and end apart: 134, of which 63 were waited for; matrix products, arithmetic and copies ran while one was open for 17% of the time, Pallas kernels for 29%

profile of v2, /device:TPU:0, one launch (start us, length us, event | category | flops | bytes accessed | tf_op | source)
XLA Modules:
  0.0 741.1 jit_solution(8612649086689155951)
XLA Ops:
  23.1 6.7 collective-permute-done.5.refs_3_
  29.9 5.7 collective-permute-done.4.refs_2_
  71.4 7.7 %fusion.17 = f32[4,272,1024]{2,1,0:T(8,128)S(1)} fusion(bf16[2048,1024]{1,0:T(8,128)(2,1)} %shard_map.237, bf16[1,272,2048]{2,1,0:T(8,128)(2,1)} %bitcast.10, bf16[1,272,2048]{2,1,0:T(8,128)(2,1)S(1)} %bitcast.291, bf16[1,272,2048]{2,1,0:T(8,128)(2,1)} %bitcast.8, bf16[1,272,2048]{2,1,0:T(8,128)(2,1)S(1)} %bitcast.282), kind=kOutput, calls=%fused_computation.27 | convolution fusion | flops 4570087424 | bytes 13107200 | tf_op jit(solution)/shard_map/dot_general | solution.py:25
  94.6 6.9 collective-permute-done.21
  110.8 9.9 %shard_map.238 = (f32[2,16,1024]{2,1,0:T(8,128)}, f32[2,1,1024]{2,1,0:T(1,128)}) custom-call(f32[1024,1024]{1,0:T(8,128)} %compare_select_fusion.step_ref, bf16[1024,1024]{1,0:T(8,128)(2,1)} %copy-done.7, f32[32,1024]{1,0:T(8,128)} %slice_convert_fusion.2.bc_ref, f32[16,1024]{1,0:T(8,128)} %fusion.77.rate_ref), custom_call_target="tpu_custom_call" | custom-call | flops 8999999488 | tf_op jit(solution)/shard_map/pallas_call | solution.py:98
  129.3 9.9 %shard_map.239 = (f32[2,16,1024]{2,1,0:T(8,128)}, f32[2,1,1024]{2,1,0:T(1,128)}) custom-call(f32[1024,1024]{1,0:T(8,128)} %compare_select_fusion.step_ref, bf16[1024,1024]{1,0:T(8,128)(2,1)} %copy-done.7, f32[32,1024]{1,0:T(8,128)} %slice_convert_fusion.2.bc_ref, f32[16,1024]{1,0:T(8,128)} %fusion.77.rate_ref), custom_call_target="tpu_custom_call" | custom-call | flops 8999999488 | tf_op jit(solution)/shard_map/pallas_call | solution.py:98
  155.8 8.3 %fusion.101.z_ref = f32[1024,1024]{1,0:T(8,128)} fusion(bf16[1024,2048]{1,0:T(8,128)(2,1)S(1)} %bitcast.285, bf16[2048,1024]{1,0:T(8,128)(2,1)} %shard_map.240), kind=kOutput, calls=%fused_computation.316 | convolution fusion | flops 4294967296 | bytes 12582912 | tf_op jit(solution)/shard_map/dot_general | solution.py:25
  169.1 17.6 %shard_map.241 = (f32[512,1024]{1,0:T(8,128)}, bf16[512,1024]{1,0:T(8,128)(2,1)}, f32[2,8,16,1024]{3,2,1,0:T(8,128)}) custom-call(f32[1024,1024]{1,0:T(8,128)} %compare_select_fusion.step_ref, bf16[1024,1024]{1,0:T(8,128)(2,1)} %copy-done.7, f32[1024,1024]{1,0:T(8,128)} %fusion.101.z_ref, f32[32,1024]{1,0:T(8,128)} %slice_convert_fusion.2.bc_ref, ...), custom_call_target="tpu_custom_call" | custom-call | flops 16000000000 | tf_op jit(solution)/shard_map/pallas_call | solution.py:158
  195.2 17.3 %shard_map.242 = (f32[512,1024]{1,0:T(8,128)}, bf16[512,1024]{1,0:T(8,128)(2,1)}, f32[2,8,16,1024]{3,2,1,0:T(8,128)}) custom-call(f32[1024,1024]{1,0:T(8,128)} %compare_select_fusion.step_ref, bf16[1024,1024]{1,0:T(8,128)(2,1)} %copy-done.7, f32[1024,1024]{1,0:T(8,128)} %fusion.101.z_ref, f32[32,1024]{1,0:T(8,128)} %slice_convert_fusion.2.bc_ref, ...), custom_call_target="tpu_custom_call" | custom-call | flops 16000000000 | tf_op jit(solution)/shard_map/pallas_call | solution.py:158
  212.4 6.4 collective-permute-done.40
  241.6 10.6 %shard_map.243 = f32[2,16,1024]{2,1,0:T(8,128)} custom-call(f32[1024,1024]{1,0:T(8,128)} %compare_select_fusion.step_ref, f32[512,1024]{1,0:T(8,128)} %get-tuple-element.448.dy_ref, f32[32,1024]{1,0:T(8,128)} %slice_convert_fusion.2.bc_ref, f32[16,1024]{1,0:T(8,128)} %fusion.77.rate_ref), custom_call_target="tpu_custom_call" | custom-call | flops 8999999488 | tf_op jit(solution)/shard_map/pallas_call | solution.py:201
  252.2 7.7 %collective-permute-done.43 = bf16[256,2048]{1,0:T(8,128)(2,1)} collective-permute-done((bf16[256,2048]{1,0:T(8,128)(2,1)S(1)}, bf16[256,2048]{1,0:T(8,128)(2,1)}, u32[]{:S(2)}, u32[]{:S(2)}) %collective-permute-start.43) | collective-permute-done | bytes 1048608 | tf_op jit(solution)/shard_map/ppermute | solution.py:486
  262.8 8.8 %multiply_convert_fusion.1 = (bf16[512,1024]{1,0:T(8,128)(2,1)}, f32[512,1024]{1,0:T(8,128)}) fusion(f32[512,1024]{1,0:T(8,128)} %get-tuple-element.265, f32[1024,1024]{1,0:T(8,128)} %fusion.101.z_ref, bf16[1024,2048]{1,0:T(8,128)(2,1)} %param.27, bf16[256,2048]{1,0:T(8,128)(2,1)S(1)} %collective-permute-done.45, bf16[256,2048]{1,0:T(8,128)(2,1)} %collective-permute-done.43), kind=kOutput, calls=%fused_computation.85 | convolution fusion | flops 2157969408 | bytes 13631488 | tf_op jit(solution)/shard_map/dot_general | solution.py:25
  275.7 8.2 %fusion.19 = bf16[1024,2048]{1,0:T(8,128)(2,1)} fusion(bf16[256,2048]{1,0:T(8,128)(2,1)} %copy-done.123, bf16[256,2048]{1,0:T(8,128)(2,1)} %collective-permute-done.43, bf16[256,2048]{1,0:T(8,128)(2,1)S(1)} %copy-done.122, bf16[256,2048]{1,0:T(8,128)(2,1)S(1)} %fusion.66, bf16[512,1024]{1,0:T(8,128)(2,1)S(1)} %copy-done.143, ...), kind=kOutput, calls=%fused_computation.39 | convolution fusion | flops 4318035968 | bytes 10485760 | tf_op jit(solution)/shard_map/dot_general | solution.py:25
  284.0 10.2 %shard_map.244 = f32[2,16,1024]{2,1,0:T(8,128)} custom-call(f32[1024,1024]{1,0:T(8,128)} %compare_select_fusion.step_ref, f32[512,1024]{1,0:T(8,128)} %get-tuple-element.268.dy_ref, f32[32,1024]{1,0:T(8,128)} %slice_convert_fusion.2.bc_ref, f32[16,1024]{1,0:T(8,128)} %fusion.77.rate_ref), custom_call_target="tpu_custom_call" | custom-call | flops 8999999488 | tf_op jit(solution)/shard_map/pallas_call | solution.py:201
  297.3 26.5 %shard_map.245 = (bf16[1024,1024]{1,0:T(8,128)(2,1)}, f32[1024,1024]{1,0:T(8,128)}, f32[1,32,128]{2,1,0:T(8,128)}, f32[1,32,128]{2,1,0:T(8,128)}, f32[1,16,1024]{2,1,0:T(8,128)}, /*index=5*/f32[1,2,8,1024]{3,2,1,0:T(8,128)}) custom-call(f32[1024,1024]{1,0:T(8,128)} %compare_select_fusion.step_ref, bf16[1024,1024]{1,0:T(8,128)(2,1)} %copy-done.7, ...), custom_call_target="tpu_custom_call" | custom-call | flops 24999999488 | tf_op jit(solution)/shard_map/pallas_call | solution.py:319
  328.2 27.0 %shard_map.246 = (bf16[1024,1024]{1,0:T(8,128)(2,1)}, f32[1024,1024]{1,0:T(8,128)}, f32[1,32,128]{2,1,0:T(8,128)}, f32[1,32,128]{2,1,0:T(8,128)}, f32[1,16,1024]{2,1,0:T(8,128)}, /*index=5*/f32[1,2,8,1024]{3,2,1,0:T(8,128)}) custom-call(f32[1024,1024]{1,0:T(8,128)} %compare_select_fusion.step_ref, ...), custom_call_target="tpu_custom_call", output_to_operand_aliasing={{0}: (8, {}), {1}: (9, {})} | custom-call | flops 24999999488 | tf_op jit(solution)/shard_map/pallas_call | solution.py:319
  363.3 26.5 %shard_map.247 = (bf16[1024,1024]{1,0:T(8,128)(2,1)}, f32[1024,1024]{1,0:T(8,128)}, f32[1,32,128]{2,1,0:T(8,128)}, f32[1,32,128]{2,1,0:T(8,128)}, f32[1,16,1024]{2,1,0:T(8,128)}, /*index=5*/f32[1,2,8,1024]{3,2,1,0:T(8,128)}) custom-call(f32[1024,1024]{1,0:T(8,128)} %compare_select_fusion.step_ref, ...), custom_call_target="tpu_custom_call", output_to_operand_aliasing={{0}: (8, {}), {1}: (9, {})} | custom-call | flops 24999999488 | tf_op jit(solution)/shard_map/pallas_call | solution.py:319
  389.9 26.6 %shard_map.248 = (bf16[1024,1024]{1,0:T(8,128)(2,1)}, f32[1024,1024]{1,0:T(8,128)}, f32[1,32,128]{2,1,0:T(8,128)}, f32[1,32,128]{2,1,0:T(8,128)}, f32[1,16,1024]{2,1,0:T(8,128)}, /*index=5*/f32[1,2,8,1024]{3,2,1,0:T(8,128)}) custom-call(f32[1024,1024]{1,0:T(8,128)} %compare_select_fusion.step_ref, ...), custom_call_target="tpu_custom_call", output_to_operand_aliasing={{0}: (8, {}), {1}: (9, {})} | custom-call | flops 24999999488 | tf_op jit(solution)/shard_map/pallas_call | solution.py:319
  429.8 6.1 collective-permute-done.54
  443.2 8.8 %multiply_convert_fusion = bf16[4,272,1024]{2,1,0:T(8,128)(2,1)S(1)} fusion(f32[4,256,1024]{2,1,0:T(8,128)} %bitcast.276, f32[1024]{0:T(1024)S(1)} %bitcast.337, f32[1024]{0:T(1024)S(1)} %bitcast.335, f32[1024]{0:T(1024)S(1)} %bitcast.333, f32[1024]{0:T(1024)S(1)} %bitcast.331, f32[4,272]{1,0:T(4,128)S(1)} %copy-done.95), kind=kLoop, calls=%fused_computation.3 | loop fusion | flops 10027008 | bytes 6443264 | tf_op jit(solution)/shard_map/convert_element_type | solution.py:882
  452.0 8.8 %bitcast_convert_fusion = bf16[2048,1024]{1,0:T(8,128)(2,1)} fusion(bf16[4,272,1024]{2,1,0:T(8,128)(2,1)S(1)} %multiply_convert_fusion, bf16[1,272,2048]{2,1,0:T(8,128)(2,1)} %bitcast.10, bf16[1,272,2048]{2,1,0:T(8,128)(2,1)} %bitcast.292, bf16[1,272,2048]{2,1,0:T(8,128)(2,1)} %bitcast.8, bf16[1,272,2048]{2,1,0:T(8,128)(2,1)} %bitcast.283), kind=kOutput, calls=%fused_computation.1 | convolution fusion | flops 4572184576 | bytes 10878976 | tf_op jit(solution)/shard_map/dot_general | solution.py:25
  460.8 19.8 %reduce-scatter.5.cloned.1.call-done = bf16[256,1024]{1,0:T(8,128)(2,1)} async-done(((bf16[2048,1024]{1,0:T(8,128)(2,1)}), bf16[256,1024]{1,0:T(8,128)(2,1)}) %reduce-scatter.5.cloned.1.call-update) | async-done | bytes 524304 | tf_op jit(solution)/shard_map/reduce_scatter | solution.py:680
  493.3 8.8 %collective-permute-done.58.refs_9_ = bf16[128,1024]{1,0:T(8,128)(2,1)S(1)} collective-permute-done((bf16[128,1024]{1,0:T(8,128)(2,1)S(1)}, bf16[128,1024]{1,0:T(8,128)(2,1)S(1)}, u32[]{:S(2)}, u32[]{:S(2)}) %collective-permute-start.58) | collective-permute-done | bytes 262176 | tf_op jit(solution)/shard_map/ppermute | solution.py:639
  515.2 7.9 %collective-permute-done.67.refs_9_ = bf16[256,512]{1,0:T(8,128)(2,1)S(1)} collective-permute-done((bf16[256,512]{1,0:T(8,128)(2,1)S(1)}, bf16[256,512]{1,0:T(8,128)(2,1)S(1)}, u32[]{:S(2)}, u32[]{:S(2)}) %collective-permute-start.67) | collective-permute-done | bytes 262176 | tf_op jit(solution)/shard_map/ppermute | solution.py:639
  625.6 9.7 %collective-permute-done.107 = bf16[64,512]{1,0:T(8,128)(2,1)S(1)} collective-permute-done((bf16[64,512]{1,0:T(8,128)(2,1)S(1)}, bf16[64,512]{1,0:T(8,128)(2,1)S(1)}, u32[]{:S(2)}, u32[]{:S(2)}) %collective-permute-start.107) | collective-permute-done | bytes 65568 | tf_op jit(solution)/shard_map/ppermute | solution.py:486
  648.3 5.6 collective-permute-done.108.refs_9_
  656.6 5.8 collective-permute-done.111.refs_2_
  668.7 5.5 shard_map.249.refs_16_
  686.8 5.5 shard_map.251.refs_16_
  703.9 5.5 shard_map.252.refs_16_
  721.9 8.3 %shard_map.253 = (f32[512,8192]{1,0:T(8,128)}, f32[384,1024]{1,0:T(8,128)}) custom-call(s32[17]{0:T(128)} %stack.191.at_ref, bf16[304,512]{1,0:T(8,128)(2,1)} %copy-done.63, bf16[304,512]{1,0:T(8,128)(2,1)} %collective-permute-done.104.refs_1_, bf16[304,512]{1,0:T(8,128)(2,1)} %collective-permute-done.111.refs_2_, ...), custom_call_target="tpu_custom_call", output_to_operand_aliasing={{0}: (17, {})} | custom-call | flops 7000000000 | tf_op jit(solution)/shard_map/pallas_call | solution.py:393
  (778 shorter events, 366.3 us)
Async XLA Ops:
  7.2 382.7 %reduce-scatter.3.cloned.1.call-start = ((), (), s32[]{:S(2)}) async-start(), calls=%async_computation.2 | async-start | bytes 4718592 | tf_op jit(solution)/shard_map/reduce_scatter | solution.py:680
  35.6 26.5 %collective-permute-start.6 = (bf16[272,2048]{1,0:T(8,128)(2,1)S(1)}, bf16[272,2048]{1,0:T(8,128)(2,1)S(1)}, u32[]{:S(2)}, u32[]{:S(2)}) collective-permute-start(bf16[272,2048]{1,0:T(8,128)(2,1)S(1)} %pad_maximum_fusion.3), channel_id=1, source_target_pairs={{0,2},{1,3},{2,0},{3,1},{4,6},{5,7},{6,4},{7,5},{8,10},{9,11},{10,... | collective-permute-start | bytes 3342344 | tf_op jit(solution)/shard_map/ppermute | solution.py:486
  51.2 15.7 %collective-permute-start.19 = (bf16[512,1024]{1,0:T(8,128)(2,1)}, bf16[512,1024]{1,0:T(8,128)(2,1)}, u32[]{:S(2)}, u32[]{:S(2)}) collective-permute-start(bf16[512,1024]{1,0:T(8,128)(2,1)} %get-tuple-element.441), channel_id=1, source_target_pairs={{0,1},{1,0},{2,3},{3,2},{4,5},{5,4},{6,7},{7,6},{8,9},{9,8},{10,11... | collective-permute-start | bytes 3145736 | tf_op jit(solution)/shard_map/ppermute | solution.py:486
  64.9 19.3 %collective-permute-start.16 = (bf16[128,1024]{1,0:T(8,128)(2,1)S(1)}, bf16[128,1024]{1,0:T(8,128)(2,1)S(1)}, u32[]{:S(2)}, u32[]{:S(2)}) collective-permute-start(bf16[128,1024]{1,0:T(8,128)(2,1)S(1)} %get-tuple-element.443), channel_id=1, source_target_pairs={{0,3},{1,2},{2,1},{3,0},{4,7},{5,6},{6,5},{7,4},{8,11},{9,10},{10,... | collective-permute-start | bytes 786440 | tf_op jit(solution)/shard_map/ppermute | solution.py:486
  66.4 17.8 %collective-permute-start.15 = (bf16[128,1024]{1,0:T(8,128)(2,1)S(1)}, bf16[128,1024]{1,0:T(8,128)(2,1)S(1)}, u32[]{:S(2)}, u32[]{:S(2)}) collective-permute-start(bf16[128,1024]{1,0:T(8,128)(2,1)S(1)} %get-tuple-element.444), channel_id=1, source_target_pairs={{0,2},{1,3},{2,0},{3,1},{4,6},{5,7},{6,4},{7,5},{8,10},{9,11},{10,... | collective-permute-start | bytes 786440 | tf_op jit(solution)/shard_map/ppermute | solution.py:486
  123.5 15.8 %collective-permute-start.26 = (bf16[2,18,1024]{2,1,0:T(8,128)(2,1)S(1)}, bf16[2,18,1024]{2,1,0:T(8,128)(2,1)S(1)}, u32[]{:S(2)}, u32[]{:S(2)}) collective-permute-start(bf16[2,18,1024]{2,1,0:T(8,128)(2,1)S(1)} %pad_maximum_fusion.15), channel_id=1, source_target_pairs={{0,4},{4,0},{8,12},{12,8},{16,20},{20,16},{24,28},{28,24},{1,5},{5... | collective-permute-start | bytes 221192 | tf_op jit(solution)/shard_map/ppermute | solution.py:589
  139.6 24.6 %collective-permute-start.34 = (bf16[2,18,1024]{2,1,0:T(8,128)(2,1)S(1)}, bf16[2,18,1024]{2,1,0:T(8,128)(2,1)S(1)}, u32[]{:S(2)}, u32[]{:S(2)}) collective-permute-start(bf16[2,18,1024]{2,1,0:T(8,128)(2,1)S(1)} %pad_maximum_fusion.22), channel_id=1, source_target_pairs={{0,24},{4,28},{1,25},{5,29},{2,26},{6,30},{3,27},{7,31}} | collective-permute-start | bytes 221192 | tf_op jit(solution)/shard_map/ppermute | solution.py:493
  143.9 20.2 %collective-permute-start.33 = (bf16[2,18,1024]{2,1,0:T(8,128)(2,1)S(1)}, bf16[2,18,1024]{2,1,0:T(8,128)(2,1)S(1)}, u32[]{:S(2)}, u32[]{:S(2)}) collective-permute-start(bf16[2,18,1024]{2,1,0:T(8,128)(2,1)S(1)} %pad_maximum_fusion.22), channel_id=1, source_target_pairs={{0,16},{4,20},{8,24},{12,28},{1,17},{5,21},{9,25},{13,29},{2,18},{... | collective-permute-start | bytes 221192 | tf_op jit(solution)/shard_map/ppermute | solution.py:493
  145.3 18.9 %collective-permute-start.32 = (bf16[2,18,1024]{2,1,0:T(8,128)(2,1)S(1)}, bf16[2,18,1024]{2,1,0:T(8,128)(2,1)S(1)}, u32[]{:S(2)}, u32[]{:S(2)}) collective-permute-start(bf16[2,18,1024]{2,1,0:T(8,128)(2,1)S(1)} %pad_maximum_fusion.22), channel_id=1, source_target_pairs={{0,8},{4,12},{8,16},{12,20},{16,24},{20,28},{1,9},{5,13},{9,17},{1... | collective-permute-start | bytes 221192 | tf_op jit(solution)/shard_map/ppermute | solution.py:493
  165.2 21.5 %collective-permute-start.38 = (bf16[2,18,1024]{2,1,0:T(8,128)(2,1)S(1)}, bf16[2,18,1024]{2,1,0:T(8,128)(2,1)S(1)}, u32[]{:S(2)}, u32[]{:S(2)}) collective-permute-start(bf16[2,18,1024]{2,1,0:T(8,128)(2,1)S(1)} %pad_maximum_fusion.23), channel_id=1, source_target_pairs={{0,24},{4,28},{1,25},{5,29},{2,26},{6,30},{3,27},{7,31}} | collective-permute-start | bytes 221192 | tf_op jit(solution)/shard_map/ppermute | solution.py:493
  166.5 20.2 %collective-permute-start.37 = (bf16[2,18,1024]{2,1,0:T(8,128)(2,1)S(1)}, bf16[2,18,1024]{2,1,0:T(8,128)(2,1)S(1)}, u32[]{:S(2)}, u32[]{:S(2)}) collective-permute-start(bf16[2,18,1024]{2,1,0:T(8,128)(2,1)S(1)} %pad_maximum_fusion.23), channel_id=1, source_target_pairs={{0,16},{4,20},{8,24},{12,28},{1,17},{5,21},{9,25},{13,29},{2,18},{... | collective-permute-start | bytes 221192 | tf_op jit(solution)/shard_map/ppermute | solution.py:493
  167.8 19.0 %collective-permute-start.36 = (bf16[2,18,1024]{2,1,0:T(8,128)(2,1)S(1)}, bf16[2,18,1024]{2,1,0:T(8,128)(2,1)S(1)}, u32[]{:S(2)}, u32[]{:S(2)}) collective-permute-start(bf16[2,18,1024]{2,1,0:T(8,128)(2,1)S(1)} %pad_maximum_fusion.23), channel_id=1, source_target_pairs={{0,8},{4,12},{8,16},{12,20},{16,24},{20,28},{1,9},{5,13},{9,17},{1... | collective-permute-start | bytes 221192 | tf_op jit(solution)/shard_map/ppermute | solution.py:493
  193.6 25.3 %collective-permute-start.40 = (bf16[256,2048]{1,0:T(8,128)(2,1)S(1)}, bf16[256,2048]{1,0:T(8,128)(2,1)S(1)}, u32[]{:S(2)}, u32[]{:S(2)}) collective-permute-start(bf16[256,2048]{1,0:T(8,128)(2,1)S(1)} %fusion.39), channel_id=1, source_target_pairs={{0,2},{1,3},{2,0},{3,1},{4,6},{5,7},{6,4},{7,5},{8,10},{9,11},{10,... | collective-permute-start | bytes 3145736 | tf_op jit(solution)/shard_map/ppermute | solution.py:486
  234.3 25.5 %collective-permute-start.43 = (bf16[256,2048]{1,0:T(8,128)(2,1)S(1)}, bf16[256,2048]{1,0:T(8,128)(2,1)}, u32[]{:S(2)}, u32[]{:S(2)}) collective-permute-start(bf16[256,2048]{1,0:T(8,128)(2,1)S(1)} %fusion.66), channel_id=1, source_target_pairs={{0,2},{1,3},{2,0},{3,1},{4,6},{5,7},{6,4},{7,5},{8,10},{9,11},{10,... | collective-permute-start | bytes 3145736 | tf_op jit(solution)/shard_map/ppermute | solution.py:486
  271.7 22.7 %collective-permute-start.48 = (bf16[2,18,1024]{2,1,0:T(8,128)(2,1)S(1)}, bf16[2,18,1024]{2,1,0:T(8,128)(2,1)S(1)}, u32[]{:S(2)}, u32[]{:S(2)}) collective-permute-start(bf16[2,18,1024]{2,1,0:T(8,128)(2,1)S(1)} %pad_maximum_fusion.24), channel_id=1, source_target_pairs={{24,0},{28,4},{25,1},{29,5},{26,2},{30,6},{27,3},{31,7}} | collective-permute-start | bytes 221192 | tf_op jit(solution)/shard_map/ppermute | solution.py:493
  273.0 21.4 %collective-permute-start.47 = (bf16[2,18,1024]{2,1,0:T(8,128)(2,1)S(1)}, bf16[2,18,1024]{2,1,0:T(8,128)(2,1)S(1)}, u32[]{:S(2)}, u32[]{:S(2)}) collective-permute-start(bf16[2,18,1024]{2,1,0:T(8,128)(2,1)S(1)} %pad_maximum_fusion.24), channel_id=1, source_target_pairs={{16,0},{20,4},{24,8},{28,12},{17,1},{21,5},{25,9},{29,13},{18,2},{... | collective-permute-start | bytes 221192 | tf_op jit(solution)/shard_map/ppermute | solution.py:493
  274.3 20.1 %collective-permute-start.46 = (bf16[2,18,1024]{2,1,0:T(8,128)(2,1)S(1)}, bf16[2,18,1024]{2,1,0:T(8,128)(2,1)S(1)}, u32[]{:S(2)}, u32[]{:S(2)}) collective-permute-start(bf16[2,18,1024]{2,1,0:T(8,128)(2,1)S(1)} %pad_maximum_fusion.24), channel_id=1, source_target_pairs={{8,0},{12,4},{16,8},{20,12},{24,16},{28,20},{9,1},{13,5},{17,9},{2... | collective-permute-start | bytes 221192 | tf_op jit(solution)/shard_map/ppermute | solution.py:493
  283.9 196.7 %reduce-scatter.5.cloned.1.call-start = ((), (), s32[]{:S(2)}) async-start(), calls=%async_computation.3 | async-start | bytes 4718592 | tf_op jit(solution)/shard_map/reduce_scatter | solution.py:680
  295.2 28.6 %collective-permute-start.49 = (bf16[2,18,1024]{2,1,0:T(8,128)(2,1)S(1)}, bf16[2,18,1024]{2,1,0:T(8,128)(2,1)S(1)}, u32[]{:S(2)}, u32[]{:S(2)}) collective-permute-start(bf16[2,18,1024]{2,1,0:T(8,128)(2,1)S(1)} %pad_maximum_fusion.14), channel_id=1, source_target_pairs={{0,4},{4,0},{8,12},{12,8},{16,20},{20,16},{24,28},{28,24},{1,5},{5... | collective-permute-start | bytes 221192 | tf_op jit(solution)/shard_map/ppermute | solution.py:589
  324.0 38.4 %collective-permute-start.52 = (bf16[2,18,1024]{2,1,0:T(8,128)(2,1)S(1)}, bf16[2,18,1024]{2,1,0:T(8,128)(2,1)S(1)}, u32[]{:S(2)}, u32[]{:S(2)}) collective-permute-start(bf16[2,18,1024]{2,1,0:T(8,128)(2,1)S(1)} %pad_maximum_fusion.25), channel_id=1, source_target_pairs={{24,0},{28,4},{25,1},{29,5},{26,2},{30,6},{27,3},{31,7}} | collective-permute-start | bytes 221192 | tf_op jit(solution)/shard_map/ppermute | solution.py:493
  325.6 36.9 %collective-permute-start.51 = (bf16[2,18,1024]{2,1,0:T(8,128)(2,1)S(1)}, bf16[2,18,1024]{2,1,0:T(8,128)(2,1)S(1)}, u32[]{:S(2)}, u32[]{:S(2)}) collective-permute-start(bf16[2,18,1024]{2,1,0:T(8,128)(2,1)S(1)} %pad_maximum_fusion.25), channel_id=1, source_target_pairs={{16,0},{20,4},{24,8},{28,12},{17,1},{21,5},{25,9},{29,13},{18,2},{... | collective-permute-start | bytes 221192 | tf_op jit(solution)/shard_map/ppermute | solution.py:493
  326.9 35.6 %collective-permute-start.50 = (bf16[2,18,1024]{2,1,0:T(8,128)(2,1)S(1)}, bf16[2,18,1024]{2,1,0:T(8,128)(2,1)S(1)}, u32[]{:S(2)}, u32[]{:S(2)}) collective-permute-start(bf16[2,18,1024]{2,1,0:T(8,128)(2,1)S(1)} %pad_maximum_fusion.25), channel_id=1, source_target_pairs={{8,0},{12,4},{16,8},{20,12},{24,16},{28,20},{9,1},{13,5},{17,9},{2... | collective-permute-start | bytes 221192 | tf_op jit(solution)/shard_map/ppermute | solution.py:493
  485.4 16.8 %collective-permute-start.55 = (bf16[304,512]{1,0:T(8,128)(2,1)S(1)}, bf16[304,512]{1,0:T(8,128)(2,1)S(1)}, u32[]{:S(2)}, u32[]{:S(2)}) collective-permute-start(bf16[304,512]{1,0:T(8,128)(2,1)S(1)} %pad_maximum_fusion.8), channel_id=1, source_target_pairs={{0,8},{8,16},{16,24},{24,28},{28,20},{20,12},{12,4},{4,0},{1,9},{9... | collective-permute-start | bytes 933896 | tf_op jit(solution)/shard_map/ppermute | solution.py:639
  487.2 15.0 %collective-permute-start.56 = (bf16[304,512]{1,0:T(8,128)(2,1)S(1)}, bf16[304,512]{1,0:T(8,128)(2,1)S(1)}, u32[]{:S(2)}, u32[]{:S(2)}) collective-permute-start(bf16[304,512]{1,0:T(8,128)(2,1)S(1)} %pad_maximum_fusion.9), channel_id=1, source_target_pairs={{0,4},{8,0},{16,8},{24,16},{28,24},{20,28},{12,20},{4,12},{1,5},{9... | collective-permute-start | bytes 933896 | tf_op jit(solution)/shard_map/ppermute | solution.py:639
  504.4 18.7 %collective-permute-start.63 = (bf16[304,512]{1,0:T(8,128)(2,1)S(1)}, bf16[304,512]{1,0:T(8,128)(2,1)S(1)}, u32[]{:S(2)}, u32[]{:S(2)}) collective-permute-start(bf16[304,512]{1,0:T(8,128)(2,1)S(1)} %add_convert_fusion.15), channel_id=1, source_target_pairs={{0,4},{8,0},{16,8},{24,16},{28,24},{20,28},{12,20},{4,12},{1,5},{9... | collective-permute-start | bytes 933896 | tf_op jit(solution)/shard_map/ppermute | solution.py:639
  504.9 18.3 %collective-permute-start.62 = (bf16[304,512]{1,0:T(8,128)(2,1)S(1)}, bf16[304,512]{1,0:T(8,128)(2,1)S(1)}, u32[]{:S(2)}, u32[]{:S(2)}) collective-permute-start(bf16[304,512]{1,0:T(8,128)(2,1)S(1)} %add_convert_fusion.16), channel_id=1, source_target_pairs={{0,8},{8,16},{16,24},{24,28},{28,20},{20,12},{12,4},{4,0},{1,9},{9... | collective-permute-start | bytes 933896 | tf_op jit(solution)/shard_map/ppermute | solution.py:639
  506.7 16.4 %collective-permute-start.67 = (bf16[256,512]{1,0:T(8,128)(2,1)S(1)}, bf16[256,512]{1,0:T(8,128)(2,1)S(1)}, u32[]{:S(2)}, u32[]{:S(2)}) collective-permute-start(bf16[256,512]{1,0:T(8,128)(2,1)S(1)} %get-tuple-element.481.refs_8_), channel_id=1, source_target_pairs={{0,4},{8,0},{16,8},{24,16},{28,24},{20,28},{12,20},{4,12},{1,5},{9... | collective-permute-start | bytes 786440 | tf_op jit(solution)/shard_map/ppermute | solution.py:639
  577.4 24.1 %collective-permute-start.93 = (bf16[256,2048]{1,0:T(8,128)(2,1)S(1)}, bf16[256,2048]{1,0:T(8,128)(2,1)S(1)}, u32[]{:S(2)}, u32[]{:S(2)}) collective-permute-start(bf16[256,2048]{1,0:T(8,128)(2,1)S(1)} %fusion.23), channel_id=1, source_target_pairs={{0,1},{1,0},{2,3},{3,2},{4,5},{5,4},{6,7},{7,6},{8,9},{9,8},{10,11... | collective-permute-start | bytes 3145736 | tf_op jit(solution)/shard_map/ppermute | solution.py:486
  577.4 24.1 %collective-permute-start.94 = (bf16[256,2048]{1,0:T(8,128)(2,1)S(1)}, bf16[256,2048]{1,0:T(8,128)(2,1)S(1)}, u32[]{:S(2)}, u32[]{:S(2)}) collective-permute-start(bf16[256,2048]{1,0:T(8,128)(2,1)S(1)} %fusion.24), channel_id=1, source_target_pairs={{0,1},{1,0},{2,3},{3,2},{4,5},{5,4},{6,7},{7,6},{8,9},{9,8},{10,11... | collective-permute-start | bytes 3145736 | tf_op jit(solution)/shard_map/ppermute | solution.py:486
  605.7 16.0 %collective-permute-start.96 = (bf16[304,512]{1,0:T(8,128)(2,1)S(1)}, bf16[304,512]{1,0:T(8,128)(2,1)S(1)}, u32[]{:S(2)}, u32[]{:S(2)}) collective-permute-start(bf16[304,512]{1,0:T(8,128)(2,1)S(1)} %add_convert_fusion.5), channel_id=1, source_target_pairs={{0,4},{8,0},{16,8},{24,16},{28,24},{20,28},{12,20},{4,12},{1,5},{9... | collective-permute-start | bytes 933896 | tf_op jit(solution)/shard_map/ppermute | solution.py:639
  613.8 49.1 %collective-permute-start.113 = (bf16[256,2048]{1,0:T(8,128)(2,1)}, bf16[256,2048]{1,0:T(8,128)(2,1)}, u32[]{:S(2)}, u32[]{:S(2)}) collective-permute-start(bf16[256,2048]{1,0:T(8,128)(2,1)} %add_convert_fusion), channel_id=1, source_target_pairs={{0,2},{1,3},{2,0},{3,1},{4,6},{5,7},{6,4},{7,5},{8,10},{9,11},{10,... | collective-permute-start | bytes 3145736 | tf_op jit(solution)/shard_map/ppermute | solution.py:486
  624.1 14.9 %collective-permute-start.103 = (bf16[64,512]{1,0:T(8,128)(2,1)S(1)}, bf16[64,512]{1,0:T(8,128)(2,1)S(1)}, u32[]{:S(2)}, u32[]{:S(2)}) collective-permute-start(bf16[64,512]{1,0:T(8,128)(2,1)S(1)} %get-tuple-element.514), channel_id=1, source_target_pairs={{0,3},{1,2},{2,1},{3,0},{4,7},{5,6},{6,5},{7,4},{8,11},{9,10},{10,... | collective-permute-start | bytes 196616 | tf_op jit(solution)/shard_map/ppermute | solution.py:486
  (251 other events, 2964.8 us)
Sparse Core Ops, SparseCore 0:
  284.0 90.7 reduce-scatter.2
  390.0 90.5 reduce-scatter.4

commit v3 on v2

--- a/solution.py
+++ b/solution.py
@@ -859,10 +859,13 @@
     back_far = back_far.result()
     z_shares, back_far = lax.optimization_barrier((z_shares, back_far))
     pair_far = (step, act, g_mixed_far, bc, rate, skip, starts_far, back_far, tokens)
+    out_own, z_shares, *one = lax.optimization_barrier((out_own, z_shares, *one))
+    z_own = reduced(z_shares)
+    early = [Ring(None, None, [way(out_own, d) for d in range(2)])] if by_steps else []
     two = b2(2, 1, one[:2], *pair_far)
-    out_own, *two = lax.optimization_barrier((out_own, *two))
-    z_own = reduced(tied(z_shares, out_own))
+    two = advance(early, *two)
     three = b2(3, 1, two[:2], *pair_far)
+    three = advance(early, *three)
     far = [*three[:2], *[jnp.concatenate([v, w]) for v, w in zip(two[2:], three[2:])]]
     near = [jnp.concatenate([v, w]) for v, w in zip(zero[2:], one[2:])]
     g_pre, g_act_part = far[:2]
@@ -873,6 +876,7 @@
     g_proj = sum_all(
         jnp.concatenate([g_dt_low, g_b, g_c], axis=0)
     ).astype(BF16)
+    g_proj = advance(early, g_proj)
     g_act = g_act_part + product(g_proj, x_weight, ROWS_FIRST)
     g_conv = (g_act * silu_slope(conv_out)).reshape(seqs, tokens, inner)
     g_padded = jnp.pad(g_conv, ((0, 0), (HALO, taps - 1), (0, 0)))
@@ -901,7 +905,7 @@
     if by_steps:
         x_shares = in_shares(g_x_all, normed_all)
         small_shares = small.astype(BF16).reshape(seq_count, -1, inner)
-        z_own, x_shares, small_shares, g_x = lax.optimization_barrier((z_own, x_shares, small_shares, g_x))
+        z_own, x_shares, small_shares, g_x = advance(early, z_own, x_shares, small_shares, g_x)
         large = width // seq_count
         chunk_of = in_chunk(x_shares)
 
@@ -912,7 +916,7 @@
             return [jnp.concatenate([x, v[large:]], axis=0) for x, v in zip(in_between([v[:large] for v in own]), own)]
 
         x_ring = Ring(x_chunk, x_between)
-        out_ring = Ring(None, None, [way(out_own, d) for d in range(2)])
+        out_ring = early[0]
         z_row = crossed_blocks(z_own.reshape(seqs, -1, inner)).reshape(-1, inner)
         rings = [x_ring, out_ring]
         z_row, g_x = advance(rings, z_row, g_x)
@@ -935,25 +939,31 @@
     g_x = advanced((g_x[:, HALO:] + fixed).reshape(rows, inner))
     normed_1 += to_normed(g_x, x_columns, 1)
     normed_3 += to_normed(g_x, x_columns, 3)
-    normed_1, normed_3 = advanced(normed_1.astype(BF16), normed_3.astype(BF16))
+    ready = ()
+    if by_steps:
+        where = jnp.stack([me] + ring_order()).astype(jnp.int32)
+        out_is = partial(settle, where, out_ring.result(), out_weight.shape, 1, width)
+        ready = (out_is(part=0)[0],)
+    normed_1, normed_3, *ready = advanced(normed_1.astype(BF16), normed_3.astype(BF16), *ready)
     got1, got3 = swap((normed_1, normed_3), 1)
-    got1, got3, normed_2 = advanced(got1, got3, normed_2 + to_normed(g_x, x_columns, 2))
-    other = swap((normed_2 + got3.astype(F32)).astype(BF16), 2)
+    if by_steps:
+        ready = (out_is(part=1, filled=ready[0])[0],)
+    got1, got3, normed_2, *ready = advanced(got1, got3, normed_2 + to_normed(g_x, x_columns, 2), *ready)
     normed_0 = advanced(to_normed(g_z, z_columns, 0))
+    other = swap(tied((normed_2 + got3.astype(F32)).astype(BF16), normed_0), 2)
     normed_0 = advanced(normed_0 + to_normed(g_x, x_columns, 0) + got1.astype(F32))
     if by_steps:
-        other = advanced(other)
+        (out_owned,) = ready
+        z_is = partial(settle, where, z_ring.result(), in_weight.shape, seqs, inner, half=1)
+        assert out_ring.done() and z_ring.done()
+        in_owned = advanced(z_is(part=0)[0])
+        other, in_owned = advanced(other, z_is(part=1, filled=in_owned)[0])
     g_normed = normed_0 + other.astype(F32)
     gain_part = jnp.sum(g_normed * rows_in * scale, axis=0)
     tail = jnp.concatenate([gain_part, jnp.full((128,), loss_part)])
     if by_steps:
-        where = jnp.stack([me] + ring_order()).astype(jnp.int32)
-        out_is = partial(settle, where, out_ring.result(), out_weight.shape, 1, width)
-        z_is = partial(settle, where, z_ring.result(), in_weight.shape, seqs, inner, half=1)
-        assert out_ring.done() and z_ring.done()
-        tail, out_owned = advanced(tail + seq_xor(tail, 1), out_is(part=0)[0])
-        tail, out_owned = advanced(tail + seq_xor(tail, 2), out_is(part=1, filled=out_owned)[0])
-        tail, in_owned = advanced(tail + seq_xor(tail, 4), z_is(part=0)[0])
+        for bit in (1, 2, 4):
+            tail = advanced(tail + seq_xor(tail, bit))
     else:
         tail = lax.psum(tail, "seq")
     gain_share = slots(tail[:width].reshape(seqs, -1))
@@ -961,7 +971,7 @@
     loss_sum = tail[width:] + swap(tail[width:], 1)
     loss = (loss_sum + swap(loss_sum, 2))[0] / (width * count)
     if by_steps:
-        gain_grad, loss, in_owned = advanced(gain_grad, loss, z_is(part=1, filled=in_owned)[0])
+        gain_grad, loss, in_owned = advanced(gain_grad, loss, in_owned)
         while not x_ring.done():
             in_owned = advanced(in_owned)
         in_owned, small = settle(

time: 748 us -> 718 us (0.960)
  waiting for transfers between devices: 194 us -> 142 us
  matrix products: 79.3 us -> 93 us
  local copies, waits for them, and re-layouts: 29.9 us -> 39.2 us
  starting transfers between devices: 140 us -> 132 us
    ppermute x56, waiting for transfers between devices: 94.3 us -> 53.4 us  [send(): self.moving.append(lax.ppermute(held[d], 'seq', route))]
    dot_general x23, matrix products: 79.3 us -> 93 us  [product(): return lax.dot_general(left, right, dims, preferred_element_type=F32)]
    ppermute x39, waiting for transfers between devices: 63.6 us -> 51.2 us  [swap(): lax.ppermute(a, 'wsh', [(i, i ^ bit) for i in range(lax.axis_size('wsh'))])]
    ppermute x23, waiting for transfers between devices: 15.5 us -> 26.1 us  [seq_xor(): lax.ppermute(v, 'seq', [(i, i ^ bits) for i in range(lax.axis_size('seq'))])]
    reduce_scatter x2, waiting for transfers between devices: 19.8 us -> 11.5 us  [reduced(): return lax.psum_scatter(rows, 'seq', scatter_dimension=0, tiled=True)]
  transfers between devices with their start and end apart: 134 -> 134, of which waited for: 63 -> 55; matrix products, arithmetic and copies ran while one was open for 17% -> 21% of each run, Pallas kernels for 29% -> 30%
where the time goes in v3:
time: 718 us; the launch traced here: 710 us
  Pallas kernels  224 us (31%)
  waiting for transfers between devices  142 us (20%)
  starting transfers between devices  132 us (18%)
  matrix products  93 us (13%)
  other arithmetic  59.5 us (8%)
  local copies, waits for them, and re-layouts  39.2 us (5%)
  between operations  20.2 us (3%)
    pallas_call x4, Pallas kernels, b2(): pl.pallas_call(partial(b2_kernel, eb=eb, n=n), grid=(count,), in_specs=[b...  107 us
    dot_general x23, matrix products, product(): return lax.dot_general(left, right, dims, preferred_element_type=F32)  93 us
    ppermute x56, starting transfers between devices, send(): self.moving.append(lax.ppermute(held[d], 'seq', route))  56.4 us
    ppermute x56, waiting for transfers between devices, send(): self.moving.append(lax.ppermute(held[d], 'seq', route))  53.4 us
    ppermute x39, waiting for transfers between devices, swap(): lax.ppermute(a, 'wsh', [(i, i ^ bit) for i in range(lax.axis_size('wsh'))])  51.2 us
    pallas_call x2, Pallas kernels, p2(): pl.pallas_call(partial(p2_kernel, eb=eb, n=n), grid=(2,), in_specs=[blk,...  34.9 us
    pallas_call x5, Pallas kernels, settle(): pl.pallas_call(partial(settle_kernel, steps=steps, base=base, blocks=bloc...  30.4 us
    ppermute x23, starting transfers between devices, seq_xor(): lax.ppermute(v, 'seq', [(i, i ^ bits) for i in range(lax.axis_size('seq'))])  27.7 us
  transfers between devices with their start and end apart: 134, of which 55 were waited for; matrix products, arithmetic and copies ran while one was open for 21% of the time, Pallas kernels for 30%

profile of v3, /device:TPU:0, one launch (start us, length us, event | category | flops | bytes accessed | tf_op | source)
XLA Modules:
  0.0 710.5 jit_solution(3808484098207504911)
XLA Ops:
  23.1 6.7 collective-permute-done.5.refs_3_
  29.9 5.7 collective-permute-done.4.refs_2_
  41.1 5.4 collective-permute-done.13.refs_5_
  71.4 7.7 %fusion.17 = f32[4,272,1024]{2,1,0:T(8,128)S(1)} fusion(bf16[2048,1024]{1,0:T(8,128)(2,1)} %shard_map.237, bf16[1,272,2048]{2,1,0:T(8,128)(2,1)} %bitcast.10, bf16[1,272,2048]{2,1,0:T(8,128)(2,1)S(1)} %bitcast.291, bf16[1,272,2048]{2,1,0:T(8,128)(2,1)} %bitcast.8, bf16[1,272,2048]{2,1,0:T(8,128)(2,1)S(1)} %bitcast.282), kind=kOutput, calls=%fused_computation.27 | convolution fusion | flops 4570087424 | bytes 13107200 | tf_op jit(solution)/shard_map/dot_general | solution.py:25
  94.6 6.9 collective-permute-done.21
  110.8 9.9 %shard_map.238 = (f32[2,16,1024]{2,1,0:T(8,128)}, f32[2,1,1024]{2,1,0:T(1,128)}) custom-call(f32[1024,1024]{1,0:T(8,128)} %compare_select_fusion.step_ref, bf16[1024,1024]{1,0:T(8,128)(2,1)} %copy-done.6, f32[32,1024]{1,0:T(8,128)} %slice_convert_fusion.2.bc_ref, f32[16,1024]{1,0:T(8,128)} %fusion.77.rate_ref), custom_call_target="tpu_custom_call" | custom-call | flops 8999999488 | tf_op jit(solution)/shard_map/pallas_call | solution.py:98
  129.3 9.9 %shard_map.239 = (f32[2,16,1024]{2,1,0:T(8,128)}, f32[2,1,1024]{2,1,0:T(1,128)}) custom-call(f32[1024,1024]{1,0:T(8,128)} %compare_select_fusion.step_ref, bf16[1024,1024]{1,0:T(8,128)(2,1)} %copy-done.6, f32[32,1024]{1,0:T(8,128)} %slice_convert_fusion.2.bc_ref, f32[16,1024]{1,0:T(8,128)} %fusion.77.rate_ref), custom_call_target="tpu_custom_call" | custom-call | flops 8999999488 | tf_op jit(solution)/shard_map/pallas_call | solution.py:98
  155.8 8.3 %fusion.101.z_ref = f32[1024,1024]{1,0:T(8,128)} fusion(bf16[1024,2048]{1,0:T(8,128)(2,1)S(1)} %bitcast.285, bf16[2048,1024]{1,0:T(8,128)(2,1)} %shard_map.240), kind=kOutput, calls=%fused_computation.316 | convolution fusion | flops 4294967296 | bytes 12582912 | tf_op jit(solution)/shard_map/dot_general | solution.py:25
  169.1 17.6 %shard_map.241 = (f32[512,1024]{1,0:T(8,128)}, bf16[512,1024]{1,0:T(8,128)(2,1)}, f32[2,8,16,1024]{3,2,1,0:T(8,128)}) custom-call(f32[1024,1024]{1,0:T(8,128)} %compare_select_fusion.step_ref, bf16[1024,1024]{1,0:T(8,128)(2,1)} %copy-done.6, f32[1024,1024]{1,0:T(8,128)} %fusion.101.z_ref, f32[32,1024]{1,0:T(8,128)} %slice_convert_fusion.2.bc_ref, ...), custom_call_target="tpu_custom_call" | custom-call | flops 16000000000 | tf_op jit(solution)/shard_map/pallas_call | solution.py:158
  195.2 17.3 %shard_map.242 = (f32[512,1024]{1,0:T(8,128)}, bf16[512,1024]{1,0:T(8,128)(2,1)}, f32[2,8,16,1024]{3,2,1,0:T(8,128)}) custom-call(f32[1024,1024]{1,0:T(8,128)} %compare_select_fusion.step_ref, bf16[1024,1024]{1,0:T(8,128)(2,1)} %copy-done.6, f32[1024,1024]{1,0:T(8,128)} %fusion.101.z_ref, f32[32,1024]{1,0:T(8,128)} %slice_convert_fusion.2.bc_ref, ...), custom_call_target="tpu_custom_call" | custom-call | flops 16000000000 | tf_op jit(solution)/shard_map/pallas_call | solution.py:158
  212.4 6.4 collective-permute-done.40
  241.6 10.6 %shard_map.243 = f32[2,16,1024]{2,1,0:T(8,128)} custom-call(f32[1024,1024]{1,0:T(8,128)} %compare_select_fusion.step_ref, f32[512,1024]{1,0:T(8,128)} %get-tuple-element.476.dy_ref, f32[32,1024]{1,0:T(8,128)} %slice_convert_fusion.2.bc_ref, f32[16,1024]{1,0:T(8,128)} %fusion.77.rate_ref), custom_call_target="tpu_custom_call" | custom-call | flops 8999999488 | tf_op jit(solution)/shard_map/pallas_call | solution.py:201
  252.2 7.7 %collective-permute-done.43 = bf16[256,2048]{1,0:T(8,128)(2,1)} collective-permute-done((bf16[256,2048]{1,0:T(8,128)(2,1)S(1)}, bf16[256,2048]{1,0:T(8,128)(2,1)}, u32[]{:S(2)}, u32[]{:S(2)}) %collective-permute-start.43) | collective-permute-done | bytes 1048608 | tf_op jit(solution)/shard_map/ppermute | solution.py:486
  262.9 8.7 %multiply_convert_fusion.1 = (bf16[512,1024]{1,0:T(8,128)(2,1)}, f32[512,1024]{1,0:T(8,128)}) fusion(f32[512,1024]{1,0:T(8,128)} %get-tuple-element.279, f32[1024,1024]{1,0:T(8,128)} %fusion.101.z_ref, bf16[1024,2048]{1,0:T(8,128)(2,1)} %param.27, bf16[256,2048]{1,0:T(8,128)(2,1)} %collective-permute-done.44, bf16[256,2048]{1,0:T(8,128)(2,1)} %collective-permute-done.43), kind=kOutput, calls=%fused_computation.85 | convolution fusion | flops 2157969408 | bytes 13631488 | tf_op jit(solution)/shard_map/dot_general | solution.py:25
  275.8 8.2 %fusion.19 = bf16[1024,2048]{1,0:T(8,128)(2,1)} fusion(bf16[256,2048]{1,0:T(8,128)(2,1)} %collective-permute-done.44, bf16[256,2048]{1,0:T(8,128)(2,1)} %collective-permute-done.43, bf16[256,2048]{1,0:T(8,128)(2,1)S(1)} %copy-done.141, bf16[256,2048]{1,0:T(8,128)(2,1)S(1)} %copy-done.68, bf16[512,1024]{1,0:T(8,128)(2,1)S(1)} %copy-done.165, ...), kind=kOutput, calls=%fused_computation.39 | convolution fusion | flops 4318035968 | bytes 10485760 | tf_op jit(solution)/shard_map/dot_general | solution.py:25
  284.0 10.2 %shard_map.244 = f32[2,16,1024]{2,1,0:T(8,128)} custom-call(f32[1024,1024]{1,0:T(8,128)} %compare_select_fusion.step_ref, f32[512,1024]{1,0:T(8,128)} %get-tuple-element.282.dy_ref, f32[32,1024]{1,0:T(8,128)} %slice_convert_fusion.2.bc_ref, f32[16,1024]{1,0:T(8,128)} %fusion.77.rate_ref), custom_call_target="tpu_custom_call" | custom-call | flops 8999999488 | tf_op jit(solution)/shard_map/pallas_call | solution.py:201
  297.3 26.5 %shard_map.245 = (bf16[1024,1024]{1,0:T(8,128)(2,1)}, f32[1024,1024]{1,0:T(8,128)}, f32[1,32,128]{2,1,0:T(8,128)}, f32[1,32,128]{2,1,0:T(8,128)}, f32[1,16,1024]{2,1,0:T(8,128)}, /*index=5*/f32[1,2,8,1024]{3,2,1,0:T(8,128)}) custom-call(f32[1024,1024]{1,0:T(8,128)} %compare_select_fusion.step_ref, bf16[1024,1024]{1,0:T(8,128)(2,1)} %copy-done.6, ...), custom_call_target="tpu_custom_call" | custom-call | flops 24999999488 | tf_op jit(solution)/shard_map/pallas_call | solution.py:319
  328.2 27.0 %shard_map.246 = (bf16[1024,1024]{1,0:T(8,128)(2,1)}, f32[1024,1024]{1,0:T(8,128)}, f32[1,32,128]{2,1,0:T(8,128)}, f32[1,32,128]{2,1,0:T(8,128)}, f32[1,16,1024]{2,1,0:T(8,128)}, /*index=5*/f32[1,2,8,1024]{3,2,1,0:T(8,128)}) custom-call(f32[1024,1024]{1,0:T(8,128)} %compare_select_fusion.step_ref, ...), custom_call_target="tpu_custom_call", output_to_operand_aliasing={{0}: (8, {}), {1}: (9, {})} | custom-call | flops 24999999488 | tf_op jit(solution)/shard_map/pallas_call | solution.py:319
  363.3 11.5 %reduce-scatter.3.cloned.1.call-done = bf16[128,2048]{1,0:T(8,128)(2,1)} async-done(((bf16[1024,2048]{1,0:T(8,128)(2,1)}), bf16[128,2048]{1,0:T(8,128)(2,1)}) %reduce-scatter.3.cloned.1.call-update) | async-done | bytes 524304 | tf_op jit(solution)/shard_map/reduce_scatter | solution.py:680
  378.0 26.5 %shard_map.247 = (bf16[1024,1024]{1,0:T(8,128)(2,1)}, f32[1024,1024]{1,0:T(8,128)}, f32[1,32,128]{2,1,0:T(8,128)}, f32[1,32,128]{2,1,0:T(8,128)}, f32[1,16,1024]{2,1,0:T(8,128)}, /*index=5*/f32[1,2,8,1024]{3,2,1,0:T(8,128)}) custom-call(f32[1024,1024]{1,0:T(8,128)} %compare_select_fusion.step_ref, ...), custom_call_target="tpu_custom_call", output_to_operand_aliasing={{0}: (8, {}), {1}: (9, {})} | custom-call | flops 24999999488 | tf_op jit(solution)/shard_map/pallas_call | solution.py:319
  406.7 26.6 %shard_map.248 = (bf16[1024,1024]{1,0:T(8,128)(2,1)}, f32[1024,1024]{1,0:T(8,128)}, f32[1,32,128]{2,1,0:T(8,128)}, f32[1,32,128]{2,1,0:T(8,128)}, f32[1,16,1024]{2,1,0:T(8,128)}, /*index=5*/f32[1,2,8,1024]{3,2,1,0:T(8,128)}) custom-call(f32[1024,1024]{1,0:T(8,128)} %compare_select_fusion.step_ref, ...), custom_call_target="tpu_custom_call", output_to_operand_aliasing={{0}: (8, {}), {1}: (9, {})} | custom-call | flops 24999999488 | tf_op jit(solution)/shard_map/pallas_call | solution.py:319
  468.4 9.3 %bitcast_convert_fusion = bf16[2048,1024]{1,0:T(8,128)(2,1)} fusion(bf16[4,272,1024]{2,1,0:T(8,128)(2,1)S(1)} %multiply_convert_fusion, bf16[1,272,2048]{2,1,0:T(8,128)(2,1)} %bitcast.10, bf16[1,272,2048]{2,1,0:T(8,128)(2,1)S(1)} %bitcast.293, bf16[1,272,2048]{2,1,0:T(8,128)(2,1)} %bitcast.8, bf16[1,272,2048]{2,1,0:T(8,128)(2,1)S(1)} %bitcast.284), kind=kOutput, calls=%fused_computation.1 | convolution fusion | flops 4572184576 | bytes 10878976 | tf_op jit(solution)/shard_map/dot_general | solution.py:25
  498.8 7.3 %collective-permute-done.65.refs_5_ = bf16[128,1024]{1,0:T(8,128)(2,1)} collective-permute-done((bf16[128,1024]{1,0:T(8,128)(2,1)}, bf16[128,1024]{1,0:T(8,128)(2,1)}, u32[]{:S(2)}, u32[]{:S(2)}) %collective-permute-start.65) | collective-permute-done | bytes 262176 | tf_op jit(solution)/shard_map/ppermute | solution.py:639
  555.6 5.6 shard_map.249.refs_16_
  588.3 5.4 shard_map.250
  625.1 5.5 collective-permute-done.108.refs_9_
  632.6 5.6 shard_map.251.refs_16_
  641.7 5.5 shard_map.252.refs_16_
  659.5 6.9 collective-permute-done.121
  671.7 5.1 collective-permute-done.124
  683.5 5.3 fusion.51
  691.3 8.3 %shard_map.253 = (f32[512,8192]{1,0:T(8,128)}, f32[384,1024]{1,0:T(8,128)}) custom-call(s32[17]{0:T(128)} %stack.183.at_ref, bf16[304,512]{1,0:T(8,128)(2,1)} %copy-done.76, bf16[304,512]{1,0:T(8,128)(2,1)} %collective-permute-done.104.refs_1_, bf16[304,512]{1,0:T(8,128)(2,1)} %copy-done.143, ...), custom_call_target="tpu_custom_call", output_to_operand_aliasing={{0}: (17, {})} | custom-call | flops 7000000000 | tf_op jit(solution)/shard_map/pallas_call | solution.py:393
  (822 shorter events, 355.1 us)
Async XLA Ops:
  7.2 367.6 %reduce-scatter.3.cloned.1.call-start = ((), (), s32[]{:S(2)}) async-start(), calls=%async_computation.2 | async-start | bytes 4718592 | tf_op jit(solution)/shard_map/reduce_scatter | solution.py:680
  35.6 26.5 %collective-permute-start.6 = (bf16[272,2048]{1,0:T(8,128)(2,1)S(1)}, bf16[272,2048]{1,0:T(8,128)(2,1)S(1)}, u32[]{:S(2)}, u32[]{:S(2)}) collective-permute-start(bf16[272,2048]{1,0:T(8,128)(2,1)S(1)} %pad_maximum_fusion.3), channel_id=1, source_target_pairs={{0,2},{1,3},{2,0},{3,1},{4,6},{5,7},{6,4},{7,5},{8,10},{9,11},{10,... | collective-permute-start | bytes 3342344 | tf_op jit(solution)/shard_map/ppermute | solution.py:486
  64.9 19.3 %collective-permute-start.16 = (bf16[128,1024]{1,0:T(8,128)(2,1)S(1)}, bf16[128,1024]{1,0:T(8,128)(2,1)S(1)}, u32[]{:S(2)}, u32[]{:S(2)}) collective-permute-start(bf16[128,1024]{1,0:T(8,128)(2,1)S(1)} %get-tuple-element.471), channel_id=1, source_target_pairs={{0,3},{1,2},{2,1},{3,0},{4,7},{5,6},{6,5},{7,4},{8,11},{9,10},{10,... | collective-permute-start | bytes 786440 | tf_op jit(solution)/shard_map/ppermute | solution.py:486
  66.4 17.8 %collective-permute-start.15 = (bf16[128,1024]{1,0:T(8,128)(2,1)S(1)}, bf16[128,1024]{1,0:T(8,128)(2,1)S(1)}, u32[]{:S(2)}, u32[]{:S(2)}) collective-permute-start(bf16[128,1024]{1,0:T(8,128)(2,1)S(1)} %get-tuple-element.472), channel_id=1, source_target_pairs={{0,2},{1,3},{2,0},{3,1},{4,6},{5,7},{6,4},{7,5},{8,10},{9,11},{10,... | collective-permute-start | bytes 786440 | tf_op jit(solution)/shard_map/ppermute | solution.py:486
  139.6 24.6 %collective-permute-start.34 = (bf16[2,18,1024]{2,1,0:T(8,128)(2,1)S(1)}, bf16[2,18,1024]{2,1,0:T(8,128)(2,1)S(1)}, u32[]{:S(2)}, u32[]{:S(2)}) collective-permute-start(bf16[2,18,1024]{2,1,0:T(8,128)(2,1)S(1)} %pad_maximum_fusion.22), channel_id=1, source_target_pairs={{0,24},{4,28},{1,25},{5,29},{2,26},{6,30},{3,27},{7,31}} | collective-permute-start | bytes 221192 | tf_op jit(solution)/shard_map/ppermute | solution.py:493
  144.0 20.2 %collective-permute-start.33 = (bf16[2,18,1024]{2,1,0:T(8,128)(2,1)S(1)}, bf16[2,18,1024]{2,1,0:T(8,128)(2,1)S(1)}, u32[]{:S(2)}, u32[]{:S(2)}) collective-permute-start(bf16[2,18,1024]{2,1,0:T(8,128)(2,1)S(1)} %pad_maximum_fusion.22), channel_id=1, source_target_pairs={{0,16},{4,20},{8,24},{12,28},{1,17},{5,21},{9,25},{13,29},{2,18},{... | collective-permute-start | bytes 221192 | tf_op jit(solution)/shard_map/ppermute | solution.py:493
  145.3 18.9 %collective-permute-start.32 = (bf16[2,18,1024]{2,1,0:T(8,128)(2,1)S(1)}, bf16[2,18,1024]{2,1,0:T(8,128)(2,1)S(1)}, u32[]{:S(2)}, u32[]{:S(2)}) collective-permute-start(bf16[2,18,1024]{2,1,0:T(8,128)(2,1)S(1)} %pad_maximum_fusion.22), channel_id=1, source_target_pairs={{0,8},{4,12},{8,16},{12,20},{16,24},{20,28},{1,9},{5,13},{9,17},{1... | collective-permute-start | bytes 221192 | tf_op jit(solution)/shard_map/ppermute | solution.py:493
  165.2 21.6 %collective-permute-start.38 = (bf16[2,18,1024]{2,1,0:T(8,128)(2,1)S(1)}, bf16[2,18,1024]{2,1,0:T(8,128)(2,1)S(1)}, u32[]{:S(2)}, u32[]{:S(2)}) collective-permute-start(bf16[2,18,1024]{2,1,0:T(8,128)(2,1)S(1)} %pad_maximum_fusion.23), channel_id=1, source_target_pairs={{0,24},{4,28},{1,25},{5,29},{2,26},{6,30},{3,27},{7,31}} | collective-permute-start | bytes 221192 | tf_op jit(solution)/shard_map/ppermute | solution.py:493
  166.5 20.3 %collective-permute-start.37 = (bf16[2,18,1024]{2,1,0:T(8,128)(2,1)S(1)}, bf16[2,18,1024]{2,1,0:T(8,128)(2,1)S(1)}, u32[]{:S(2)}, u32[]{:S(2)}) collective-permute-start(bf16[2,18,1024]{2,1,0:T(8,128)(2,1)S(1)} %pad_maximum_fusion.23), channel_id=1, source_target_pairs={{0,16},{4,20},{8,24},{12,28},{1,17},{5,21},{9,25},{13,29},{2,18},{... | collective-permute-start | bytes 221192 | tf_op jit(solution)/shard_map/ppermute | solution.py:493
  167.8 19.0 %collective-permute-start.36 = (bf16[2,18,1024]{2,1,0:T(8,128)(2,1)S(1)}, bf16[2,18,1024]{2,1,0:T(8,128)(2,1)S(1)}, u32[]{:S(2)}, u32[]{:S(2)}) collective-permute-start(bf16[2,18,1024]{2,1,0:T(8,128)(2,1)S(1)} %pad_maximum_fusion.23), channel_id=1, source_target_pairs={{0,8},{4,12},{8,16},{12,20},{16,24},{20,28},{1,9},{5,13},{9,17},{1... | collective-permute-start | bytes 221192 | tf_op jit(solution)/shard_map/ppermute | solution.py:493
  193.6 25.3 %collective-permute-start.40 = (bf16[256,2048]{1,0:T(8,128)(2,1)S(1)}, bf16[256,2048]{1,0:T(8,128)(2,1)S(1)}, u32[]{:S(2)}, u32[]{:S(2)}) collective-permute-start(bf16[256,2048]{1,0:T(8,128)(2,1)S(1)} %fusion.39), channel_id=1, source_target_pairs={{0,2},{1,3},{2,0},{3,1},{4,6},{5,7},{6,4},{7,5},{8,10},{9,11},{10,... | collective-permute-start | bytes 3145736 | tf_op jit(solution)/shard_map/ppermute | solution.py:486
  234.4 25.5 %collective-permute-start.43 = (bf16[256,2048]{1,0:T(8,128)(2,1)S(1)}, bf16[256,2048]{1,0:T(8,128)(2,1)}, u32[]{:S(2)}, u32[]{:S(2)}) collective-permute-start(bf16[256,2048]{1,0:T(8,128)(2,1)S(1)} %fusion.66), channel_id=1, source_target_pairs={{0,2},{1,3},{2,0},{3,1},{4,6},{5,7},{6,4},{7,5},{8,10},{9,11},{10,... | collective-permute-start | bytes 3145736 | tf_op jit(solution)/shard_map/ppermute | solution.py:486
  271.8 22.7 %collective-permute-start.48 = (bf16[2,18,1024]{2,1,0:T(8,128)(2,1)S(1)}, bf16[2,18,1024]{2,1,0:T(8,128)(2,1)S(1)}, u32[]{:S(2)}, u32[]{:S(2)}) collective-permute-start(bf16[2,18,1024]{2,1,0:T(8,128)(2,1)S(1)} %pad_maximum_fusion.24), channel_id=1, source_target_pairs={{24,0},{28,4},{25,1},{29,5},{26,2},{30,6},{27,3},{31,7}} | collective-permute-start | bytes 221192 | tf_op jit(solution)/shard_map/ppermute | solution.py:493
  273.1 21.4 %collective-permute-start.47 = (bf16[2,18,1024]{2,1,0:T(8,128)(2,1)S(1)}, bf16[2,18,1024]{2,1,0:T(8,128)(2,1)S(1)}, u32[]{:S(2)}, u32[]{:S(2)}) collective-permute-start(bf16[2,18,1024]{2,1,0:T(8,128)(2,1)S(1)} %pad_maximum_fusion.24), channel_id=1, source_target_pairs={{16,0},{20,4},{24,8},{28,12},{17,1},{21,5},{25,9},{29,13},{18,2},{... | collective-permute-start | bytes 221192 | tf_op jit(solution)/shard_map/ppermute | solution.py:493
  274.4 20.1 %collective-permute-start.46 = (bf16[2,18,1024]{2,1,0:T(8,128)(2,1)S(1)}, bf16[2,18,1024]{2,1,0:T(8,128)(2,1)S(1)}, u32[]{:S(2)}, u32[]{:S(2)}) collective-permute-start(bf16[2,18,1024]{2,1,0:T(8,128)(2,1)S(1)} %pad_maximum_fusion.24), channel_id=1, source_target_pairs={{8,0},{12,4},{16,8},{20,12},{24,16},{28,20},{9,1},{13,5},{17,9},{2... | collective-permute-start | bytes 221192 | tf_op jit(solution)/shard_map/ppermute | solution.py:493
  284.0 199.0 %reduce-scatter.5.cloned.1.call-start = ((), (), s32[]{:S(2)}) async-start(), calls=%async_computation.3 | async-start | bytes 4718592 | tf_op jit(solution)/shard_map/reduce_scatter | solution.py:680
  295.3 28.6 %collective-permute-start.49 = (bf16[2,18,1024]{2,1,0:T(8,128)(2,1)S(1)}, bf16[2,18,1024]{2,1,0:T(8,128)(2,1)S(1)}, u32[]{:S(2)}, u32[]{:S(2)}) collective-permute-start(bf16[2,18,1024]{2,1,0:T(8,128)(2,1)S(1)} %pad_maximum_fusion.14), channel_id=1, source_target_pairs={{0,4},{4,0},{8,12},{12,8},{16,20},{20,16},{24,28},{28,24},{1,5},{5... | collective-permute-start | bytes 221192 | tf_op jit(solution)/shard_map/ppermute | solution.py:589
  324.0 38.4 %collective-permute-start.52 = (bf16[2,18,1024]{2,1,0:T(8,128)(2,1)S(1)}, bf16[2,18,1024]{2,1,0:T(8,128)(2,1)S(1)}, u32[]{:S(2)}, u32[]{:S(2)}) collective-permute-start(bf16[2,18,1024]{2,1,0:T(8,128)(2,1)S(1)} %pad_maximum_fusion.25), channel_id=1, source_target_pairs={{24,0},{28,4},{25,1},{29,5},{26,2},{30,6},{27,3},{31,7}} | collective-permute-start | bytes 221192 | tf_op jit(solution)/shard_map/ppermute | solution.py:493
  325.6 36.9 %collective-permute-start.51 = (bf16[2,18,1024]{2,1,0:T(8,128)(2,1)S(1)}, bf16[2,18,1024]{2,1,0:T(8,128)(2,1)S(1)}, u32[]{:S(2)}, u32[]{:S(2)}) collective-permute-start(bf16[2,18,1024]{2,1,0:T(8,128)(2,1)S(1)} %pad_maximum_fusion.25), channel_id=1, source_target_pairs={{16,0},{20,4},{24,8},{28,12},{17,1},{21,5},{25,9},{29,13},{18,2},{... | collective-permute-start | bytes 221192 | tf_op jit(solution)/shard_map/ppermute | solution.py:493
  326.9 35.6 %collective-permute-start.50 = (bf16[2,18,1024]{2,1,0:T(8,128)(2,1)S(1)}, bf16[2,18,1024]{2,1,0:T(8,128)(2,1)S(1)}, u32[]{:S(2)}, u32[]{:S(2)}) collective-permute-start(bf16[2,18,1024]{2,1,0:T(8,128)(2,1)S(1)} %pad_maximum_fusion.25), channel_id=1, source_target_pairs={{8,0},{12,4},{16,8},{20,12},{24,16},{28,20},{9,1},{13,5},{17,9},{2... | collective-permute-start | bytes 221192 | tf_op jit(solution)/shard_map/ppermute | solution.py:493
  375.9 28.6 %collective-permute-start.54 = (bf16[128,1024]{1,0:T(8,128)(2,1)S(1)}, bf16[128,1024]{1,0:T(8,128)(2,1)S(1)}, u32[]{:S(2)}, u32[]{:S(2)}) collective-permute-start(bf16[128,1024]{1,0:T(8,128)(2,1)S(1)} %get-tuple-element.515.refs_8_), channel_id=1, source_target_pairs={{0,4},{8,0},{16,8},{24,16},{28,24},{20,28},{12,20},{4,12},{1,5},{9... | collective-permute-start | bytes 786440 | tf_op jit(solution)/shard_map/ppermute | solution.py:639
  377.4 27.1 %collective-permute-start.53 = (bf16[128,1024]{1,0:T(8,128)(2,1)S(1)}, bf16[128,1024]{1,0:T(8,128)(2,1)S(1)}, u32[]{:S(2)}, u32[]{:S(2)}) collective-permute-start(bf16[128,1024]{1,0:T(8,128)(2,1)S(1)} %get-tuple-element.516.refs_0_), channel_id=1, source_target_pairs={{0,8},{8,16},{16,24},{24,28},{28,20},{20,12},{12,4},{4,0},{1,9},{9... | collective-permute-start | bytes 786440 | tf_op jit(solution)/shard_map/ppermute | solution.py:639
  404.6 28.7 %collective-permute-start.55 = (bf16[128,1024]{1,0:T(8,128)(2,1)S(1)}, bf16[128,1024]{1,0:T(8,128)(2,1)S(1)}, u32[]{:S(2)}, u32[]{:S(2)}) collective-permute-start(bf16[128,1024]{1,0:T(8,128)(2,1)S(1)} %collective-permute-done.53.refs_1_), channel_id=1, source_target_pairs={{0,8},{8,16},{16,24},{24,28},{28,20},{20,12},{12,4},{4,0},{1,9},{9... | collective-permute-start | bytes 786440 | tf_op jit(solution)/shard_map/ppermute | solution.py:639
  406.4 27.0 %collective-permute-start.56 = (bf16[128,1024]{1,0:T(8,128)(2,1)S(1)}, bf16[128,1024]{1,0:T(8,128)(2,1)S(1)}, u32[]{:S(2)}, u32[]{:S(2)}) collective-permute-start(bf16[128,1024]{1,0:T(8,128)(2,1)S(1)} %collective-permute-done.54.refs_9_), channel_id=1, source_target_pairs={{0,4},{8,0},{16,8},{24,16},{28,24},{20,28},{12,20},{4,12},{1,5},{9... | collective-permute-start | bytes 786440 | tf_op jit(solution)/shard_map/ppermute | solution.py:639
  457.8 25.1 %collective-permute-start.61 = (bf16[128,1024]{1,0:T(8,128)(2,1)}, bf16[128,1024]{1,0:T(8,128)(2,1)}, u32[]{:S(2)}, u32[]{:S(2)}) collective-permute-start(bf16[128,1024]{1,0:T(8,128)(2,1)} %collective-permute-done.57.refs_3_), channel_id=1, source_target_pairs={{0,8},{8,16},{16,24},{24,28},{28,20},{20,12},{12,4},{4,0},{1,9},{9... | collective-permute-start | bytes 786440 | tf_op jit(solution)/shard_map/ppermute | solution.py:639
  457.8 25.1 %collective-permute-start.62 = (bf16[128,1024]{1,0:T(8,128)(2,1)}, bf16[128,1024]{1,0:T(8,128)(2,1)}, u32[]{:S(2)}, u32[]{:S(2)}) collective-permute-start(bf16[128,1024]{1,0:T(8,128)(2,1)} %collective-permute-done.58.refs_11_), channel_id=1, source_target_pairs={{0,4},{8,0},{16,8},{24,16},{28,24},{20,28},{12,20},{4,12},{1,5},{9... | collective-permute-start | bytes 786440 | tf_op jit(solution)/shard_map/ppermute | solution.py:639
  507.1 19.4 %collective-permute-start.73 = (bf16[128,1024]{1,0:T(8,128)(2,1)}, bf16[128,1024]{1,0:T(8,128)(2,1)S(1)}, u32[]{:S(2)}, u32[]{:S(2)}) collective-permute-start(bf16[128,1024]{1,0:T(8,128)(2,1)} %collective-permute-done.66.refs_13_), channel_id=1, source_target_pairs={{0,4},{8,0},{16,8},{24,16},{28,24},{20,28},{12,20},{4,12},{1,5},{9... | collective-permute-start | bytes 786440 | tf_op jit(solution)/shard_map/ppermute | solution.py:639
  510.4 21.2 %collective-permute-start.71 = (bf16[304,512]{1,0:T(8,128)(2,1)S(1)}, bf16[304,512]{1,0:T(8,128)(2,1)S(1)}, u32[]{:S(2)}, u32[]{:S(2)}) collective-permute-start(bf16[304,512]{1,0:T(8,128)(2,1)S(1)} %add_convert_fusion.15), channel_id=1, source_target_pairs={{0,4},{8,0},{16,8},{24,16},{28,24},{20,28},{12,20},{4,12},{1,5},{9... | collective-permute-start | bytes 933896 | tf_op jit(solution)/shard_map/ppermute | solution.py:639
  513.6 18.1 %collective-permute-start.70 = (bf16[304,512]{1,0:T(8,128)(2,1)S(1)}, bf16[304,512]{1,0:T(8,128)(2,1)S(1)}, u32[]{:S(2)}, u32[]{:S(2)}) collective-permute-start(bf16[304,512]{1,0:T(8,128)(2,1)S(1)} %add_convert_fusion.16), channel_id=1, source_target_pairs={{0,8},{8,16},{16,24},{24,28},{28,20},{20,12},{12,4},{4,0},{1,9},{9... | collective-permute-start | bytes 933896 | tf_op jit(solution)/shard_map/ppermute | solution.py:639
  577.3 18.8 %collective-permute-start.95 = (bf16[256,2048]{1,0:T(8,128)(2,1)}, bf16[256,2048]{1,0:T(8,128)(2,1)}, u32[]{:S(2)}, u32[]{:S(2)}) collective-permute-start(bf16[256,2048]{1,0:T(8,128)(2,1)} %fusion.23), channel_id=1, source_target_pairs={{0,1},{1,0},{2,3},{3,2},{4,5},{5,4},{6,7},{7,6},{8,9},{9,8},{10,11... | collective-permute-start | bytes 3145736 | tf_op jit(solution)/shard_map/ppermute | solution.py:486
  577.3 18.8 %collective-permute-start.96 = (bf16[256,2048]{1,0:T(8,128)(2,1)}, bf16[256,2048]{1,0:T(8,128)(2,1)}, u32[]{:S(2)}, u32[]{:S(2)}) collective-permute-start(bf16[256,2048]{1,0:T(8,128)(2,1)} %fusion.24), channel_id=1, source_target_pairs={{0,1},{1,0},{2,3},{3,2},{4,5},{5,4},{6,7},{7,6},{8,9},{9,8},{10,11... | collective-permute-start | bytes 3145736 | tf_op jit(solution)/shard_map/ppermute | solution.py:486
  617.4 30.1 %collective-permute-start.115 = (bf16[256,2048]{1,0:T(8,128)(2,1)}, bf16[256,2048]{1,0:T(8,128)(2,1)}, u32[]{:S(2)}, u32[]{:S(2)}) collective-permute-start(bf16[256,2048]{1,0:T(8,128)(2,1)} %add_convert_fusion), channel_id=1, source_target_pairs={{0,2},{1,3},{2,0},{3,1},{4,6},{5,7},{6,4},{7,5},{8,10},{9,11},{10,... | collective-permute-start | bytes 3145736 | tf_op jit(solution)/shard_map/ppermute | solution.py:486
  (273 other events, 3237.6 us)
Sparse Core Ops, SparseCore 0:
  284.1 90.6 reduce-scatter.2
  378.9 99.9 reduce-scatter.4

commit v4 on v3

--- a/solution.py
+++ b/solution.py
@@ -91,7 +91,7 @@
             return h
         last_ref[0,:,sl]=lax.fori_loop(0,tokens//GROUP,group,jnp.zeros((n,eb),F32))
 
-def p1(first, step, act, bc, rate, tokens, eb=512):
+def p1(first, step, act, bc, rate, tokens, eb=1024):
     width = step.shape[1]
     n = rate.shape[0]
     blk = pl.BlockSpec((tokens, width), lambda s: (first + s, 0))
@@ -148,7 +148,7 @@
         return 0
     lax.fori_loop(0,tokens//16,gate,0)
 
-def p2(first, step, act, z, bc, rate, skip, carry, tokens, eb=512):
+def p2(first, step, act, z, bc, rate, skip, carry, tokens, eb=1024):
     width = step.shape[1]
     n = rate.shape[0]
     nch = tokens // CHUNK
@@ -195,7 +195,7 @@
             return h
         first_ref[0,:,sl]=lax.fori_loop(0,tokens//GROUP,group,jnp.zeros((n,eb),F32))
 
-def b1(first, step, dy, bc, rate, tokens, eb=512):
+def b1(first, step, dy, bc, rate, tokens, eb=1024):
     width = step.shape[1]
     n = rate.shape[0]
     return pl.pallas_call(
@@ -405,6 +405,46 @@
     )(at, *both[0], *both[1], *given)
 
 
+def settle_some_kernel(at_ref, *refs, count, blocks, cols):
+    out_ref, small_ref = refs[-2:]
+    rows = out_ref.shape[0]
+    for j in range(count):
+
+        @pl.when(pl.program_id(0) == j)
+        def _():
+            for d in range(2):
+                ref = refs[2 * j + d]
+                wide = ref.shape[1]
+                for r in range(blocks):
+                    start = pl.multiple_of((at_ref[0] ^ r) * cols + d * wide, 128)
+                    out_ref[:, pl.ds(start, wide)] = ref[r * rows : (r + 1) * rows, :].astype(F32)
+                small_ref[:, d * wide : (d + 1) * wide] = ref[blocks * rows :, :].astype(F32)
+
+
+def settle_some(me, devices, both, turns, shape, blocks, cols, extra, filled):
+    steps = len(RING)
+    pairs = [(both[0][t], both[1][(steps - t) % steps]) for t in turns]
+    rows, wide = pairs[0][0].shape
+    piece = (rows - extra // steps) // blocks
+    whole = pl.BlockSpec((rows, wide), lambda i, at_ref: (0, 0))
+    return pl.pallas_call(
+        partial(settle_some_kernel, count=len(turns), blocks=blocks, cols=cols),
+        grid_spec=pltpu.PrefetchScalarGridSpec(
+            num_scalar_prefetch=1,
+            grid=(len(turns),),
+            in_specs=[whole] * (2 * len(turns)) + [pl.BlockSpec(memory_space=pl.ANY)] * len(filled),
+            out_specs=[
+                pl.BlockSpec((piece, blocks * cols), lambda i, at_ref: (at_ref[1 + i], 0)),
+                pl.BlockSpec((extra // steps, 2 * wide), lambda i, at_ref: (at_ref[1 + i], 0)),
+            ],
+        ),
+        out_shape=[jax.ShapeDtypeStruct(shape, F32), jax.ShapeDtypeStruct((extra, 2 * wide), F32)],
+        input_output_aliases={1 + 2 * len(turns) + j: j for j in range(len(filled))},
+        cost_estimate=cost(len(turns)),
+        compiler_params=kernel_params(),
+    )(jnp.stack([me] + devices).astype(jnp.int32), *[v for pair in pairs for v in pair], *filled)
+
+
 def cut_rows_kernel(v_ref, *out_refs, cut):
     for ref, first in zip(out_refs, cut):
         ref[...] = v_ref[first : first + ref.shape[0], :]
@@ -971,12 +1011,16 @@
     loss_sum = tail[width:] + swap(tail[width:], 1)
     loss = (loss_sum + swap(loss_sum, 2))[0] / (width * count)
     if by_steps:
-        gain_grad, loss, in_owned = advanced(gain_grad, loss, in_owned)
-        while not x_ring.done():
+        while len(x_ring.rounds[0]) < seq_count - 1:
             in_owned = advanced(in_owned)
-        in_owned, small = settle(
-            where, x_ring.result(), in_weight.shape, seqs, inner, filled=in_owned, extra=small.shape[0]
-        )
+        blocks_of = partial(settle_some, shape=in_weight.shape, blocks=seqs, cols=inner, extra=small.shape[0])
+        gap = jnp.zeros(small.shape, F32)
+        for turns in ((0, 2, 3, 4, 5, 6), (1, 7)):
+            devices = [ring_device(x_ring.place + seq_count - t) for t in turns]
+            in_owned, gap = blocks_of(me, devices, x_ring.result(), turns, filled=(in_owned, gap))
+            if not x_ring.done():
+                in_owned, gap = advanced(in_owned, gap)
+        small = gap
     if not by_steps:
         x_shares = jnp.swapaxes(in_shares(g_x_all, normed_all), 0, 1)
         x_row = crossed_blocks(reduced(x_shares.reshape(width, inner)).reshape(seqs, -1, inner))

time: 718 us -> 715 us (level)
    pallas_call x0 -> x2, Pallas kernels: none -> 10 us  [settle_some(): pl.pallas_call(partial(settle_some_kernel, count=len(turns), blocks=block...]
    pallas_call x5 -> x4, Pallas kernels: 30.4 us -> 22 us  [settle(): pl.pallas_call(partial(settle_kernel, steps=steps, base=base, blocks=bloc...]
  transfers between devices with their start and end apart: 134 -> 134, of which waited for: 55 -> 51; matrix products, arithmetic and copies ran while one was open for 21% -> 21% of each run, Pallas kernels for 30% -> 31%
where the time goes in v4:
time: 715 us; the launch traced here: 708 us
  Pallas kernels  223 us (31%)
  waiting for transfers between devices  137 us (19%)
  starting transfers between devices  133 us (19%)
  matrix products  93 us (13%)
  other arithmetic  60 us (8%)
  local copies, waits for them, and re-layouts  42 us (6%)
  between operations  20.1 us (3%)
    pallas_call x4, Pallas kernels, b2(): pl.pallas_call(partial(b2_kernel, eb=eb, n=n), grid=(count,), in_specs=[b...  107 us
    dot_general x23, matrix products, product(): return lax.dot_general(left, right, dims, preferred_element_type=F32)  93 us
    ppermute x56, starting transfers between devices, send(): self.moving.append(lax.ppermute(held[d], 'seq', route))  55.9 us
    ppermute x39, waiting for transfers between devices, swap(): lax.ppermute(a, 'wsh', [(i, i ^ bit) for i in range(lax.axis_size('wsh'))])  53.9 us
    ppermute x56, waiting for transfers between devices, send(): self.moving.append(lax.ppermute(held[d], 'seq', route))  49.9 us
    pallas_call x2, Pallas kernels, p2(): pl.pallas_call(partial(p2_kernel, eb=eb, n=n), grid=(2,), in_specs=[blk,...  33.8 us
    ppermute x23, starting transfers between devices, seq_xor(): lax.ppermute(v, 'seq', [(i, i ^ bits) for i in range(lax.axis_size('seq'))])  26.9 us
    ppermute x39, starting transfers between devices, swap(): lax.ppermute(a, 'wsh', [(i, i ^ bit) for i in range(lax.axis_size('wsh'))])  25.2 us
  transfers between devices with their start and end apart: 134, of which 51 were waited for; matrix products, arithmetic and copies ran while one was open for 21% of the time, Pallas kernels for 31%

profile of v4, /device:TPU:0, one launch (start us, length us, event | category | flops | bytes accessed | tf_op | source)
XLA Modules:
  0.0 708.2 jit_solution(4273574331343131419)
XLA Ops:
  23.1 7.4 %collective-permute-done.4.refs_2_ = bf16[128,1024]{1,0:T(8,128)(2,1)} collective-permute-done((bf16[128,1024]{1,0:T(8,128)(2,1)S(1)}, bf16[128,1024]{1,0:T(8,128)(2,1)}, u32[]{:S(2)}, u32[]{:S(2)}) %collective-permute-start.4) | collective-permute-done | bytes 262176 | tf_op jit(solution)/shard_map/ppermute | solution.py:526
  39.5 5.3 collective-permute-done.7.refs_6_
  70.4 7.7 %fusion.17 = f32[4,272,1024]{2,1,0:T(8,128)S(1)} fusion(bf16[2048,1024]{1,0:T(8,128)(2,1)} %shard_map.237, bf16[1,272,2048]{2,1,0:T(8,128)(2,1)} %bitcast.10, bf16[1,272,2048]{2,1,0:T(8,128)(2,1)S(1)} %bitcast.299, bf16[1,272,2048]{2,1,0:T(8,128)(2,1)} %bitcast.8, bf16[1,272,2048]{2,1,0:T(8,128)(2,1)S(1)} %bitcast.290), kind=kOutput, calls=%fused_computation.27 | convolution fusion | flops 4570087424 | bytes 13107200 | tf_op jit(solution)/shard_map/dot_general | solution.py:25
  94.0 6.4 collective-permute-done.21
  109.8 9.4 %shard_map.238 = (f32[2,16,1024]{2,1,0:T(8,128)}, f32[2,1,1024]{2,1,0:T(1,128)}) custom-call(f32[1024,1024]{1,0:T(8,128)} %compare_select_fusion.step_ref, bf16[1024,1024]{1,0:T(8,128)(2,1)} %copy-done.6, f32[32,1024]{1,0:T(8,128)} %slice_convert_fusion.2.bc_ref, f32[16,1024]{1,0:T(8,128)} %fusion.77.rate_ref), custom_call_target="tpu_custom_call" | custom-call | flops 8999999488 | tf_op jit(solution)/shard_map/pallas_call | solution.py:98
  127.2 9.7 %shard_map.239 = (f32[2,16,1024]{2,1,0:T(8,128)}, f32[2,1,1024]{2,1,0:T(1,128)}) custom-call(f32[1024,1024]{1,0:T(8,128)} %compare_select_fusion.step_ref, bf16[1024,1024]{1,0:T(8,128)(2,1)} %copy-done.6, f32[32,1024]{1,0:T(8,128)} %slice_convert_fusion.2.bc_ref, f32[16,1024]{1,0:T(8,128)} %fusion.77.rate_ref), custom_call_target="tpu_custom_call" | custom-call | flops 8999999488 | tf_op jit(solution)/shard_map/pallas_call | solution.py:98
  154.0 8.3 %fusion.101.z_ref = f32[1024,1024]{1,0:T(8,128)} fusion(bf16[1024,2048]{1,0:T(8,128)(2,1)S(1)} %bitcast.293, bf16[2048,1024]{1,0:T(8,128)(2,1)} %shard_map.240), kind=kOutput, calls=%fused_computation.317 | convolution fusion | flops 4294967296 | bytes 12582912 | tf_op jit(solution)/shard_map/dot_general | solution.py:25
  167.3 17.1 %shard_map.241 = (f32[512,1024]{1,0:T(8,128)}, bf16[512,1024]{1,0:T(8,128)(2,1)}, f32[2,8,16,1024]{3,2,1,0:T(8,128)}) custom-call(f32[1024,1024]{1,0:T(8,128)} %compare_select_fusion.step_ref, bf16[1024,1024]{1,0:T(8,128)(2,1)} %copy-done.6, f32[1024,1024]{1,0:T(8,128)} %fusion.101.z_ref, f32[32,1024]{1,0:T(8,128)} %slice_convert_fusion.2.bc_ref, ...), custom_call_target="tpu_custom_call" | custom-call | flops 16000000000 | tf_op jit(solution)/shard_map/pallas_call | solution.py:158
  192.8 16.7 %shard_map.242 = (f32[512,1024]{1,0:T(8,128)}, bf16[512,1024]{1,0:T(8,128)(2,1)}, f32[2,8,16,1024]{3,2,1,0:T(8,128)}) custom-call(f32[1024,1024]{1,0:T(8,128)} %compare_select_fusion.step_ref, bf16[1024,1024]{1,0:T(8,128)(2,1)} %copy-done.6, f32[1024,1024]{1,0:T(8,128)} %fusion.101.z_ref, f32[32,1024]{1,0:T(8,128)} %slice_convert_fusion.2.bc_ref, ...), custom_call_target="tpu_custom_call" | custom-call | flops 16000000000 | tf_op jit(solution)/shard_map/pallas_call | solution.py:158
  209.6 7.0 collective-permute-done.40
  239.3 10.1 %shard_map.243 = f32[2,16,1024]{2,1,0:T(8,128)} custom-call(f32[1024,1024]{1,0:T(8,128)} %compare_select_fusion.step_ref, f32[512,1024]{1,0:T(8,128)} %get-tuple-element.478.dy_ref, f32[32,1024]{1,0:T(8,128)} %slice_convert_fusion.2.bc_ref, f32[16,1024]{1,0:T(8,128)} %fusion.77.rate_ref), custom_call_target="tpu_custom_call" | custom-call | flops 8999999488 | tf_op jit(solution)/shard_map/pallas_call | solution.py:201
  249.4 8.2 %collective-permute-done.43 = bf16[256,2048]{1,0:T(8,128)(2,1)} collective-permute-done((bf16[256,2048]{1,0:T(8,128)(2,1)S(1)}, bf16[256,2048]{1,0:T(8,128)(2,1)}, u32[]{:S(2)}, u32[]{:S(2)}) %collective-permute-start.43) | collective-permute-done | bytes 1048608 | tf_op jit(solution)/shard_map/ppermute | solution.py:526
  260.6 8.7 %multiply_convert_fusion.1 = (bf16[512,1024]{1,0:T(8,128)(2,1)}, f32[512,1024]{1,0:T(8,128)}) fusion(f32[512,1024]{1,0:T(8,128)} %get-tuple-element.280, f32[1024,1024]{1,0:T(8,128)} %fusion.101.z_ref, bf16[1024,2048]{1,0:T(8,128)(2,1)} %param.27, bf16[256,2048]{1,0:T(8,128)(2,1)} %collective-permute-done.44, bf16[256,2048]{1,0:T(8,128)(2,1)} %collective-permute-done.43), kind=kOutput, calls=%fused_computation.85 | convolution fusion | flops 2157969408 | bytes 13631488 | tf_op jit(solution)/shard_map/dot_general | solution.py:25
  273.4 8.2 %fusion.19 = bf16[1024,2048]{1,0:T(8,128)(2,1)} fusion(bf16[256,2048]{1,0:T(8,128)(2,1)} %collective-permute-done.44, bf16[256,2048]{1,0:T(8,128)(2,1)} %collective-permute-done.43, bf16[256,2048]{1,0:T(8,128)(2,1)S(1)} %copy-done.146, bf16[256,2048]{1,0:T(8,128)(2,1)S(1)} %copy-done.69, bf16[512,1024]{1,0:T(8,128)(2,1)S(1)} %copy-done.165, ...), kind=kOutput, calls=%fused_computation.39 | convolution fusion | flops 4318035968 | bytes 10485760 | tf_op jit(solution)/shard_map/dot_general | solution.py:25
  281.7 9.8 %shard_map.244 = f32[2,16,1024]{2,1,0:T(8,128)} custom-call(f32[1024,1024]{1,0:T(8,128)} %compare_select_fusion.step_ref, f32[512,1024]{1,0:T(8,128)} %get-tuple-element.283.dy_ref, f32[32,1024]{1,0:T(8,128)} %slice_convert_fusion.2.bc_ref, f32[16,1024]{1,0:T(8,128)} %fusion.77.rate_ref), custom_call_target="tpu_custom_call" | custom-call | flops 8999999488 | tf_op jit(solution)/shard_map/pallas_call | solution.py:201
  294.1 26.5 %shard_map.245 = (bf16[1024,1024]{1,0:T(8,128)(2,1)}, f32[1024,1024]{1,0:T(8,128)}, f32[1,32,128]{2,1,0:T(8,128)}, f32[1,32,128]{2,1,0:T(8,128)}, f32[1,16,1024]{2,1,0:T(8,128)}, /*index=5*/f32[1,2,8,1024]{3,2,1,0:T(8,128)}) custom-call(f32[1024,1024]{1,0:T(8,128)} %compare_select_fusion.step_ref, bf16[1024,1024]{1,0:T(8,128)(2,1)} %copy-done.6, ...), custom_call_target="tpu_custom_call" | custom-call | flops 24999999488 | tf_op jit(solution)/shard_map/pallas_call | solution.py:319
  325.0 27.0 %shard_map.246 = (bf16[1024,1024]{1,0:T(8,128)(2,1)}, f32[1024,1024]{1,0:T(8,128)}, f32[1,32,128]{2,1,0:T(8,128)}, f32[1,32,128]{2,1,0:T(8,128)}, f32[1,16,1024]{2,1,0:T(8,128)}, /*index=5*/f32[1,2,8,1024]{3,2,1,0:T(8,128)}) custom-call(f32[1024,1024]{1,0:T(8,128)} %compare_select_fusion.step_ref, ...), custom_call_target="tpu_custom_call", output_to_operand_aliasing={{0}: (8, {}), {1}: (9, {})} | custom-call | flops 24999999488 | tf_op jit(solution)/shard_map/pallas_call | solution.py:319
  360.1 12.0 %reduce-scatter.3.cloned.1.call-done = bf16[128,2048]{1,0:T(8,128)(2,1)} async-done(((bf16[1024,2048]{1,0:T(8,128)(2,1)}), bf16[128,2048]{1,0:T(8,128)(2,1)}) %reduce-scatter.3.cloned.1.call-update) | async-done | bytes 524304 | tf_op jit(solution)/shard_map/reduce_scatter | solution.py:720
  375.3 26.5 %shard_map.247 = (bf16[1024,1024]{1,0:T(8,128)(2,1)}, f32[1024,1024]{1,0:T(8,128)}, f32[1,32,128]{2,1,0:T(8,128)}, f32[1,32,128]{2,1,0:T(8,128)}, f32[1,16,1024]{2,1,0:T(8,128)}, /*index=5*/f32[1,2,8,1024]{3,2,1,0:T(8,128)}) custom-call(f32[1024,1024]{1,0:T(8,128)} %compare_select_fusion.step_ref, ...), custom_call_target="tpu_custom_call", output_to_operand_aliasing={{0}: (8, {}), {1}: (9, {})} | custom-call | flops 24999999488 | tf_op jit(solution)/shard_map/pallas_call | solution.py:319
  404.1 26.6 %shard_map.248 = (bf16[1024,1024]{1,0:T(8,128)(2,1)}, f32[1024,1024]{1,0:T(8,128)}, f32[1,32,128]{2,1,0:T(8,128)}, f32[1,32,128]{2,1,0:T(8,128)}, f32[1,16,1024]{2,1,0:T(8,128)}, /*index=5*/f32[1,2,8,1024]{3,2,1,0:T(8,128)}) custom-call(f32[1024,1024]{1,0:T(8,128)} %compare_select_fusion.step_ref, ...), custom_call_target="tpu_custom_call", output_to_operand_aliasing={{0}: (8, {}), {1}: (9, {})} | custom-call | flops 24999999488 | tf_op jit(solution)/shard_map/pallas_call | solution.py:319
  445.2 5.9 collective-permute-done.60
  462.0 9.3 %bitcast_convert_fusion = bf16[2048,1024]{1,0:T(8,128)(2,1)} fusion(bf16[4,272,1024]{2,1,0:T(8,128)(2,1)S(1)} %multiply_convert_fusion, bf16[1,272,2048]{2,1,0:T(8,128)(2,1)} %bitcast.10, bf16[1,272,2048]{2,1,0:T(8,128)(2,1)S(1)} %bitcast.301, bf16[1,272,2048]{2,1,0:T(8,128)(2,1)} %bitcast.8, bf16[1,272,2048]{2,1,0:T(8,128)(2,1)S(1)} %bitcast.292), kind=kOutput, calls=%fused_computation.1 | convolution fusion | flops 4572184576 | bytes 10878976 | tf_op jit(solution)/shard_map/dot_general | solution.py:25
  497.5 6.3 collective-permute-done.66.refs_13_
  552.8 5.6 shard_map.249.refs_16_
  584.9 5.4 shard_map.250
  602.1 5.5 collective-permute-done.99.refs_6_
  625.1 5.1 collective-permute-done.104.refs_0_
  632.7 5.5 shard_map.251.refs_16_
  641.9 5.5 shard_map.252.refs_12_
  661.4 7.0 collective-permute-done.121
  671.9 5.3 fusion.51
  685.8 6.5 shard_map.253
  (826 shorter events, 356.3 us)
Async XLA Ops:
  7.2 365.0 %reduce-scatter.3.cloned.1.call-start = ((), (), s32[]{:S(2)}) async-start(), calls=%async_computation.2 | async-start | bytes 4718592 | tf_op jit(solution)/shard_map/reduce_scatter | solution.py:720
  33.9 27.4 %collective-permute-start.6 = (bf16[272,2048]{1,0:T(8,128)(2,1)S(1)}, bf16[272,2048]{1,0:T(8,128)(2,1)S(1)}, u32[]{:S(2)}, u32[]{:S(2)}) collective-permute-start(bf16[272,2048]{1,0:T(8,128)(2,1)S(1)} %pad_maximum_fusion.3), channel_id=1, source_target_pairs={{0,2},{1,3},{2,0},{3,1},{4,6},{5,7},{6,4},{7,5},{8,10},{9,11},{10,... | collective-permute-start | bytes 3342344 | tf_op jit(solution)/shard_map/ppermute | solution.py:526
  64.2 18.9 %collective-permute-start.15 = (bf16[128,1024]{1,0:T(8,128)(2,1)S(1)}, bf16[128,1024]{1,0:T(8,128)(2,1)S(1)}, u32[]{:S(2)}, u32[]{:S(2)}) collective-permute-start(bf16[128,1024]{1,0:T(8,128)(2,1)S(1)} %get-tuple-element.474), channel_id=1, source_target_pairs={{0,2},{1,3},{2,0},{3,1},{4,6},{5,7},{6,4},{7,5},{8,10},{9,11},{10,... | collective-permute-start | bytes 786440 | tf_op jit(solution)/shard_map/ppermute | solution.py:526
  137.3 25.1 %collective-permute-start.32 = (bf16[2,18,1024]{2,1,0:T(8,128)(2,1)S(1)}, bf16[2,18,1024]{2,1,0:T(8,128)(2,1)S(1)}, u32[]{:S(2)}, u32[]{:S(2)}) collective-permute-start(bf16[2,18,1024]{2,1,0:T(8,128)(2,1)S(1)} %pad_maximum_fusion.22), channel_id=1, source_target_pairs={{0,8},{4,12},{8,16},{12,20},{16,24},{20,28},{1,9},{5,13},{9,17},{1... | collective-permute-start | bytes 221192 | tf_op jit(solution)/shard_map/ppermute | solution.py:533
  140.5 21.9 %collective-permute-start.33 = (bf16[2,18,1024]{2,1,0:T(8,128)(2,1)S(1)}, bf16[2,18,1024]{2,1,0:T(8,128)(2,1)S(1)}, u32[]{:S(2)}, u32[]{:S(2)}) collective-permute-start(bf16[2,18,1024]{2,1,0:T(8,128)(2,1)S(1)} %pad_maximum_fusion.22), channel_id=1, source_target_pairs={{0,16},{4,20},{8,24},{12,28},{1,17},{5,21},{9,25},{13,29},{2,18},{... | collective-permute-start | bytes 221192 | tf_op jit(solution)/shard_map/ppermute | solution.py:533
  144.2 18.2 %collective-permute-start.34 = (bf16[2,18,1024]{2,1,0:T(8,128)(2,1)S(1)}, bf16[2,18,1024]{2,1,0:T(8,128)(2,1)S(1)}, u32[]{:S(2)}, u32[]{:S(2)}) collective-permute-start(bf16[2,18,1024]{2,1,0:T(8,128)(2,1)S(1)} %pad_maximum_fusion.22), channel_id=1, source_target_pairs={{0,24},{4,28},{1,25},{5,29},{2,26},{6,30},{3,27},{7,31}} | collective-permute-start | bytes 221192 | tf_op jit(solution)/shard_map/ppermute | solution.py:533
  163.4 21.0 %collective-permute-start.36 = (bf16[2,18,1024]{2,1,0:T(8,128)(2,1)S(1)}, bf16[2,18,1024]{2,1,0:T(8,128)(2,1)S(1)}, u32[]{:S(2)}, u32[]{:S(2)}) collective-permute-start(bf16[2,18,1024]{2,1,0:T(8,128)(2,1)S(1)} %pad_maximum_fusion.23), channel_id=1, source_target_pairs={{0,8},{4,12},{8,16},{12,20},{16,24},{20,28},{1,9},{5,13},{9,17},{1... | collective-permute-start | bytes 221192 | tf_op jit(solution)/shard_map/ppermute | solution.py:533
  164.7 19.7 %collective-permute-start.37 = (bf16[2,18,1024]{2,1,0:T(8,128)(2,1)S(1)}, bf16[2,18,1024]{2,1,0:T(8,128)(2,1)S(1)}, u32[]{:S(2)}, u32[]{:S(2)}) collective-permute-start(bf16[2,18,1024]{2,1,0:T(8,128)(2,1)S(1)} %pad_maximum_fusion.23), channel_id=1, source_target_pairs={{0,16},{4,20},{8,24},{12,28},{1,17},{5,21},{9,25},{13,29},{2,18},{... | collective-permute-start | bytes 221192 | tf_op jit(solution)/shard_map/ppermute | solution.py:533
  166.0 18.4 %collective-permute-start.38 = (bf16[2,18,1024]{2,1,0:T(8,128)(2,1)S(1)}, bf16[2,18,1024]{2,1,0:T(8,128)(2,1)S(1)}, u32[]{:S(2)}, u32[]{:S(2)}) collective-permute-start(bf16[2,18,1024]{2,1,0:T(8,128)(2,1)S(1)} %pad_maximum_fusion.23), channel_id=1, source_target_pairs={{0,24},{4,28},{1,25},{5,29},{2,26},{6,30},{3,27},{7,31}} | collective-permute-start | bytes 221192 | tf_op jit(solution)/shard_map/ppermute | solution.py:533
  191.3 25.3 %collective-permute-start.40 = (bf16[256,2048]{1,0:T(8,128)(2,1)S(1)}, bf16[256,2048]{1,0:T(8,128)(2,1)S(1)}, u32[]{:S(2)}, u32[]{:S(2)}) collective-permute-start(bf16[256,2048]{1,0:T(8,128)(2,1)S(1)} %fusion.39), channel_id=1, source_target_pairs={{0,2},{1,3},{2,0},{3,1},{4,6},{5,7},{6,4},{7,5},{8,10},{9,11},{10,... | collective-permute-start | bytes 3145736 | tf_op jit(solution)/shard_map/ppermute | solution.py:526
  232.0 25.5 %collective-permute-start.43 = (bf16[256,2048]{1,0:T(8,128)(2,1)S(1)}, bf16[256,2048]{1,0:T(8,128)(2,1)}, u32[]{:S(2)}, u32[]{:S(2)}) collective-permute-start(bf16[256,2048]{1,0:T(8,128)(2,1)S(1)} %fusion.66), channel_id=1, source_target_pairs={{0,2},{1,3},{2,0},{3,1},{4,6},{5,7},{6,4},{7,5},{8,10},{9,11},{10,... | collective-permute-start | bytes 3145736 | tf_op jit(solution)/shard_map/ppermute | solution.py:526
  269.5 22.2 %collective-permute-start.46 = (bf16[2,18,1024]{2,1,0:T(8,128)(2,1)S(1)}, bf16[2,18,1024]{2,1,0:T(8,128)(2,1)S(1)}, u32[]{:S(2)}, u32[]{:S(2)}) collective-permute-start(bf16[2,18,1024]{2,1,0:T(8,128)(2,1)S(1)} %pad_maximum_fusion.24), channel_id=1, source_target_pairs={{8,0},{12,4},{16,8},{20,12},{24,16},{28,20},{9,1},{13,5},{17,9},{2... | collective-permute-start | bytes 221192 | tf_op jit(solution)/shard_map/ppermute | solution.py:533
  270.8 20.9 %collective-permute-start.47 = (bf16[2,18,1024]{2,1,0:T(8,128)(2,1)S(1)}, bf16[2,18,1024]{2,1,0:T(8,128)(2,1)S(1)}, u32[]{:S(2)}, u32[]{:S(2)}) collective-permute-start(bf16[2,18,1024]{2,1,0:T(8,128)(2,1)S(1)} %pad_maximum_fusion.24), channel_id=1, source_target_pairs={{16,0},{20,4},{24,8},{28,12},{17,1},{21,5},{25,9},{29,13},{18,2},{... | collective-permute-start | bytes 221192 | tf_op jit(solution)/shard_map/ppermute | solution.py:533
  272.1 19.7 %collective-permute-start.48 = (bf16[2,18,1024]{2,1,0:T(8,128)(2,1)S(1)}, bf16[2,18,1024]{2,1,0:T(8,128)(2,1)S(1)}, u32[]{:S(2)}, u32[]{:S(2)}) collective-permute-start(bf16[2,18,1024]{2,1,0:T(8,128)(2,1)S(1)} %pad_maximum_fusion.24), channel_id=1, source_target_pairs={{24,0},{28,4},{25,1},{29,5},{26,2},{30,6},{27,3},{31,7}} | collective-permute-start | bytes 221192 | tf_op jit(solution)/shard_map/ppermute | solution.py:533
  281.6 194.9 %reduce-scatter.5.cloned.1.call-start = ((), (), s32[]{:S(2)}) async-start(), calls=%async_computation.3 | async-start | bytes 4718592 | tf_op jit(solution)/shard_map/reduce_scatter | solution.py:720
  292.4 28.2 %collective-permute-start.49 = (bf16[2,18,1024]{2,1,0:T(8,128)(2,1)S(1)}, bf16[2,18,1024]{2,1,0:T(8,128)(2,1)S(1)}, u32[]{:S(2)}, u32[]{:S(2)}) collective-permute-start(bf16[2,18,1024]{2,1,0:T(8,128)(2,1)S(1)} %pad_maximum_fusion.14), channel_id=1, source_target_pairs={{0,4},{4,0},{8,12},{12,8},{16,20},{20,16},{24,28},{28,24},{1,5},{5... | collective-permute-start | bytes 221192 | tf_op jit(solution)/shard_map/ppermute | solution.py:629
  320.8 38.4 %collective-permute-start.50 = (bf16[2,18,1024]{2,1,0:T(8,128)(2,1)S(1)}, bf16[2,18,1024]{2,1,0:T(8,128)(2,1)S(1)}, u32[]{:S(2)}, u32[]{:S(2)}) collective-permute-start(bf16[2,18,1024]{2,1,0:T(8,128)(2,1)S(1)} %pad_maximum_fusion.25), channel_id=1, source_target_pairs={{8,0},{12,4},{16,8},{20,12},{24,16},{28,20},{9,1},{13,5},{17,9},{2... | collective-permute-start | bytes 221192 | tf_op jit(solution)/shard_map/ppermute | solution.py:533
  322.4 36.9 %collective-permute-start.51 = (bf16[2,18,1024]{2,1,0:T(8,128)(2,1)S(1)}, bf16[2,18,1024]{2,1,0:T(8,128)(2,1)S(1)}, u32[]{:S(2)}, u32[]{:S(2)}) collective-permute-start(bf16[2,18,1024]{2,1,0:T(8,128)(2,1)S(1)} %pad_maximum_fusion.25), channel_id=1, source_target_pairs={{16,0},{20,4},{24,8},{28,12},{17,1},{21,5},{25,9},{29,13},{18,2},{... | collective-permute-start | bytes 221192 | tf_op jit(solution)/shard_map/ppermute | solution.py:533
  323.7 35.6 %collective-permute-start.52 = (bf16[2,18,1024]{2,1,0:T(8,128)(2,1)S(1)}, bf16[2,18,1024]{2,1,0:T(8,128)(2,1)S(1)}, u32[]{:S(2)}, u32[]{:S(2)}) collective-permute-start(bf16[2,18,1024]{2,1,0:T(8,128)(2,1)S(1)} %pad_maximum_fusion.25), channel_id=1, source_target_pairs={{24,0},{28,4},{25,1},{29,5},{26,2},{30,6},{27,3},{31,7}} | collective-permute-start | bytes 221192 | tf_op jit(solution)/shard_map/ppermute | solution.py:533
  373.2 28.6 %collective-permute-start.53 = (bf16[128,1024]{1,0:T(8,128)(2,1)S(1)}, bf16[128,1024]{1,0:T(8,128)(2,1)S(1)}, u32[]{:S(2)}, u32[]{:S(2)}) collective-permute-start(bf16[128,1024]{1,0:T(8,128)(2,1)S(1)} %get-tuple-element.518.refs_0_), channel_id=1, source_target_pairs={{0,8},{8,16},{16,24},{24,28},{28,20},{20,12},{12,4},{4,0},{1,9},{9... | collective-permute-start | bytes 786440 | tf_op jit(solution)/shard_map/ppermute | solution.py:679
  375.0 26.9 %collective-permute-start.54 = (bf16[128,1024]{1,0:T(8,128)(2,1)S(1)}, bf16[128,1024]{1,0:T(8,128)(2,1)S(1)}, u32[]{:S(2)}, u32[]{:S(2)}) collective-permute-start(bf16[128,1024]{1,0:T(8,128)(2,1)S(1)} %get-tuple-element.517.refs_8_), channel_id=1, source_target_pairs={{0,4},{8,0},{16,8},{24,16},{28,24},{20,28},{12,20},{4,12},{1,5},{9... | collective-permute-start | bytes 786440 | tf_op jit(solution)/shard_map/ppermute | solution.py:679
  402.0 28.7 %collective-permute-start.55 = (bf16[128,1024]{1,0:T(8,128)(2,1)S(1)}, bf16[128,1024]{1,0:T(8,128)(2,1)S(1)}, u32[]{:S(2)}, u32[]{:S(2)}) collective-permute-start(bf16[128,1024]{1,0:T(8,128)(2,1)S(1)} %collective-permute-done.53.refs_1_), channel_id=1, source_target_pairs={{0,8},{8,16},{16,24},{24,28},{28,20},{20,12},{12,4},{4,0},{1,9},{9... | collective-permute-start | bytes 786440 | tf_op jit(solution)/shard_map/ppermute | solution.py:679
  403.7 27.0 %collective-permute-start.56 = (bf16[128,1024]{1,0:T(8,128)(2,1)S(1)}, bf16[128,1024]{1,0:T(8,128)(2,1)S(1)}, u32[]{:S(2)}, u32[]{:S(2)}) collective-permute-start(bf16[128,1024]{1,0:T(8,128)(2,1)S(1)} %collective-permute-done.54.refs_9_), channel_id=1, source_target_pairs={{0,4},{8,0},{16,8},{24,16},{28,24},{20,28},{12,20},{4,12},{1,5},{9... | collective-permute-start | bytes 786440 | tf_op jit(solution)/shard_map/ppermute | solution.py:679
  451.4 25.1 %collective-permute-start.61 = (bf16[128,1024]{1,0:T(8,128)(2,1)}, bf16[128,1024]{1,0:T(8,128)(2,1)}, u32[]{:S(2)}, u32[]{:S(2)}) collective-permute-start(bf16[128,1024]{1,0:T(8,128)(2,1)} %collective-permute-done.57.refs_3_), channel_id=1, source_target_pairs={{0,8},{8,16},{16,24},{24,28},{28,20},{20,12},{12,4},{4,0},{1,9},{9... | collective-permute-start | bytes 786440 | tf_op jit(solution)/shard_map/ppermute | solution.py:679
  453.1 23.4 %collective-permute-start.62 = (bf16[128,1024]{1,0:T(8,128)(2,1)}, bf16[128,1024]{1,0:T(8,128)(2,1)}, u32[]{:S(2)}, u32[]{:S(2)}) collective-permute-start(bf16[128,1024]{1,0:T(8,128)(2,1)} %collective-permute-done.58.refs_11_), channel_id=1, source_target_pairs={{0,4},{8,0},{16,8},{24,16},{28,24},{20,28},{12,20},{4,12},{1,5},{9... | collective-permute-start | bytes 786440 | tf_op jit(solution)/shard_map/ppermute | solution.py:679
  481.7 22.1 %collective-permute-start.63 = (bf16[304,512]{1,0:T(8,128)(2,1)}, bf16[304,512]{1,0:T(8,128)(2,1)}, u32[]{:S(2)}, u32[]{:S(2)}) collective-permute-start(bf16[304,512]{1,0:T(8,128)(2,1)} %pad_maximum_fusion.8), channel_id=1, source_target_pairs={{0,8},{8,16},{16,24},{24,28},{28,20},{20,12},{12,4},{4,0},{1,9},{9... | collective-permute-start | bytes 933896 | tf_op jit(solution)/shard_map/ppermute | solution.py:679
  504.8 22.9 %collective-permute-start.70 = (bf16[304,512]{1,0:T(8,128)(2,1)S(1)}, bf16[304,512]{1,0:T(8,128)(2,1)S(1)}, u32[]{:S(2)}, u32[]{:S(2)}) collective-permute-start(bf16[304,512]{1,0:T(8,128)(2,1)S(1)} %add_convert_fusion.16), channel_id=1, source_target_pairs={{0,8},{8,16},{16,24},{24,28},{28,20},{20,12},{12,4},{4,0},{1,9},{9... | collective-permute-start | bytes 933896 | tf_op jit(solution)/shard_map/ppermute | solution.py:679
  507.2 20.6 %collective-permute-start.71 = (bf16[304,512]{1,0:T(8,128)(2,1)S(1)}, bf16[304,512]{1,0:T(8,128)(2,1)S(1)}, u32[]{:S(2)}, u32[]{:S(2)}) collective-permute-start(bf16[304,512]{1,0:T(8,128)(2,1)S(1)} %add_convert_fusion.15), channel_id=1, source_target_pairs={{0,4},{8,0},{16,8},{24,16},{28,24},{20,28},{12,20},{4,12},{1,5},{9... | collective-permute-start | bytes 933896 | tf_op jit(solution)/shard_map/ppermute | solution.py:679
  529.1 19.3 %collective-permute-start.76 = (bf16[304,512]{1,0:T(8,128)(2,1)S(1)}, bf16[304,512]{1,0:T(8,128)(2,1)S(1)}, u32[]{:S(2)}, u32[]{:S(2)}) collective-permute-start(bf16[304,512]{1,0:T(8,128)(2,1)S(1)} %add_convert_fusion.14), channel_id=1, source_target_pairs={{0,8},{8,16},{16,24},{24,28},{28,20},{20,12},{12,4},{4,0},{1,9},{9... | collective-permute-start | bytes 933896 | tf_op jit(solution)/shard_map/ppermute | solution.py:679
  573.4 19.6 %collective-permute-start.95 = (bf16[256,2048]{1,0:T(8,128)(2,1)}, bf16[256,2048]{1,0:T(8,128)(2,1)}, u32[]{:S(2)}, u32[]{:S(2)}) collective-permute-start(bf16[256,2048]{1,0:T(8,128)(2,1)} %fusion.23), channel_id=1, source_target_pairs={{0,1},{1,0},{2,3},{3,2},{4,5},{5,4},{6,7},{7,6},{8,9},{9,8},{10,11... | collective-permute-start | bytes 3145736 | tf_op jit(solution)/shard_map/ppermute | solution.py:526
  573.4 19.6 %collective-permute-start.96 = (bf16[256,2048]{1,0:T(8,128)(2,1)}, bf16[256,2048]{1,0:T(8,128)(2,1)}, u32[]{:S(2)}, u32[]{:S(2)}) collective-permute-start(bf16[256,2048]{1,0:T(8,128)(2,1)} %fusion.24), channel_id=1, source_target_pairs={{0,1},{1,0},{2,3},{3,2},{4,5},{5,4},{6,7},{7,6},{8,9},{9,8},{10,11... | collective-permute-start | bytes 3145736 | tf_op jit(solution)/shard_map/ppermute | solution.py:526
  617.4 30.9 %collective-permute-start.115 = (bf16[256,2048]{1,0:T(8,128)(2,1)}, bf16[256,2048]{1,0:T(8,128)(2,1)}, u32[]{:S(2)}, u32[]{:S(2)}) collective-permute-start(bf16[256,2048]{1,0:T(8,128)(2,1)} %add_convert_fusion), channel_id=1, source_target_pairs={{0,2},{1,3},{2,0},{3,1},{4,6},{5,7},{6,4},{7,5},{8,10},{9,11},{10,... | collective-permute-start | bytes 3145736 | tf_op jit(solution)/shard_map/ppermute | solution.py:526
  (273 other events, 3123.5 us)
Sparse Core Ops, SparseCore 0:
  281.8 90.3 reduce-scatter.2
  376.2 98.8 reduce-scatter.4
